TPU v7x, 32 devices: a whole 2x2x4 slice. The times are simulated.
32 devices in a mesh: groups: 2 (over y), ctx: 4 (over z), head: 2 (over x), rep: 2 (over core).
Axes of the slice: x: 2, y: 2, z: 4, core: 2. Of those that a mesh axis runs over, the one named last changes fastest.
Arguments:
- kv_rows: bfloat16 [1536, 8, 256], P(('groups', 'ctx'), ('head', 'rep')), parts along dimension 0, may hold values from -8 to 8
- kv_scales: float32 [8, 2], replicated, may hold values from 0.004 to 0.04
- queries: bfloat16 [2, 512, 16384], P(None, ('groups', 'ctx'), ('head', 'rep')), parts along dimension 1, may hold values from -8 to 8
- shard_counts: int32 [8], P(('groups', 'ctx')), parts along dimension 0, may hold values from 1 to 192, 576 in all
- span_starts: int32 [4], P('groups'), parts along dimension 0, may hold values from 0 to 320
- block_slots: int32 [96], P('groups'), parts along dimension 0, may hold values from 0 to 47, each once
Outputs:
- attention: bfloat16 [2, 512, 16384], P(None, ('groups', 'ctx'), ('head', 'rep')), parts along dimension 1
- decode_cache: float32 [1536, 8, 256], P(('groups', 'ctx'), 'head'), parts along dimension 0
There are 2 independent parts, one for each index of `groups`. A program takes and returns all parts, laid end to end along the dimension named above; an argument that names none is the same for every part. Nothing has to cross between parts.
Inputs may be any that keep to these rules, and one draw needn't show every extreme that they name: `shard_counts`: one shard is full. `block_slots`: each slot once.
All inputs are finite; a program needn't handle non-finite values.
Results may differ from a plain program's by a relative error of at most 0.0095.
Values may be sent and summed in bfloat16 or wider, within the bound.
No kernel may reach another device: no remote copies, remote signals or barrier semaphores. Data moves between devices by JAX's collectives and lax.ppermute only.
A program may use at most 128 MiB of HBM per device.

v0:
```python
import math

import jax
import jax.numpy as jnp
from jax import lax
from jax.sharding import PartitionSpec as P

BLK = 16


def sign_matrix(order):
    index_col = jnp.arange(order, dtype=jnp.int32)
    shared = jnp.bitwise_and(index_col[:, None], index_col[None, :])
    parity = jnp.zeros((order, order), jnp.int32)
    for bit_pos in range(order.bit_length()):
        parity = parity + jnp.bitwise_and(jnp.right_shift(shared, bit_pos), 1)
    parity = jnp.bitwise_and(parity, 1)
    return (1 - 2 * parity).astype(jnp.bfloat16)


def quantize(kv_values, scales):
    tokens, head_count, row_width = kv_values.shape
    half_width = row_width // 2
    rotated = jnp.dot(
        kv_values.reshape(tokens * head_count * 2, half_width),
        sign_matrix(half_width),
        preferred_element_type=jnp.float32,
    ) * (1.0 / math.sqrt(half_width))
    rotated = rotated.reshape(tokens, head_count, 2, half_width) / scales[None, :, :, None]
    return (
        jnp.clip(rotated, -448.0, 448.0).astype(jnp.bfloat16).reshape(tokens, head_count, row_width)
    )


def dequantize(kv_codes, scales):
    tokens, head_count, row_width = kv_codes.shape
    expanded = kv_codes.reshape(tokens, head_count, 2, row_width // 2) * scales[None, :, :, None]
    return expanded.reshape(tokens, head_count, row_width)


def body(kv_rows, kv_scales, queries, shard_counts, span_starts, block_slots):
    tok_rows, kv_local, row_width = kv_rows.shape
    head_dim = row_width // 2
    query_sets, query_rows, query_width = queries.shape
    group_size = query_width // head_dim // kv_local
    rep_size = lax.axis_size("rep")
    rep_id = lax.axis_index("rep")
    head_id = lax.axis_index("head")
    ctx_id = lax.axis_index("ctx")
    first_head = (head_id * rep_size + rep_id) * kv_local
    own_scales = lax.dynamic_slice_in_dim(kv_scales, first_head, kv_local, 0)
    kv_codes = quantize(kv_rows, own_scales)
    count_all = lax.all_gather(shard_counts, "ctx", axis=0, tiled=True)
    offsets = jnp.cumsum(count_all) - count_all
    shard_total = count_all.shape[0]
    shard_ids = jnp.arange(shard_total, dtype=jnp.int32)
    query_pos = (
        span_starts[:, None]
        + ctx_id * query_rows
        + jnp.arange(query_rows, dtype=jnp.int32)[None, :]
    )
    query_mat = queries.reshape(query_sets, query_rows, kv_local, group_size, head_dim)
    query_mat = jnp.transpose(query_mat, (2, 0, 1, 3, 4)).reshape(
        kv_local, query_sets * query_rows * group_size, head_dim
    )
    row_pos = jnp.broadcast_to(query_pos[:, :, None], (query_sets, query_rows, group_size)).reshape(
        -1
    )
    latest = jnp.max(query_pos)
    slot_count = tok_rows // BLK
    page_total = block_slots.shape[0]
    page_ids = jnp.arange(page_total, dtype=jnp.int32)
    target_ids = jnp.arange(tok_rows, dtype=jnp.int32)
    key_scale = own_scales[:, 0]
    value_scale = own_scales[:, 1]
    row_total = row_pos.shape[0]

    def attend(running, key_codes, value_codes, is_valid, key_pos):
        row_max, row_sum, weighted_sum = running
        scores = (
            jnp.einsum("jrd,njd->jrn", query_mat, key_codes, preferred_element_type=jnp.float32)
            * key_scale[:, None, None]
        )
        counted = (is_valid[None, :] & (key_pos[None, :] <= row_pos[:, None]))[None]
        scores = jnp.where(counted, scores, -1e30)
        new_max = jnp.maximum(row_max, jnp.max(scores, axis=2))
        weights = jnp.where(counted, jnp.exp(scores - new_max[:, :, None]), 0.0)
        row_sum = jnp.sum(weights, axis=2)
        weighted_sum = jnp.einsum(
            "jrn,njd->jrd",
            weights.astype(jnp.bfloat16),
            value_codes,
            preferred_element_type=jnp.float32,
        )
        return (new_max, row_sum, weighted_sum)

    paired = lax.all_gather(kv_codes, "rep", axis=1, tiled=True)
    kv_piece = lax.all_gather(paired, "ctx", axis=0, tiled=True)
    row_count = kv_piece.shape[0]
    row_ids = jnp.arange(row_count, dtype=jnp.int32)
    shard_id = row_ids // tok_rows
    within = row_ids % tok_rows
    matches = shard_id[:, None] == shard_ids[None, :]
    shard_len = jnp.sum(jnp.where(matches, count_all[None, :], 0), axis=1)
    shard_base = jnp.sum(jnp.where(matches, offsets[None, :], 0), axis=1)
    is_valid = within < shard_len
    key_pos = shard_base + within
    own_heads = lax.dynamic_slice_in_dim(kv_piece, rep_id * kv_local, kv_local, 1)
    needed = jnp.any(is_valid & (key_pos <= latest))
    running = lax.cond(
        needed,
        lambda current: attend(
            current, own_heads[:, :, :head_dim], own_heads[:, :, head_dim:], is_valid, key_pos
        ),
        lambda current: current,
        (
            jnp.full((kv_local, row_total), -1e30, jnp.float32),
            jnp.zeros((kv_local, row_total), jnp.float32),
            jnp.zeros((kv_local, row_total, head_dim), jnp.float32),
            jnp.zeros((tok_rows, paired.shape[1], row_width), jnp.float32),
        )[:3],
    )
    block_id = key_pos // BLK
    slot_full = jnp.sum(
        jnp.where(block_id[:, None] == page_ids[None, :], block_slots[None, :], 0), axis=1
    )
    slot_id = slot_full - ctx_id * slot_count
    owned = is_valid & (slot_id >= 0) & (slot_id < slot_count)
    target = jnp.where(owned, slot_id * BLK + key_pos % BLK, -1)
    select = (target_ids[:, None] == target[None, :]).astype(jnp.bfloat16)
    moved = jnp.einsum("ti,ihw->thw", select, kv_piece, preferred_element_type=jnp.float32)
    folded = running + (moved,)
    decode_codes = folded[3]
    row_sum = folded[1]
    weighted_sum = folded[2]
    result = (weighted_sum * value_scale[:, None, None] / row_sum[:, :, None]).astype(jnp.bfloat16)
    result = result.reshape(kv_local, query_sets, query_rows, group_size, head_dim)
    attention = jnp.transpose(result, (1, 2, 0, 3, 4)).reshape(query_sets, query_rows, query_width)
    pair_scales = lax.dynamic_slice_in_dim(
        kv_scales, head_id * rep_size * kv_local, rep_size * kv_local, 0
    )
    decode_cache = dequantize(decode_codes, pair_scales)
    return (attention, decode_cache)


def solution(mesh):
    in_specs = (
        P(("groups", "ctx"), ("head", "rep"), None),
        P(),
        P(None, ("groups", "ctx"), ("head", "rep")),
        P(("groups", "ctx")),
        P("groups"),
        P("groups"),
    )
    out_specs = (P(None, ("groups", "ctx"), ("head", "rep")), P(("groups", "ctx"), "head", None))
    return jax.shard_map(body, mesh=mesh, in_specs=in_specs, out_specs=out_specs, check_vma=False)
```

profile of v0, /device:TPU:0, one launch (start us, length us, event | category | flops | bytes accessed | tf_op | source)
XLA Modules:
  0.0 88.9 jit_solution(922267862463995841)
XLA Ops:
  7.3 0.6 copy-done
  7.9 0.1 copy.31
  8.1 1.1 %reshape.202 = bf16[768,128]{1,0:T(8,128)(2,1)S(1)} reshape(bf16[192,2,256]{2,1,0:T(2,128)(2,1)} %param.8) | data formatting | bytes 393216 | tf_op jit(solution)/shard_map/reshape | solution.py:25
  9.2 0.3 fusion.13
  9.4 0.2 copy.30
  9.6 0.3 reshape.203
  9.9 0.2 clamp_convert_fusion
  10.1 2.3 %all_gather.10 = bf16[192,4,256]{2,0,1:T(8,128)(2,1)} all-gather(bf16[192,2,256]{2,0,1:T(8,128)(2,1)S(1)} %copy.32), channel_id=1, replica_groups=mesh['groups'=2,'ctx'=4,'head'=2,'rep'=2] {'rep'}, dimensions={1}, use_global_device_ids=true | all-gather | bytes 589824 | tf_op jit(solution)/shard_map/all_gather | solution.py:97
  13.1 1.2 %dynamic-slice = u32[1]{0:T(128)} dynamic-slice(u32[32]{0:T(128)} %constant.118, u32[]{:T(128)S(6)} %add.138), dynamic_slice_sizes={1} | dynamic-slice | bytes 12
  14.3 0.8 dynamic-update-slice
  15.1 9.8 %all-reduce = s32[4]{0:T(128)S(1)} all-reduce(s32[4]{0:T(128)S(1)} %dynamic-update-slice), channel_id=1, replica_groups=mesh['groups'=2,'ctx'=4,'head'=2,'rep'=2] {'ctx'}, use_global_device_ids=true, to_apply=%add | all-reduce | flops 4 | bytes 32
  24.9 0.2 reduce-window.9
  25.1 1.4 %copy.39 = bf16[16,8,32,128]{3,2,1,0:T(8,128)(2,1)S(1)} copy(bf16[16,8,32,128]{3,1,2,0:T(8,128)(2,1)} %bitcast.55) | data formatting | bytes 2097152
  26.6 0.7 add_reduce_fusion
  27.3 0.1 select_reduce_fusion.1
  27.4 0.1 select_reduce_fusion
  27.5 1.3 %and_reduce_fusion = pred[]{:T(512)} fusion(pred[768]{0:T(1024)(128)(4,1)S(1)} %get-tuple-element.129, s32[]{:T(128)} %add_reduce_fusion, s32[768]{0:T(1024)S(1)} %get-tuple-element.126), kind=kLoop, calls=%fused_computation.63 | loop fusion | flops 7679 | bytes 3845 | tf_op jit(solution)/shard_map/reduce_or | solution.py:109
  29.4 0.1 constant_dynamic-slice_fusion.1
  29.5 0.1 copy.35
  29.7 22.6 %all-gather.2.cloned.1.call-done = bf16[768,4,256]{2,0,1:T(8,128)(2,1)} async-done(((bf16[192,4,256]{2,0,1:T(8,128)(2,1)}), bf16[768,4,256]{2,0,1:T(8,128)(2,1)}) %all-gather.2.cloned.1.call-update) | async-done | bytes 1572880 | tf_op jit(solution)/shard_map/all_gather | solution.py:98
  52.3 24.2 %conditional.1 = (f32[2,2048]{1,0:T(2,128)S(1)}, f32[2,2048,128]{2,1,0:T(8,128)S(1)}) conditional(s32[]{:T(128)} %convert_element_type.19, () %tuple.21, (pred[768]{0:T(1024)(128)(4,1)S(1)}, s32[768]{0:T(1024)S(1)}, s32[2]{0:T(128)S(1)}, s32[2,64,1]{1,0,2:T(2,128)S(1)}, s32[]{:T(128)}, /*index=5*/bf16[768,4,256]{2,0,1:T(8,128)(2,1)}, ...), branch_computations={%region_5.6_spmd, %region_6.9_spmd} | conditional | flops 1654648960 | bytes 62789052 | solution.py:110
  52.5 0.1 le.22
  52.5 1.3 %compare_and_fusion = pred[2048,768]{0,1:T(8,128)(4,1)S(1)} fusion(s32[2048]{0:T(1024)S(1)} %le.22, s32[768]{0:T(1024)S(1)} %get-tuple-element.81, pred[768]{0:T(1024)(128)(4,1)S(1)} %get-tuple-element.80), kind=kLoop, calls=%fused_computation.7 | loop fusion | flops 3145728 | bytes 1584896 | tf_op jit(solution)/shard_map/cond/branch_1_fun/and | solution.py:84
  53.9 0.2 copy.33
  54.1 7.2 %fusion = (f32[2,2048]{1,0:T(2,128)S(1)}, f32[2,768,2048]{2,1,0:T(8,128)}) fusion(f32[2]{0:T(128)S(1)} %slice_bitcast_fusion, pred[2048,768]{0,1:T(8,128)(4,1)S(1)} %compare_and_fusion, bf16[2,2048,128]{2,1,0:T(8,128)(2,1)S(1)} %bitcast.56, bf16[768,4,256]{2,0,1:T(8,128)(2,1)} %get-tuple-element.84, s32[]{:T(128)S(6)} %select_n.70), kind=kOutput, calls=%fused_computation.2 | convolution fusion | flops 814739456 | bytes 15613964 | tf_op jit(solution)/shard_map/cond/branch_1_fun/jrd,njd->jrn/dot_general | solution.py:81
  61.3 8.4 %fusion.3 = f32[2,2048,128]{2,1,0:T(8,128)S(1)} fusion(f32[2,768,2048]{2,1,0:T(8,128)} %get-tuple-element.131, f32[2,2048]{1,0:T(2,128)S(1)} %broadcast_maximum_fusion, f32[2]{0:T(128)S(1)} %slice_bitcast_fusion, pred[2048,768]{0,1:T(8,128)(4,1)} %copy-done.1, bf16[768,4,256]{2,0,1:T(8,128)(2,1)} %get-tuple-element.84, s32[]{:T(128)S(6)} %select_n.70, ...), kind=kOutput, calls=%fused_computation.5 | convolution fusion | flops 821035008 | bytes 16662544 | tf_op jit(solution)/shard_map/cond/branch_1_fun/jrn,njd->jrd/dot_general | solution.py:89
  69.7 6.8 %fusion.2 = f32[2,2048]{1,0:T(2,128)S(1)} fusion(f32[2,768,2048]{2,1,0:T(8,128)} %get-tuple-element.131, f32[2,2048]{1,0:T(2,128)S(1)} %broadcast_maximum_fusion, f32[2]{0:T(128)S(1)} %slice_bitcast_fusion, pred[2048,768]{0,1:T(8,128)(4,1)S(1)} %copy-done.2), kind=kLoop, calls=%fused_computation.4 | loop fusion | flops 15724544 | bytes 14188552 | tf_op jit(solution)/shard_map/cond/branch_1_fun/reduce_sum | solution.py:88
  76.5 0.7 divide_convert_fusion
  77.3 0.2 copy.44
  77.5 1.3 %reshape.206 = bf16[2,64,4096]{2,1,0:T(8,128)(2,1)} reshape(bf16[2,64,2,16,128]{4,3,2,1,0:T(8,128)(2,1)S(1)} %bitcast.54) | data formatting | bytes 2097152 | tf_op jit(solution)/shard_map/reshape | solution.py:138
  78.7 1.9 %convolution_multiply_fusion = f32[192,4,256]{2,0,1:T(8,128)S(1)} fusion(bf16[768,4,256]{2,0,1:T(8,128)(2,1)} %all-gather.2.cloned.1.call-done, f32[4,256]{1,0:T(4,128)S(1)} %bitcast.57, s32[768]{0:T(1024)S(1)} %get-tuple-element.128), kind=kOutput, calls=%fused_computation.19 | convolution fusion | flops 302333952 | bytes 2366464 | tf_op jit(solution)/shard_map/ti,ihw->thw/dot_general | solution.py:131
  80.6 1.4 %copy.36 = f32[192,4,256]{2,1,0:T(4,128)} copy(f32[192,4,256]{2,0,1:T(8,128)S(1)} %convolution_multiply_fusion) | data formatting | bytes 1572864
  (29 shorter events, 0.6 us)
Async XLA Ops:
  7.2 0.7 copy-start
  7.2 19.4 %copy-start.4 = (s32[2]{0:T(128)S(1)}, s32[2]{0:T(128)}, u32[]{:S(2)}) copy-start(s32[2]{0:T(128)} %param.12) | copy-start | bytes 28
  7.2 20.2 %copy-start.3 = (s32[48]{0:T(128)S(1)}, s32[48]{0:T(128)}, u32[]{:S(2)}) copy-start(s32[48]{0:T(128)} %param.13) | copy-start | bytes 580
  7.2 45.1 %all-gather.2.cloned.1.call-start = ((), (), s32[]{:S(2)}) async-start(), calls=%async_computation | async-start | bytes 1966080 | tf_op jit(solution)/shard_map/all_gather | solution.py:98
  53.9 7.4 %copy-start.1 = (pred[2048,768]{0,1:T(8,128)(4,1)}, pred[2048,768]{0,1:T(8,128)(4,1)S(1)}, u32[]{:S(2)}) copy-start(pred[2048,768]{0,1:T(8,128)(4,1)S(1)} %compare_and_fusion) | copy-start | bytes 4718596 | tf_op jit(solution)/shard_map/cond
  61.3 8.4 %copy-start.2 = (pred[2048,768]{0,1:T(8,128)(4,1)S(1)}, pred[2048,768]{0,1:T(8,128)(4,1)}, u32[]{:S(2)}) copy-start(pred[2048,768]{0,1:T(8,128)(4,1)} %copy-done.1) | copy-start | bytes 4718596 | tf_op jit(solution)/shard_map/cond
Sparse Core Ops, SparseCore 0:
  12.5 39.7 all-gather.1
where the time goes:
time: 89.2 us; the launch traced here: 88.9 us
  waiting for transfers between devices  22.6 us (25%)
  matrix products  17.7 us (20%)
  between operations  15.5 us (17%)
  blocking collectives  12.1 us (14%)
  other arithmetic  11.5 us (13%)
  local copies, waits for them, and re-layouts  9.25 us (10%)
    all_gather x1, waiting for transfers between devices, body(): kv_piece = lax.all_gather(paired, 'ctx', axis=0, tiled=True)  22.6 us
    unnamed x1, blocking collectives  9.81 us
    dot_general x1, matrix products, attend(): jnp.einsum('jrn,njd->jrd', weights.astype(jnp.bfloat16), value_codes, pre...  8.37 us
    dot_general x1, matrix products, attend(): jnp.einsum('jrd,njd->jrn', query_mat, key_codes, preferred_element_type=j...  7.22 us
    reduce_sum x1, other arithmetic, attend(): row_sum = jnp.sum(weights, axis=2)  6.81 us
    unnamed x15, local copies, waits for them, and re-layouts  5.6 us
    all_gather x1, blocking collectives, body(): paired = lax.all_gather(kv_codes, 'rep', axis=1, tiled=True)  2.3 us
    dot_general x1, matrix products, body(): jnp.einsum('ti,ihw->thw', select, kv_piece, preferred_element_type=jnp.fl...  1.88 us
  transfers between devices with their start and end apart: 1, of which 1 were waited for; matrix products, arithmetic and copies ran while one was open for 7% of the time, Pallas kernels for 0%

commit v1 on v0

v1 whole, which is shorter than its diff:
```python
import functools
import math

import jax
import jax.numpy as jnp
from jax import lax
from jax.experimental import pallas as pl
from jax.experimental.pallas import tpu as pltpu
from jax.sharding import PartitionSpec as P

BLK = 16
FLOOR = -1e9
MASKED = -1e30
LOG2E = math.log2(math.e)
VMEM_LIMIT = 48 * 1024 * 1024
SMEM_SPEC = pl.BlockSpec(memory_space=pltpu.SMEM)
VMEM_SPEC = pl.BlockSpec(memory_space=pltpu.VMEM)


def sign_pair(width):
    half = width // 2
    row = lax.broadcasted_iota(jnp.int32, (width, width), 0)
    col = lax.broadcasted_iota(jnp.int32, (width, width), 1)
    parity = row & col & (half - 1)
    parity = parity ^ (parity >> 4)
    parity = parity ^ (parity >> 2)
    parity = (parity ^ (parity >> 1)) & 1
    same = (row >= half) == (col >= half)
    return jnp.where(same, (1 - 2 * parity).astype(jnp.float32), 0.0).astype(jnp.bfloat16)


def codes_of(rows_ref, scale_of, signs, rot_scr):
    tokens, heads, width = rows_ref.shape
    half = width // 2
    flat = rows_ref[...].reshape(tokens * heads, width)
    rotated = jnp.dot(flat, signs, preferred_element_type=jnp.float32)
    rotated = rotated * (1.0 / math.sqrt(half))
    for w in range(2):
        rot_scr[w] = rotated[:, w * half : (w + 1) * half]
    found = []
    for j in range(heads):
        parts = []
        for w in range(2):
            own = rot_scr[w, pl.ds(j, tokens, stride=heads), :] if heads > 1 else rot_scr[w]
            parts.append(jnp.clip(own / scale_of(j, w), -448.0, 448.0).astype(jnp.bfloat16))
        found.append(parts)
    return found


def page_places(slots_ref, ctx_id, tokens):
    pages = slots_ref.shape[1]
    row = lax.broadcasted_iota(jnp.int32, (tokens, pages), 0)
    page = lax.broadcasted_iota(jnp.int32, (tokens, pages), 1)
    slot = ctx_id * (tokens // BLK) + (row >> 4)
    place = (page * BLK + (row & (BLK - 1))).astype(jnp.float32)
    hit = jnp.broadcast_to(slots_ref[...], (tokens, pages)) == slot
    return jnp.sum(jnp.where(hit, place, 0.0), axis=1, keepdims=True)


def picker(place, offset, count, tokens):
    key = lax.broadcasted_iota(jnp.int32, (tokens, tokens), 1)
    key_pos = (key + offset).astype(jnp.float32)
    hit = (jnp.broadcast_to(place, (tokens, tokens)) == key_pos) & (key < count)
    return jnp.where(hit, 1.0, 0.0).astype(jnp.bfloat16)


def span_of(meta, steps, tokens):
    if len(meta) == 1:
        return [(meta[0][0, 0], meta[0][0, 1])]
    me = lax.axis_index("ctx")
    known = [meta[0][0], meta[1][0], meta[2][0]]
    known.append(tokens * 3 - known[0] - known[1] - known[2])
    spans = []
    for step in steps:
        ident = me ^ step
        offset = jnp.int32(0)
        for other in range(4):
            offset = offset + jnp.where((me ^ other) < ident, known[other], 0)
        spans.append((offset, known[step]))
    return spans


def attend_kernel(metas, steps, has_state, last, with_pages, *refs):
    refs = list(refs)
    meta = [refs.pop(0) for _ in range(metas)]
    start_ref, scale_ref, query_ref = refs.pop(0), refs.pop(0), refs.pop(0)
    rows_refs = [refs.pop(0) for _ in steps]
    state = [refs.pop(0) for _ in range(3)] if has_state else None
    slots_ref = refs.pop(0) if with_pages else None
    if last:
        out_ref = refs.pop(0)
    else:
        acc_out, sum_out, top_out = refs.pop(0), refs.pop(0), refs.pop(0)
    moved_out = refs.pop(0) if with_pages else None
    rot_scr, score_scr, prob_scr = refs

    tokens, heads, width = rows_refs[0].shape
    half = width // 2
    sets, rows, query_width = query_ref.shape
    group = query_width // half // heads
    shards = len(steps)
    ctx_id = lax.axis_index("ctx")
    first_head = (lax.axis_index("head") * lax.axis_size("rep") + lax.axis_index("rep")) * heads
    spans = span_of(meta, steps, tokens)

    def scale_of(j, which):
        return scale_ref[which, first_head + j]

    signs = sign_pair(width)
    per_shard = [codes_of(r, scale_of, signs, rot_scr) for r in rows_refs]

    def joined(j, w):
        parts = [found[j][w] for found in per_shard]
        return jnp.concatenate(parts, axis=0) if shards > 1 else parts[0]

    keys = [joined(j, 0) for j in range(heads)]
    ones = jnp.ones((shards * tokens, half), jnp.bfloat16)
    values = [jnp.concatenate([joined(j, 1), ones], axis=1) for j in range(heads)]
    row = lax.broadcasted_iota(jnp.int32, (rows, tokens), 0)
    key = lax.broadcasted_iota(jnp.int32, (rows, tokens), 1)
    for c in range(sets):
        base = start_ref[c] + ctx_id * rows
        parts = []
        for offset, count in spans:
            counted = (key < count) & (key + offset <= base + row)
            parts.append(jnp.where(counted, 0.0, MASKED))
        bias = jnp.concatenate(parts, axis=1) if shards > 1 else parts[0]
        for j in range(heads):
            factor = scale_of(j, 0) * LOG2E
            stacked = jnp.concatenate(
                [
                    query_ref[c, :, (j * group + g) * half : (j * group + g + 1) * half]
                    for g in range(group)
                ],
                axis=0,
            )
            slot = (c * heads + j) % 2
            score_scr[slot] = lax.dot_general(
                stacked, keys[j], (((1,), (1,)), ((), ())), preferred_element_type=jnp.float32
            )
            alphas = []
            for g in range(group):
                here = slice(g * rows, (g + 1) * rows)
                scores = score_scr[slot, here, :] + bias
                top = jnp.max(scores, axis=1, keepdims=True)
                if has_state:
                    before = state[2][c, j, here, :]
                    after = jnp.maximum(jnp.broadcast_to(top, before.shape), before)
                    alphas.append(jnp.exp2((before - after) * factor))
                    top = after[:, :1]
                else:
                    top = jnp.maximum(top, FLOOR)
                probs = jnp.exp2((scores - top) * factor)
                prob_scr[slot, here, :] = probs.astype(jnp.bfloat16)
                if not last:
                    top_out[c, j, here, :] = jnp.broadcast_to(top, (rows, half))
            weighted = jnp.dot(prob_scr[slot], values[j], preferred_element_type=jnp.float32)
            for g in range(group):
                h = j * group + g
                here = slice(g * rows, (g + 1) * rows)
                acc = weighted[here, :half]
                total = weighted[here, half:]
                if has_state:
                    acc = acc + state[0][c, j, here, :] * alphas[g]
                    total = total + state[1][c, j, here, :] * alphas[g]
                if last:
                    result = acc * scale_of(j, 1) / total
                    out_ref[c, :, h * half : (h + 1) * half] = result.astype(jnp.bfloat16)
                else:
                    acc_out[c, j, here, :] = acc
                    sum_out[c, j, here, :] = total

    if with_pages:
        place = page_places(slots_ref, ctx_id, tokens)
        total = None
        for (offset, count), found in zip(spans, per_shard):
            pick = picker(place, offset, count, tokens)
            own = jnp.concatenate([part for parts in found for part in parts], axis=1)
            part = jnp.dot(pick, own, preferred_element_type=jnp.float32)
            total = part if total is None else total + part
        moved_out[...] = total.astype(jnp.bfloat16)


def attend(meta, steps, starts, scales, query, rows, state=None, last=False, slots=None):
    tokens, heads, width = rows[0].shape
    half = width // 2
    sets, query_rows, query_width = query.shape
    group = query_width // half // heads
    args = [*meta, starts, scales, query, *rows]
    specs = [SMEM_SPEC] * (len(meta) + 2) + [VMEM_SPEC] * (1 + len(rows))
    if state is not None:
        args += list(state)
        specs += [VMEM_SPEC] * 3
    if slots is not None:
        args.append(slots)
        specs.append(VMEM_SPEC)
    stacked = (sets, heads, group * query_rows, half)
    if last:
        outs = [jax.ShapeDtypeStruct(query.shape, jnp.bfloat16)]
    else:
        outs = [jax.ShapeDtypeStruct(stacked, jnp.float32)] * 3
    if slots is not None:
        outs.append(jax.ShapeDtypeStruct((tokens, heads * width), jnp.bfloat16))
    keys = tokens * len(rows)
    work = sets * heads * group * query_rows * keys
    return pl.pallas_call(
        functools.partial(
            attend_kernel, len(meta), steps, state is not None, last, slots is not None
        ),
        out_shape=outs,
        in_specs=specs,
        out_specs=[VMEM_SPEC] * len(outs),
        scratch_shapes=[
            pltpu.VMEM((2, tokens * heads, half), jnp.float32),
            pltpu.VMEM((2, group * query_rows, keys), jnp.float32),
            pltpu.VMEM((2, group * query_rows, keys), jnp.bfloat16),
        ],
        compiler_params=pltpu.CompilerParams(vmem_limit_bytes=VMEM_LIMIT),
        cost_estimate=pl.CostEstimate(
            flops=work * half * 8, bytes_accessed=4 << 20, transcendentals=work
        ),
    )(*args)


def cache_kernel(metas, steps, *refs):
    refs = list(refs)
    meta = [refs.pop(0) for _ in range(metas)]
    scale_ref, slots_ref, own, other, own_rows, other_rows, out_ref, rot_scr = refs
    tokens, heads, width = own_rows.shape
    half = width // 2
    ctx_id = lax.axis_index("ctx")
    rep_id = lax.axis_index("rep")
    pair_head = lax.axis_index("head") * lax.axis_size("rep") * heads
    signs = sign_pair(width)
    place = page_places(slots_ref, ctx_id, tokens)
    ((offset, count),) = span_of(meta, steps, tokens)
    pick = picker(place, offset, count, tokens)

    for turn in range(2):

        @pl.when(rep_id == turn)
        def _(turn=turn):
            for first, moved, rows in (
                (turn * heads, own, own_rows),
                ((1 - turn) * heads, other, other_rows),
            ):

                def scale_of(j, w, first=first):
                    return scale_ref[w, pair_head + first + j]

                found = codes_of(rows, scale_of, signs, rot_scr)
                for j in range(heads):
                    for w in range(2):
                        here = slice((2 * j + w) * half, (2 * j + w + 1) * half)
                        full = jnp.dot(pick, found[j][w], preferred_element_type=jnp.float32)
                        full = (full + moved[:, here].astype(jnp.float32)) * scale_of(j, w)
                        out_ref[:, first + j, w * half : (w + 1) * half] = full


def fill_cache(meta, steps, scales, slots, own, other, own_rows, other_rows):
    tokens, heads, width = own_rows.shape
    return pl.pallas_call(
        functools.partial(cache_kernel, len(meta), steps),
        out_shape=jax.ShapeDtypeStruct((tokens, 2 * heads, width), jnp.float32),
        in_specs=[SMEM_SPEC] * (len(meta) + 1) + [VMEM_SPEC] * 5,
        out_specs=VMEM_SPEC,
        scratch_shapes=[pltpu.VMEM((2, tokens * heads, width // 2), jnp.float32)],
        compiler_params=pltpu.CompilerParams(vmem_limit_bytes=VMEM_LIMIT),
        cost_estimate=pl.CostEstimate(
            flops=tokens * tokens * heads * width * 8, bytes_accessed=2 << 20, transcendentals=0
        ),
    )(*meta, scales, slots, own, other, own_rows, other_rows)


def pair(value, axis, step):
    size = lax.axis_size(axis)
    return lax.ppermute(value, axis, [(i, i ^ step) for i in range(size)])


def body(kv_rows, kv_scales, queries, shard_counts, span_starts, block_slots):
    scales = kv_scales.T
    slots = block_slots[None, :]
    across = pair(kv_rows, "ctx", 2)
    beside = pair(kv_rows, "ctx", 1)
    meta = [shard_counts, pair(shard_counts, "ctx", 1), pair(shard_counts, "ctx", 2)]
    corner = pair(across, "ctx", 1)
    *state, moved = attend(
        meta, (0, 1, 2), span_starts, scales, queries, [kv_rows, beside, across], slots=slots
    )
    moved_other = pair(moved, "rep", 1)
    corner_other = pair(corner, "rep", 1)
    (attention,) = attend(meta, (3,), span_starts, scales, queries, [corner], state, last=True)
    decode_cache = fill_cache(
        meta, (3,), scales, slots, moved, moved_other, corner, corner_other
    )
    return attention, decode_cache


def body_any(kv_rows, kv_scales, queries, shard_counts, span_starts, block_slots):
    tokens, heads, width = kv_rows.shape
    sets, query_rows, query_width = queries.shape
    half = width // 2
    group = query_width // half // heads
    scales = kv_scales.T
    slots = block_slots[None, :]
    counts = lax.all_gather(shard_counts, "ctx", axis=0, tiled=True)
    info = jnp.stack([jnp.cumsum(counts) - counts, counts], axis=1)
    every = lax.all_gather(kv_rows, "ctx", axis=0)

    def step(carry, turn):
        state, moved = carry
        rows, one = turn
        *state, found = attend(
            [one[None]], (0,), span_starts, scales, queries, [rows], state, slots=slots
        )
        return (tuple(state), moved + found), None

    stacked = (sets, heads, group * query_rows, half)
    state = (
        jnp.zeros(stacked, jnp.float32),
        jnp.zeros(stacked, jnp.float32),
        jnp.full(stacked, FLOOR, jnp.float32),
    )
    moved = jnp.zeros((tokens, heads * width), jnp.bfloat16)
    (state, moved), _ = lax.scan(step, (state, moved), (every[:-1], info[:-1]))
    attention, found = attend(
        [info[-1:]], (0,), span_starts, scales, queries, [every[-1]], state, last=True, slots=slots
    )
    moved = moved + found
    none = jnp.zeros((1, 2), jnp.int32)
    decode_cache = fill_cache(
        [none], (0,), scales, slots, moved, pair(moved, "rep", 1), kv_rows, kv_rows
    )
    return attention, decode_cache


def solution(mesh):
    in_specs = (
        P(("groups", "ctx"), ("head", "rep"), None),
        P(),
        P(None, ("groups", "ctx"), ("head", "rep")),
        P(("groups", "ctx")),
        P("groups"),
        P("groups"),
    )
    out_specs = (P(None, ("groups", "ctx"), ("head", "rep")), P(("groups", "ctx"), "head", None))
    chosen = body if mesh.shape["ctx"] == 4 else body_any
    return jax.shard_map(chosen, mesh=mesh, in_specs=in_specs, out_specs=out_specs, check_vma=False)
```

time: 89.2 us -> 38.8 us (0.43)
  Pallas kernels: 0 us -> 18.9 us
  matrix products: 17.7 us -> 0 us
  waiting for transfers between devices: 22.6 us -> 6.65 us
  between operations: 15.5 us -> 1.34 us
  blocking collectives: 12.1 us -> 0 us
  other arithmetic: 11.5 us -> 0 us
  starting transfers between devices: 0.04 us -> 7.45 us
  local copies, waits for them, and re-layouts: 9.25 us -> 4.14 us
    all_gather x1 -> x0, waiting for transfers between devices: 22.6 us -> none  [body(): kv_piece = lax.all_gather(paired, 'ctx', axis=0, tiled=True)]
    pallas_call x0 -> x3, Pallas kernels: none -> 18.9 us  [the longest x2 14.9 us: attend(): pl.pallas_call(functools.partial(attend_kernel, len(meta), steps, state i...]
    dot_general x4 -> x0, matrix products: 17.7 us -> none  [the longest x1 8.37 us: attend(): jnp.einsum('jrn,njd->jrd', weights.astype(jnp.bfloat16), value_codes, pre...]
    unnamed x1 -> x0, blocking collectives: 9.81 us -> none
    ppermute x0 -> x7, starting transfers between devices: none -> 7.45 us  [pair(): return lax.ppermute(value, axis, [(i, i ^ step) for i in range(size)])]
    reduce_sum x3 -> x0, other arithmetic: 6.99 us -> none  [the longest x1 6.81 us: attend(): row_sum = jnp.sum(weights, axis=2)]
    ppermute x0 -> x7, waiting for transfers between devices: none -> 6.65 us  [pair(): return lax.ppermute(value, axis, [(i, i ^ step) for i in range(size)])]
    reshape x4 -> x0, local copies, waits for them, and re-layouts: 2.77 us -> none  [the longest x1 1.27 us: body(): jnp.transpose(result, (1, 2, 0, 3, 4))]
  transfers between devices with their start and end apart: 1 -> 7, of which waited for: 1 -> 1; matrix products, arithmetic and copies ran while one was open for 7% -> 0% of each run, Pallas kernels for 0% -> 39%
where the time goes in v1:
time: 38.8 us; the launch traced here: 38.5 us
  Pallas kernels  18.9 us (49%)
  starting transfers between devices  7.45 us (19%)
  waiting for transfers between devices  6.65 us (17%)
  local copies, waits for them, and re-layouts  4.14 us (11%)
  between operations  1.34 us (3%)
    pallas_call x2, Pallas kernels, attend(): pl.pallas_call(functools.partial(attend_kernel, len(meta), steps, state i...  14.9 us
    ppermute x7, starting transfers between devices, pair(): return lax.ppermute(value, axis, [(i, i ^ step) for i in range(size)])  7.45 us
    ppermute x7, waiting for transfers between devices, pair(): return lax.ppermute(value, axis, [(i, i ^ step) for i in range(size)])  6.65 us
    unnamed x12, local copies, waits for them, and re-layouts  4.14 us
    pallas_call x1, Pallas kernels, fill_cache(): pl.pallas_call(functools.partial(cache_kernel, len(meta), steps), out_sha...  3.98 us
  transfers between devices with their start and end apart: 7, of which 1 were waited for; matrix products, arithmetic and copies ran while one was open for 0% of the time, Pallas kernels for 39%

profile of v1, /device:TPU:0, one launch (start us, length us, event | category | flops | bytes accessed | tf_op | source)
XLA Modules:
  0.0 38.5 jit_solution(4902509796364903826)
XLA Ops:
  0.6 4.1 %collective-permute-start.2 = (bf16[192,2,256]{2,1,0:T(2,128)(2,1)}, bf16[192,2,256]{2,1,0:T(2,128)(2,1)S(1)}, u32[]{:S(2)}, u32[]{:S(2)}) collective-permute-start(bf16[192,2,256]{2,1,0:T(2,128)(2,1)} %refs_6_.1), channel_id=1, source_target_pairs={{0,8},{4,12},{8,0},{12,4},{1,9},{5,13},{9,1},{13,5},{2,10},{6,14},... | collective-permute-start | bytes 589832 | tf_op jit(solution)/shard_map/ppermute | solution.py:277
  4.7 1.6 %collective-permute-start.4 = (bf16[192,2,256]{2,1,0:T(2,128)(2,1)}, bf16[192,2,256]{2,1,0:T(2,128)(2,1)S(1)}, u32[]{:S(2)}, u32[]{:S(2)}) collective-permute-start(bf16[192,2,256]{2,1,0:T(2,128)(2,1)} %refs_6_.1), channel_id=1, source_target_pairs={{0,4},{4,0},{8,12},{12,8},{1,5},{5,1},{9,13},{13,9},{2,6},{6,2},{1... | collective-permute-start | bytes 589832 | tf_op jit(solution)/shard_map/ppermute | solution.py:277
  6.3 0.4 %collective-permute-start = (s32[1]{0:T(128)}, s32[1]{0:T(128)}, u32[]{:S(2)}, u32[]{:S(2)}) collective-permute-start(s32[1]{0:T(128)} %param.9), channel_id=1, source_target_pairs={{0,4},{4,0},{8,12},{12,8},{1,5},{5,1},{9,13},{13,9},{2,6},{6,2},{1... | collective-permute-start | bytes 20 | tf_op jit(solution)/shard_map/ppermute | solution.py:277
  6.8 0.1 collective-permute-start.1
  7.5 6.6 %collective-permute-done.2.refs_8_ = bf16[192,2,256]{2,1,0:T(2,128)(2,1)S(1)} collective-permute-done((bf16[192,2,256]{2,1,0:T(2,128)(2,1)}, bf16[192,2,256]{2,1,0:T(2,128)(2,1)S(1)}, u32[]{:S(2)}, u32[]{:S(2)}) %collective-permute-start.2) | collective-permute-done | bytes 196640 | tf_op jit(solution)/shard_map/ppermute | solution.py:277
  14.2 0.7 %collective-permute-start.3 = (bf16[192,2,256]{2,1,0:T(2,128)(2,1)S(1)}, bf16[192,2,256]{2,1,0:T(2,128)(2,1)S(1)}, u32[]{:S(2)}, u32[]{:S(2)}) collective-permute-start(bf16[192,2,256]{2,1,0:T(2,128)(2,1)S(1)} %collective-permute-done.2.refs_8_), channel_id=1, source_target_pairs={{0,4},{4,0},{8,12},{12,8},{1,5},{5,1},{9,13},{13,9},{2,6},{6,2},{1... | collective-permute-start | bytes 589832 | tf_op jit(solution)/shard_map/ppermute | solution.py:277
  14.9 0.0 collective-permute-done.refs_1_
  14.9 0.0 collective-permute-done.1.refs_2_
  14.9 0.0 collective-permute-done.4.refs_7_
  14.9 0.0 copy-start
  14.9 1.2 %copy-done = bf16[2,64,4096]{2,1,0:T(8,128)(2,1)S(1)} copy-done((bf16[2,64,4096]{2,1,0:T(8,128)(2,1)S(1)}, bf16[2,64,4096]{2,1,0:T(8,128)(2,1)}, u32[]{:S(2)}) %copy-start) | copy-done | bytes 1048600
  16.1 0.0 copy-start.1
  16.1 0.7 %copy-done.1 = f32[8,2]{0,1:T(2,128)S(1)} copy-done((f32[8,2]{0,1:T(2,128)S(1)}, f32[8,2]{0,1:T(2,128)}, u32[]{:S(2)}) %copy-start.1) | copy-done | bytes 88
  16.8 0.0 copy-start.3
  16.8 0.7 %copy-done.3 = s32[2]{0:T(128)S(1)} copy-done((s32[2]{0:T(128)S(1)}, s32[2]{0:T(128)}, u32[]{:S(2)}) %copy-start.3) | copy-done | bytes 32
  17.5 0.0 copy-start.4
  17.5 0.7 %copy-done.4 = s32[48]{0:T(128)S(1)} copy-done((s32[48]{0:T(128)S(1)}, s32[48]{0:T(128)}, u32[]{:S(2)}) %copy-start.4) | copy-done | bytes 216
  18.1 0.0 copy-start.5
  18.1 0.9 %copy-done.5 = bf16[192,2,256]{2,1,0:T(2,128)(2,1)S(1)} copy-done((bf16[192,2,256]{2,1,0:T(2,128)(2,1)S(1)}, bf16[192,2,256]{2,1,0:T(2,128)(2,1)}, u32[]{:S(2)}) %copy-start.5) | copy-done | bytes 196632
  19.1 7.2 %shard_map.77 = (f32[2,2,1024,128]{3,2,1,0:T(8,128)S(1)}, f32[2,2,1024,128]{3,2,1,0:T(8,128)S(1)}, f32[2,2,1024,128]{3,2,1,0:T(8,128)}, bf16[192,512]{1,0:T(8,128)(2,1)S(1)}) custom-call(s32[1]{0:T(128)S(6)} %copy.8.refs_0_, s32[1]{0:T(128)} %collective-permute-done.refs_1_, s32[1]{0:T(128)} %collective-permute-done.1.refs_2_, s32[2]{0:T(128)S(1)} %copy-done.3, ...), custom_call_target="tpu_custom_call" | custom-call | flops 2415919104 | bytes 4194304 | tf_op jit(solution)/shard_map/pallas_call | solution.py:206
  26.3 0.0 collective-permute-start.5
  26.3 0.0 collective-permute-done.3.refs_6_.refs_7_
  26.3 0.5 %collective-permute-start.6 = (bf16[192,2,256]{2,1,0:T(2,128)(2,1)S(1)}, bf16[192,2,256]{2,1,0:T(2,128)(2,1)S(1)}, u32[]{:S(2)}, u32[]{:S(2)}) collective-permute-start(bf16[192,2,256]{2,1,0:T(2,128)(2,1)S(1)} %collective-permute-done.3.refs_6_.refs_7_), channel_id=1, source_target_pairs={{0,1},{1,0},{2,3},{3,2},{4,5},{5,4},{6,7},{7,6},{8,9},{9,8},{10,11... | collective-permute-start | bytes 589832 | tf_op jit(solution)/shard_map/ppermute | solution.py:277
  26.8 0.0 copy-start.2
  26.8 7.7 %shard_map.78 = bf16[2,64,4096]{2,1,0:T(8,128)(2,1)} custom-call(s32[1]{0:T(128)S(6)} %copy.8.refs_0_, s32[1]{0:T(128)} %collective-permute-done.refs_1_, s32[1]{0:T(128)} %collective-permute-done.1.refs_2_, s32[2]{0:T(128)S(1)} %copy-done.3, f32[2,8]{1,0:T(2,128)S(1)} %bitcast.3, bf16[2,64,4096]{2,1,0:T(8,128)(2,1)S(1)} %copy-done, ...), custom_call_target="tpu_custom_call" | custom-call | flops 805306368 | bytes 4194304 | tf_op jit(solution)/shard_map/pallas_call | solution.py:206
  34.5 0.0 collective-permute-done.5.refs_6_
  34.5 0.0 collective-permute-done.6.refs_8_
  34.5 0.0 copy-done.2
  34.5 4.0 %shard_map.79 = f32[192,4,256]{2,1,0:T(4,128)} custom-call(s32[1]{0:T(128)S(6)} %copy.8.refs_0_, s32[1]{0:T(128)} %collective-permute-done.refs_1_, s32[1]{0:T(128)} %collective-permute-done.1.refs_2_, f32[2,8]{1,0:T(2,128)S(1)} %bitcast.4, s32[1,48]{1,0:T(1,128)S(1)} %bitcast.6, bf16[192,512]{1,0:T(8,128)(2,1)S(1)} %get-tuple-element.9.refs_5_, ...), custom_call_target="tpu_custom_call" | custom-call | flops 150994944 | bytes 2097152 | tf_op jit(solution)/shard_map/pallas_call | solution.py:262
Async XLA Ops:
  0.6 13.5 %collective-permute-start.2 = (bf16[192,2,256]{2,1,0:T(2,128)(2,1)}, bf16[192,2,256]{2,1,0:T(2,128)(2,1)S(1)}, u32[]{:S(2)}, u32[]{:S(2)}) collective-permute-start(bf16[192,2,256]{2,1,0:T(2,128)(2,1)} %refs_6_.1), channel_id=1, source_target_pairs={{0,8},{4,12},{8,0},{12,4},{1,9},{5,13},{9,1},{13,5},{2,10},{6,14},... | collective-permute-start | bytes 589832 | tf_op jit(solution)/shard_map/ppermute | solution.py:277
  4.7 10.2 %collective-permute-start.4 = (bf16[192,2,256]{2,1,0:T(2,128)(2,1)}, bf16[192,2,256]{2,1,0:T(2,128)(2,1)S(1)}, u32[]{:S(2)}, u32[]{:S(2)}) collective-permute-start(bf16[192,2,256]{2,1,0:T(2,128)(2,1)} %refs_6_.1), channel_id=1, source_target_pairs={{0,4},{4,0},{8,12},{12,8},{1,5},{5,1},{9,13},{13,9},{2,6},{6,2},{1... | collective-permute-start | bytes 589832 | tf_op jit(solution)/shard_map/ppermute | solution.py:277
  6.3 8.6 %collective-permute-start = (s32[1]{0:T(128)}, s32[1]{0:T(128)}, u32[]{:S(2)}, u32[]{:S(2)}) collective-permute-start(s32[1]{0:T(128)} %param.9), channel_id=1, source_target_pairs={{0,4},{4,0},{8,12},{12,8},{1,5},{5,1},{9,13},{13,9},{2,6},{6,2},{1... | collective-permute-start | bytes 20 | tf_op jit(solution)/shard_map/ppermute | solution.py:277
  6.8 8.1 %collective-permute-start.1 = (s32[1]{0:T(128)}, s32[1]{0:T(128)}, u32[]{:S(2)}, u32[]{:S(2)}) collective-permute-start(s32[1]{0:T(128)} %param.9), channel_id=1, source_target_pairs={{0,8},{4,12},{8,0},{12,4},{1,9},{5,13},{9,1},{13,5},{2,10},{6,14},... | collective-permute-start | bytes 20 | tf_op jit(solution)/shard_map/ppermute | solution.py:277
  14.2 12.1 %collective-permute-start.3 = (bf16[192,2,256]{2,1,0:T(2,128)(2,1)S(1)}, bf16[192,2,256]{2,1,0:T(2,128)(2,1)S(1)}, u32[]{:S(2)}, u32[]{:S(2)}) collective-permute-start(bf16[192,2,256]{2,1,0:T(2,128)(2,1)S(1)} %collective-permute-done.2.refs_8_), channel_id=1, source_target_pairs={{0,4},{4,0},{8,12},{12,8},{1,5},{5,1},{9,13},{13,9},{2,6},{6,2},{1... | collective-permute-start | bytes 589832 | tf_op jit(solution)/shard_map/ppermute | solution.py:277
  14.9 1.2 %copy-start = (bf16[2,64,4096]{2,1,0:T(8,128)(2,1)S(1)}, bf16[2,64,4096]{2,1,0:T(8,128)(2,1)}, u32[]{:S(2)}) copy-start(bf16[2,64,4096]{2,1,0:T(8,128)(2,1)} %refs_5_.3) | copy-start | bytes 3145732
  16.1 0.7 %copy-start.1 = (f32[8,2]{0,1:T(2,128)S(1)}, f32[8,2]{0,1:T(2,128)}, u32[]{:S(2)}) copy-start(f32[8,2]{0,1:T(2,128)} %param.7) | copy-start | bytes 196
  16.8 0.7 %copy-start.3 = (s32[2]{0:T(128)S(1)}, s32[2]{0:T(128)}, u32[]{:S(2)}) copy-start(s32[2]{0:T(128)} %refs_3_.3) | copy-start | bytes 28
  17.5 0.7 %copy-start.4 = (s32[48]{0:T(128)S(1)}, s32[48]{0:T(128)}, u32[]{:S(2)}) copy-start(s32[48]{0:T(128)} %param.11) | copy-start | bytes 580
  18.1 0.9 %copy-start.5 = (bf16[192,2,256]{2,1,0:T(2,128)(2,1)S(1)}, bf16[192,2,256]{2,1,0:T(2,128)(2,1)}, u32[]{:S(2)}) copy-start(bf16[192,2,256]{2,1,0:T(2,128)(2,1)} %refs_6_.1) | copy-start | bytes 589828
  26.3 8.2 %collective-permute-start.5 = (bf16[192,512]{1,0:T(8,128)(2,1)S(1)}, bf16[192,512]{1,0:T(8,128)(2,1)S(1)}, u32[]{:S(2)}, u32[]{:S(2)}) collective-permute-start(bf16[192,512]{1,0:T(8,128)(2,1)S(1)} %get-tuple-element.9.refs_5_), channel_id=1, source_target_pairs={{0,1},{1,0},{2,3},{3,2},{4,5},{5,4},{6,7},{7,6},{8,9},{9,8},{10,11... | collective-permute-start | bytes 589832 | tf_op jit(solution)/shard_map/ppermute | solution.py:277
  26.3 8.2 %collective-permute-start.6 = (bf16[192,2,256]{2,1,0:T(2,128)(2,1)S(1)}, bf16[192,2,256]{2,1,0:T(2,128)(2,1)S(1)}, u32[]{:S(2)}, u32[]{:S(2)}) collective-permute-start(bf16[192,2,256]{2,1,0:T(2,128)(2,1)S(1)} %collective-permute-done.3.refs_6_.refs_7_), channel_id=1, source_target_pairs={{0,1},{1,0},{2,3},{3,2},{4,5},{5,4},{6,7},{7,6},{8,9},{9,8},{10,11... | collective-permute-start | bytes 589832 | tf_op jit(solution)/shard_map/ppermute | solution.py:277
  26.8 7.7 %copy-start.2 = (f32[8,2]{0,1:T(2,128)S(1)}, f32[8,2]{0,1:T(2,128)}, u32[]{:S(2)}) copy-start(f32[8,2]{0,1:T(2,128)} %param.7) | copy-start | bytes 196

commit v2 on v1

v2 whole, which is shorter than its diff:
```python
import functools
import math

import jax
import jax.numpy as jnp
from jax import lax
from jax.experimental import pallas as pl
from jax.experimental.pallas import tpu as pltpu
from jax.sharding import PartitionSpec as P

BLK = 16
FLOOR = -1e9
MASKED = -1e30
TINY = 1e-30
LOG2E = math.log2(math.e)
VMEM_LIMIT = 48 * 1024 * 1024
SMEM_SPEC = pl.BlockSpec(memory_space=pltpu.SMEM)
VMEM_SPEC = pl.BlockSpec(memory_space=pltpu.VMEM)


def sign_pair(width):
    half = width // 2
    row = lax.broadcasted_iota(jnp.int32, (width, width), 0)
    col = lax.broadcasted_iota(jnp.int32, (width, width), 1)
    parity = row & col & (half - 1)
    parity = parity ^ (parity >> 4)
    parity = parity ^ (parity >> 2)
    parity = (parity ^ (parity >> 1)) & 1
    same = (row >= half) == (col >= half)
    return jnp.where(same, (1 - 2 * parity).astype(jnp.float32), 0.0).astype(jnp.bfloat16)


def codes_of(rows_ref, scale_of, signs, rot_scr):
    tokens, heads, width = rows_ref.shape
    half = width // 2
    flat = rows_ref[...].reshape(tokens * heads, width)
    rotated = jnp.dot(flat, signs, preferred_element_type=jnp.float32)
    rotated = rotated * (1.0 / math.sqrt(half))
    for w in range(2):
        rot_scr[w] = rotated[:, w * half : (w + 1) * half]
    found = []
    for j in range(heads):
        parts = []
        for w in range(2):
            own = rot_scr[w, pl.ds(j, tokens, stride=heads), :] if heads > 1 else rot_scr[w]
            parts.append(jnp.clip(own / scale_of(j, w), -448.0, 448.0).astype(jnp.bfloat16))
        found.append(parts)
    return found


def page_places(slots_ref, ctx_id, tokens):
    pages = slots_ref.shape[1]
    row = lax.broadcasted_iota(jnp.int32, (tokens, pages), 0)
    page = lax.broadcasted_iota(jnp.int32, (tokens, pages), 1)
    slot = ctx_id * (tokens // BLK) + (row >> 4)
    place = (page * BLK + (row & (BLK - 1))).astype(jnp.float32)
    hit = jnp.broadcast_to(slots_ref[...], (tokens, pages)) == slot
    return jnp.sum(jnp.where(hit, place, 0.0), axis=1, keepdims=True)


def picker(distance, offset, count):
    key = lax.broadcasted_iota(jnp.int32, distance.shape, 1)
    hit = (distance == offset.astype(jnp.float32)) & (key < count)
    return jnp.where(hit, 1.0, 0.0).astype(jnp.bfloat16)


def spans_of(count_refs, info_ref, steps, tokens):
    if info_ref is not None:
        return [(info_ref[0, 0], info_ref[0, 1])]
    me = lax.axis_index("ctx")
    known = [ref[0:1, :][0, 0] for ref in count_refs]
    known.append(tokens * 3 - known[0] - known[1] - known[2])
    spans = []
    for step in steps:
        ident = me ^ step
        offset = jnp.int32(0)
        for other in range(4):
            offset = offset + jnp.where((me ^ other) < ident, known[other], 0)
        spans.append((offset, known[step]))
    return spans


def ready_kernel(*refs):
    sources, refs = refs[:6], refs[6:]
    ints_out, floats_out, signs_out, place_out, codes_out, query_ref, rot_scr = refs[:7]
    start_ref, scale_ref, count_ref, slots_ref, rows_ref, sems = refs[7:]
    held = (start_ref, scale_ref, count_ref, slots_ref, rows_ref, query_ref)
    copies = [pltpu.make_async_copy(a, b, sems.at[i]) for i, (a, b) in enumerate(zip(sources, held))]
    for copy in copies:
        copy.start()
    tokens, heads, width = rows_ref.shape
    sets, rows, _ = query_ref.shape
    ctx_id = lax.axis_index("ctx")
    rep_id = lax.axis_index("rep")
    pair_head = lax.axis_index("head") * lax.axis_size("rep") * heads
    signs = sign_pair(width)
    signs_out[...] = signs
    ints_out[...] = jnp.zeros(ints_out.shape, jnp.int32)
    floats_out[...] = jnp.zeros(floats_out.shape, jnp.float32)
    for copy in copies[:5]:
        copy.wait()
    ints_out[0:1, :] = jnp.full((1, 128), count_ref[0], jnp.int32)
    for c in range(sets):
        ints_out[1 + c : 2 + c, :] = jnp.full((1, 128), start_ref[c] + ctx_id * rows, jnp.int32)
    for side, member in enumerate((rep_id, 1 - rep_id)):
        for j in range(heads):
            for w in range(2):
                scale = scale_ref[w, pair_head + member * heads + j]
                at = (side * heads + j) * 2 + w
                floats_out[at : at + 1, :] = jnp.full((1, 128), scale, jnp.float32)
    place = jnp.broadcast_to(page_places(slots_ref, ctx_id, tokens), (tokens, tokens))
    token = lax.broadcasted_iota(jnp.int32, (tokens, tokens), 1)
    place_out[...] = place - token.astype(jnp.float32)
    found = codes_of(rows_ref, scale_reader(floats_out, 0, heads), signs, rot_scr)
    codes_out[...] = jnp.concatenate([part for parts in found for part in parts], axis=1)
    copies[5].wait()


def scale_reader(floats_ref, side, heads):
    def scale_of(j, w):
        at = (side * heads + j) * 2 + w
        return floats_ref[at : at + 1, :]

    return scale_of


def make_ready(starts, scales, counts, slots, rows, query):
    tokens, heads, width = rows.shape
    half = width // 2
    return pl.pallas_call(
        ready_kernel,
        out_shape=[
            jax.ShapeDtypeStruct((8, 128), jnp.int32),
            jax.ShapeDtypeStruct((8, 128), jnp.float32),
            jax.ShapeDtypeStruct((width, width), jnp.bfloat16),
            jax.ShapeDtypeStruct((tokens, tokens), jnp.float32),
            jax.ShapeDtypeStruct((tokens, heads * width), jnp.bfloat16),
            jax.ShapeDtypeStruct(query.shape, query.dtype),
        ],
        in_specs=[pl.BlockSpec(memory_space=pltpu.HBM)] * 6,
        out_specs=[VMEM_SPEC] * 6,
        scratch_shapes=[
            pltpu.VMEM((2, tokens * heads, half), jnp.float32),
            pltpu.SMEM(starts.shape, jnp.int32),
            pltpu.SMEM(scales.shape, jnp.float32),
            pltpu.SMEM(counts.shape, jnp.int32),
            pltpu.VMEM(slots.shape, jnp.int32),
            pltpu.VMEM(rows.shape, rows.dtype),
            pltpu.SemaphoreType.DMA((6,)),
        ],
        compiler_params=pltpu.CompilerParams(vmem_limit_bytes=VMEM_LIMIT),
        cost_estimate=pl.CostEstimate(
            flops=tokens * heads * width * width * 2, bytes_accessed=2 << 20, transcendentals=0
        ),
    )(starts, scales, counts, slots, rows, query)


def attend_kernel(metas, steps, with_codes, has_state, last, with_pages, *refs):
    refs = list(refs)
    info_ref = refs.pop(0) if metas == 0 else None
    count_refs = [refs.pop(0) for _ in range(metas)]
    ints_ref, floats_ref, signs_ref, query_ref = [refs.pop(0) for _ in range(4)]
    codes_ref = refs.pop(0) if with_codes else None
    rows_refs = [refs.pop(0) for _ in range(len(steps) - with_codes)]
    state = [refs.pop(0) for _ in range(2)] if has_state else None
    place_ref = refs.pop(0) if with_pages else None
    out_ref = refs.pop(0)
    level_out = None if last else refs.pop(0)
    moved_out = refs.pop(0) if with_pages else None
    rot_scr = refs.pop(0)

    tokens, heads, width = rows_refs[0].shape
    half = width // 2
    sets, rows, query_width = query_ref.shape
    group = query_width // half // heads
    stack = group * rows
    shards = len(steps)
    spans = spans_of(count_refs, info_ref, steps, tokens)
    bases = [ints_ref[1 + c : 2 + c, :][0, 0] for c in range(sets)]
    scale_of = scale_reader(floats_ref, 0, heads)
    if last:
        outs, sems = refs

    def finish(c, j):
        here = pl.ds(j * group * half, group * half)
        return pltpu.make_async_copy(outs.at[c, :, here], out_ref.at[c, :, here], sems.at[c * heads + j])

    def compute():
        signs = signs_ref[...]
        per_shard = []
        if with_codes:
            per_shard.append(
                [
                    [codes_ref[:, (2 * j + w) * half : (2 * j + w + 1) * half] for w in range(2)]
                    for j in range(heads)
                ]
            )
        per_shard += [codes_of(r, scale_of, signs, rot_scr) for r in rows_refs]

        def joined(j, w):
            parts = [found[j][w] for found in per_shard]
            return jnp.concatenate(parts, axis=0) if shards > 1 else parts[0]

        keys = [joined(j, 0) for j in range(heads)]
        ones = jnp.ones((shards * tokens, half), jnp.bfloat16)
        values = [jnp.concatenate([joined(j, 1), ones], axis=1) for j in range(heads)]
        row = lax.broadcasted_iota(jnp.int32, (rows, tokens), 0)
        key = lax.broadcasted_iota(jnp.int32, (rows, tokens), 1)
        for c in range(sets):
            parts = []
            for offset, count in spans:
                counted = (key < count) & (key + (offset - bases[c]) <= row)
                parts.append(jnp.where(counted, 0.0, MASKED))
            bias = jnp.concatenate(parts, axis=1) if shards > 1 else parts[0]
            bias = jnp.concatenate([bias] * group, axis=0)
            for j in range(heads):
                factor = scale_of(j, 0) * LOG2E
                stacked = jnp.concatenate(
                    [
                        query_ref[c, :, (j * group + g) * half : (j * group + g + 1) * half]
                        for g in range(group)
                    ],
                    axis=0,
                )
                scores = lax.dot_general(
                    stacked, keys[j], (((1,), (1,)), ((), ())), preferred_element_type=jnp.float32
                )
                scores = scores + bias
                top = jnp.max(scores, axis=1, keepdims=True)
                top = jnp.broadcast_to(top, (stack, half))
                if has_state:
                    level = state[1][c, j]
                    top = jnp.maximum(top, level)
                else:
                    top = jnp.maximum(top, FLOOR)
                probs = []
                for i in range(0, scores.shape[1], half):
                    part = scores[:, i : min(i + half, scores.shape[1])]
                    size = part.shape[1]
                    part = jnp.exp2((part - top[:, :size]) * factor[:, :size])
                    probs.append(part.astype(jnp.bfloat16))
                weighted = jnp.dot(
                    jnp.concatenate(probs, axis=1), values[j], preferred_element_type=jnp.float32
                )
                acc = weighted[:, :half] * scale_of(j, 1)
                total = weighted[:, half:]
                if has_state:
                    alpha = jnp.exp2((level - top) * factor)
                    total = total + alpha
                else:
                    total = jnp.maximum(total, TINY)
                target = outs if last else out_ref
                for g in range(group):
                    one = slice(g * rows, (g + 1) * rows)
                    cols = slice((j * group + g) * half, (j * group + g + 1) * half)
                    part = acc[one]
                    if has_state:
                        part = part + state[0][c, :, cols].astype(jnp.float32) * alpha[one]
                    target[c, :, cols] = (part / total[one]).astype(jnp.bfloat16)
                if last:
                    finish(c, j).start()
                else:
                    level_out[c, j] = top + jnp.log2(total) / factor
        if last:
            for c in range(sets):
                for j in range(heads):
                    finish(c, j).wait()
        return per_shard

    if last:
        latest = bases[0]
        for base in bases[1:]:
            latest = jnp.maximum(latest, base)
        needed = spans[0][0] < latest + rows

        @pl.when(needed)
        def _():
            compute()

        @pl.when(jnp.logical_not(needed))
        def _():
            whole = pltpu.make_async_copy(state[0], out_ref, sems.at[0])
            whole.start()
            whole.wait()

    else:
        per_shard = compute()
    if with_pages:
        place = place_ref[...]
        total = None
        for (offset, count), found in zip(spans, per_shard):
            pick = picker(place, offset, count)
            own = jnp.concatenate([part for parts in found for part in parts], axis=1)
            part = jnp.dot(pick, own, preferred_element_type=jnp.float32)
            total = part if total is None else total + part
        moved_out[...] = total.astype(jnp.bfloat16)


def attend(counts, info, steps, ready, rows, codes=None, state=None, last=False):
    ints, floats, signs, place, _, query = ready
    tokens, heads, width = rows[0].shape
    half = width // 2
    sets, query_rows, query_width = query.shape
    group = query_width // half // heads
    args = list(counts) if info is None else [info]
    specs = [VMEM_SPEC] * len(counts) if info is None else [SMEM_SPEC]
    args += [ints, floats, signs, query]
    if codes is not None:
        args.append(codes)
    args += rows
    if state is not None:
        args += list(state)
    if not last:
        args.append(place)
    specs += [VMEM_SPEC] * (len(args) - len(specs))
    outs = [jax.ShapeDtypeStruct(query.shape, jnp.bfloat16)]
    out_specs = [pl.BlockSpec(memory_space=pl.ANY) if last else VMEM_SPEC]
    scratch = [pltpu.VMEM((2, tokens * heads, half), jnp.float32)]
    if last:
        scratch += [
            pltpu.VMEM(query.shape, jnp.bfloat16),
            pltpu.SemaphoreType.DMA((sets * heads,)),
        ]
    else:
        outs += [
            jax.ShapeDtypeStruct((sets, heads, group * query_rows, half), jnp.float32),
            jax.ShapeDtypeStruct((tokens, heads * width), jnp.bfloat16),
        ]
        out_specs += [VMEM_SPEC] * 2
    keys = tokens * len(steps)
    work = sets * heads * group * query_rows * keys
    return pl.pallas_call(
        functools.partial(
            attend_kernel,
            len(counts) if info is None else 0,
            steps,
            codes is not None,
            state is not None,
            last,
            not last,
        ),
        out_shape=outs,
        in_specs=specs,
        out_specs=out_specs,
        scratch_shapes=scratch,
        compiler_params=pltpu.CompilerParams(vmem_limit_bytes=VMEM_LIMIT),
        cost_estimate=pl.CostEstimate(
            flops=work * half * 8, bytes_accessed=4 << 20, transcendentals=work
        ),
    )(*args)


def cache_kernel(metas, steps, *refs):
    refs = list(refs)
    info_ref = refs.pop(0) if metas == 0 else None
    count_refs = [refs.pop(0) for _ in range(metas)]
    floats_ref, signs_ref, place_ref, own, other, own_rows, other_rows, out_ref, rot_scr = refs
    tokens, heads, width = own_rows.shape
    half = width // 2
    rep_id = lax.axis_index("rep")
    signs = signs_ref[...]
    ((offset, count),) = spans_of(count_refs, info_ref, steps, tokens)
    pick = picker(place_ref[...], offset, count)
    full = []
    for side, (moved, rows) in enumerate(((own, own_rows), (other, other_rows))):
        scale_of = scale_reader(floats_ref, side, heads)
        found = codes_of(rows, scale_of, signs, rot_scr)
        for j in range(heads):
            for w in range(2):
                here = slice((2 * j + w) * half, (2 * j + w + 1) * half)
                part = jnp.dot(pick, found[j][w], preferred_element_type=jnp.float32)
                full.append((part + moved[:, here].astype(jnp.float32)) * scale_of(j, w))

    for turn in range(2):

        @pl.when(rep_id == turn)
        def _(turn=turn):
            for side in range(2):
                first = (side if turn == 0 else 1 - side) * heads
                for j in range(heads):
                    for w in range(2):
                        value = full[(side * heads + j) * 2 + w]
                        out_ref[:, first + j, w * half : (w + 1) * half] = value


def fill_cache(counts, info, steps, ready, own, other, own_rows, other_rows):
    _, floats, signs, place, _, _ = ready
    tokens, heads, width = own_rows.shape
    args = list(counts) if info is None else [info]
    specs = [VMEM_SPEC] * len(counts) if info is None else [SMEM_SPEC]
    args += [floats, signs, place, own, other, own_rows, other_rows]
    specs += [VMEM_SPEC] * 7
    return pl.pallas_call(
        functools.partial(cache_kernel, len(counts) if info is None else 0, steps),
        out_shape=jax.ShapeDtypeStruct((tokens, 2 * heads, width), jnp.float32),
        in_specs=specs,
        out_specs=VMEM_SPEC,
        scratch_shapes=[pltpu.VMEM((2, tokens * heads, width // 2), jnp.float32)],
        compiler_params=pltpu.CompilerParams(vmem_limit_bytes=VMEM_LIMIT),
        cost_estimate=pl.CostEstimate(
            flops=tokens * tokens * heads * width * 8, bytes_accessed=2 << 20, transcendentals=0
        ),
    )(*args)


def pair(value, axis, step):
    size = lax.axis_size(axis)
    return lax.ppermute(value, axis, [(i, i ^ step) for i in range(size)])


def body(kv_rows, kv_scales, queries, shard_counts, span_starts, block_slots):
    across = pair(kv_rows, "ctx", 2)
    beside = pair(kv_rows, "ctx", 1)
    ready = make_ready(
        span_starts, kv_scales.T, shard_counts, block_slots[None, :], kv_rows, queries
    )
    count = jnp.broadcast_to(shard_counts[:, None], (8, 128))
    counts = [count, pair(count, "ctx", 1), pair(count, "ctx", 2)]
    corner = pair(across, "ctx", 1)
    *state, moved = attend(counts, None, (0, 1, 2), ready, [beside, across], ready[4])
    moved_other = pair(moved, "rep", 1)
    corner_other = pair(corner, "rep", 1)
    (attention,) = attend(counts, None, (3,), ready, [corner], None, state, True)
    decode_cache = fill_cache(
        counts, None, (3,), ready, moved, moved_other, corner, corner_other
    )
    return attention, decode_cache


def body_any(kv_rows, kv_scales, queries, shard_counts, span_starts, block_slots):
    counts = lax.all_gather(shard_counts, "ctx", axis=0, tiled=True)
    info = jnp.stack([jnp.cumsum(counts) - counts, counts], axis=1)
    every = lax.all_gather(kv_rows, "ctx", axis=0)
    ready = make_ready(
        span_starts, kv_scales.T, shard_counts, block_slots[None, :], kv_rows, queries
    )

    def step(carry, turn):
        state, moved = carry
        rows, one = turn
        *state, found = attend([], one[None], (0,), ready, [rows], None, state)
        return (tuple(state), moved + found), None

    *state, moved = attend([], info[:1], (0,), ready, [every[0]])
    (state, moved), _ = lax.scan(step, (tuple(state), moved), (every[1:], info[1:]))
    none = jnp.zeros((1, 2), jnp.int32)
    decode_cache = fill_cache(
        [], none, (0,), ready, moved, pair(moved, "rep", 1), kv_rows, kv_rows
    )
    return state[0], decode_cache


def solution(mesh):
    in_specs = (
        P(("groups", "ctx"), ("head", "rep"), None),
        P(),
        P(None, ("groups", "ctx"), ("head", "rep")),
        P(("groups", "ctx")),
        P("groups"),
        P("groups"),
    )
    out_specs = (P(None, ("groups", "ctx"), ("head", "rep")), P(("groups", "ctx"), "head", None))
    chosen = body if mesh.shape["ctx"] == 4 else body_any
    return jax.shard_map(chosen, mesh=mesh, in_specs=in_specs, out_specs=out_specs, check_vma=False)
```

time: 38.8 us -> 25.8 us (0.66)
  the two profiles are of different devices: /device:TPU:0 before, /device:TPU:31 now
where the time goes in v2:
time: 25.8 us; the launch traced here: 25.5 us
  Pallas kernels  10.6 us (41%)
  starting transfers between devices  5.92 us (23%)
  local copies, waits for them, and re-layouts  4.14 us (16%)
  waiting for transfers between devices  3.52 us (14%)
  between operations  1.34 us (5%)
    pallas_call x2, Pallas kernels, attend(): pl.pallas_call(functools.partial(attend_kernel, len(counts) if info is No...  7.42 us
    ppermute x7, starting transfers between devices, pair(): return lax.ppermute(value, axis, [(i, i ^ step) for i in range(size)])  5.92 us
    unnamed x10, local copies, waits for them, and re-layouts  4.14 us
    ppermute x7, waiting for transfers between devices, pair(): return lax.ppermute(value, axis, [(i, i ^ step) for i in range(size)])  3.52 us
    pallas_call x1, Pallas kernels, fill_cache(): pl.pallas_call(functools.partial(cache_kernel, len(counts) if info is Non...  2.32 us
    pallas_call x1, Pallas kernels, make_ready(): pl.pallas_call(ready_kernel, out_shape=[jax.ShapeDtypeStruct((8, 128), jn...  0.87 us
  transfers between devices with their start and end apart: 7, of which 3 were waited for; matrix products, arithmetic and copies ran while one was open for 0% of the time, Pallas kernels for 32%

profile of v2, /device:TPU:31, one launch (start us, length us, event | category | flops | bytes accessed | tf_op | source)
XLA Modules:
  0.0 25.5 jit_solution(7547546418881295594)
XLA Ops:
  0.6 0.1 collective-permute-start.2
  0.8 0.2 collective-permute-start.4
  1.6 1.4 %collective-permute-start = (s32[8,128]{1,0:T(8,128)S(1)}, s32[8,128]{1,0:T(8,128)S(1)}, u32[]{:S(2)}, u32[]{:S(2)}) collective-permute-start(s32[8,128]{1,0:T(8,128)S(1)} %broadcast_in_dim.12.refs_0_), channel_id=1, source_target_pairs={{0,4},{4,0},{8,12},{12,8},{1,5},{5,1},{9,13},{13,9},{2,6},{6,2},{1... | collective-permute-start | bytes 12296 | tf_op jit(solution)/shard_map/ppermute | solution.py:408
  3.0 2.3 %collective-permute-start.1 = (s32[8,128]{1,0:T(8,128)S(1)}, s32[8,128]{1,0:T(8,128)S(1)}, u32[]{:S(2)}, u32[]{:S(2)}) collective-permute-start(s32[8,128]{1,0:T(8,128)S(1)} %broadcast_in_dim.12.refs_0_), channel_id=1, source_target_pairs={{0,8},{4,12},{8,0},{12,4},{1,9},{5,13},{9,1},{13,5},{2,10},{6,14},... | collective-permute-start | bytes 12296 | tf_op jit(solution)/shard_map/ppermute | solution.py:408
  5.3 0.0 copy-start
  5.3 1.2 %copy-done = bf16[2,64,4096]{2,1,0:T(8,128)(2,1)S(1)} copy-done((bf16[2,64,4096]{2,1,0:T(8,128)(2,1)S(1)}, bf16[2,64,4096]{2,1,0:T(8,128)(2,1)}, u32[]{:S(2)}) %copy-start) | copy-done | bytes 1048600
  6.5 0.0 copy-start.1
  6.5 0.9 %copy-done.1 = bf16[192,2,256]{2,1,0:T(2,128)(2,1)S(1)} copy-done((bf16[192,2,256]{2,1,0:T(2,128)(2,1)S(1)}, bf16[192,2,256]{2,1,0:T(2,128)(2,1)}, u32[]{:S(2)}) %copy-start.1) | copy-done | bytes 196632
  7.4 0.0 copy-start.2
  7.4 0.7 %copy-done.2 = f32[8,2]{0,1:T(2,128)S(1)} copy-done((f32[8,2]{0,1:T(2,128)S(1)}, f32[8,2]{0,1:T(2,128)}, u32[]{:S(2)}) %copy-start.2) | copy-done | bytes 88
  8.1 0.0 copy-start.3
  8.1 0.7 %copy-done.3 = s32[2]{0:T(128)S(1)} copy-done((s32[2]{0:T(128)S(1)}, s32[2]{0:T(128)}, u32[]{:S(2)}) %copy-start.3) | copy-done | bytes 32
  8.7 0.0 copy-start.4
  8.7 0.7 %copy-done.4 = s32[48]{0:T(128)S(1)} copy-done((s32[48]{0:T(128)S(1)}, s32[48]{0:T(128)}, u32[]{:S(2)}) %copy-start.4) | copy-done | bytes 216
  9.4 0.9 %shard_map.77 = (s32[8,128]{1,0:T(8,128)S(1)}, f32[8,128]{1,0:T(8,128)S(1)}, bf16[256,256]{1,0:T(8,128)(2,1)S(1)}, f32[192,192]{1,0:T(8,128)S(1)}, bf16[192,512]...) custom-call(s32[2]{0:T(128)S(1)} %copy-done.3, f32[2,8]{1,0:T(2,128)S(1)} %bitcast.4, s32[1]{0:T(128)} %copy.8.refs_2_, ...), custom_call_target="tpu_custom_call" | custom-call | flops 50331648 | bytes 2097152 | tf_op jit(solution)/shard_map/pallas_call | solution.py:130
  10.3 2.5 %collective-permute-done.2.refs_9_ = bf16[192,2,256]{2,1,0:T(2,128)(2,1)S(1)} collective-permute-done((bf16[192,2,256]{2,1,0:T(2,128)(2,1)}, bf16[192,2,256]{2,1,0:T(2,128)(2,1)S(1)}, u32[]{:S(2)}, u32[]{:S(2)}) %collective-permute-start.2) | collective-permute-done | bytes 196640 | tf_op jit(solution)/shard_map/ppermute | solution.py:408
  12.8 0.0 collective-permute-start.3
  12.8 0.0 collective-permute-done.refs_1_
  12.8 0.1 collective-permute-done.1.refs_2_
  12.9 0.0 collective-permute-done.4.refs_8_
  12.9 4.3 %shard_map.78 = (bf16[2,64,4096]{2,1,0:T(8,128)(2,1)S(1)}, f32[2,2,1024,128]{3,2,1,0:T(8,128)S(1)}, bf16[192,512]{1,0:T(8,128)(2,1)S(1)}) custom-call(s32[8,128]{1,0:T(8,128)S(1)} %broadcast_in_dim.12.refs_0_, s32[8,128]{1,0:T(8,128)S(1)} %collective-permute-done.refs_1_, s32[8,128]{1,0:T(8,128)S(1)} %collective-permute-done.1.refs_2_, ...), custom_call_target="tpu_custom_call" | custom-call | flops 2415919104 | bytes 4194304 | tf_op jit(solution)/shard_map/pallas_call | solution.py:332
  17.2 0.6 %collective-permute-start.5 = (bf16[192,512]{1,0:T(8,128)(2,1)S(1)}, bf16[192,512]{1,0:T(8,128)(2,1)S(1)}, u32[]{:S(2)}, u32[]{:S(2)}) collective-permute-start(bf16[192,512]{1,0:T(8,128)(2,1)S(1)} %get-tuple-element.19.refs_6_), channel_id=1, source_target_pairs={{0,1},{1,0},{2,3},{3,2},{4,5},{5,4},{6,7},{7,6},{8,9},{9,8},{10,11... | collective-permute-start | bytes 589832 | tf_op jit(solution)/shard_map/ppermute | solution.py:408
  17.8 0.9 %collective-permute-done.3.refs_7_.refs_8_ = bf16[192,2,256]{2,1,0:T(2,128)(2,1)S(1)} collective-permute-done((bf16[192,2,256]{2,1,0:T(2,128)(2,1)S(1)}, bf16[192,2,256]{2,1,0:T(2,128)(2,1)S(1)}, u32[]{:S(2)}, u32[]{:S(2)}) %collective-permute-start.3) | collective-permute-done | bytes 196640 | tf_op jit(solution)/shard_map/ppermute | solution.py:408
  18.7 1.4 %collective-permute-start.6 = (bf16[192,2,256]{2,1,0:T(2,128)(2,1)S(1)}, bf16[192,2,256]{2,1,0:T(2,128)(2,1)S(1)}, u32[]{:S(2)}, u32[]{:S(2)}) collective-permute-start(bf16[192,2,256]{2,1,0:T(2,128)(2,1)S(1)} %collective-permute-done.3.refs_7_.refs_8_), channel_id=1, source_target_pairs={{0,1},{1,0},{2,3},{3,2},{4,5},{5,4},{6,7},{7,6},{8,9},{9,8},{10,11... | collective-permute-start | bytes 589832 | tf_op jit(solution)/shard_map/ppermute | solution.py:408
  20.1 3.1 %shard_map.79 = bf16[2,64,4096]{2,1,0:T(8,128)(2,1)} custom-call(s32[8,128]{1,0:T(8,128)S(1)} %broadcast_in_dim.12.refs_0_, s32[8,128]{1,0:T(8,128)S(1)} %collective-permute-done.refs_1_, s32[8,128]{1,0:T(8,128)S(1)} %collective-permute-done.1.refs_2_, s32[8,128]{1,0:T(8,128)S(1)} %get-tuple-element.11.refs_3_, ...), custom_call_target="tpu_custom_call" | custom-call | flops 805306368 | bytes 4194304 | tf_op jit(solution)/shard_map/pallas_call | solution.py:332
  23.2 0.0 collective-permute-done.5.refs_7_
  23.2 0.0 collective-permute-done.6.refs_9_
  23.2 2.3 %shard_map.80 = f32[192,4,256]{2,1,0:T(4,128)} custom-call(s32[8,128]{1,0:T(8,128)S(1)} %broadcast_in_dim.12.refs_0_, s32[8,128]{1,0:T(8,128)S(1)} %collective-permute-done.refs_1_, s32[8,128]{1,0:T(8,128)S(1)} %collective-permute-done.1.refs_2_, f32[8,128]{1,0:T(8,128)S(1)} %get-tuple-element.12.refs_4_.refs_3_, ...), custom_call_target="tpu_custom_call" | custom-call | flops 150994944 | bytes 2097152 | tf_op jit(solution)/shard_map/pallas_call | solution.py:393
  (1 shorter events, 0.0 us)
Async XLA Ops:
  0.6 12.1 %collective-permute-start.2 = (bf16[192,2,256]{2,1,0:T(2,128)(2,1)}, bf16[192,2,256]{2,1,0:T(2,128)(2,1)S(1)}, u32[]{:S(2)}, u32[]{:S(2)}) collective-permute-start(bf16[192,2,256]{2,1,0:T(2,128)(2,1)} %refs_4_.1), channel_id=1, source_target_pairs={{0,8},{4,12},{8,0},{12,4},{1,9},{5,13},{9,1},{13,5},{2,10},{6,14},... | collective-permute-start | bytes 589832 | tf_op jit(solution)/shard_map/ppermute | solution.py:408
  0.8 12.1 %collective-permute-start.4 = (bf16[192,2,256]{2,1,0:T(2,128)(2,1)}, bf16[192,2,256]{2,1,0:T(2,128)(2,1)S(1)}, u32[]{:S(2)}, u32[]{:S(2)}) collective-permute-start(bf16[192,2,256]{2,1,0:T(2,128)(2,1)} %refs_4_.1), channel_id=1, source_target_pairs={{0,4},{4,0},{8,12},{12,8},{1,5},{5,1},{9,13},{13,9},{2,6},{6,2},{1... | collective-permute-start | bytes 589832 | tf_op jit(solution)/shard_map/ppermute | solution.py:408
  1.6 11.2 %collective-permute-start = (s32[8,128]{1,0:T(8,128)S(1)}, s32[8,128]{1,0:T(8,128)S(1)}, u32[]{:S(2)}, u32[]{:S(2)}) collective-permute-start(s32[8,128]{1,0:T(8,128)S(1)} %broadcast_in_dim.12.refs_0_), channel_id=1, source_target_pairs={{0,4},{4,0},{8,12},{12,8},{1,5},{5,1},{9,13},{13,9},{2,6},{6,2},{1... | collective-permute-start | bytes 12296 | tf_op jit(solution)/shard_map/ppermute | solution.py:408
  3.0 9.9 %collective-permute-start.1 = (s32[8,128]{1,0:T(8,128)S(1)}, s32[8,128]{1,0:T(8,128)S(1)}, u32[]{:S(2)}, u32[]{:S(2)}) collective-permute-start(s32[8,128]{1,0:T(8,128)S(1)} %broadcast_in_dim.12.refs_0_), channel_id=1, source_target_pairs={{0,8},{4,12},{8,0},{12,4},{1,9},{5,13},{9,1},{13,5},{2,10},{6,14},... | collective-permute-start | bytes 12296 | tf_op jit(solution)/shard_map/ppermute | solution.py:408
  5.3 1.2 %copy-start = (bf16[2,64,4096]{2,1,0:T(8,128)(2,1)S(1)}, bf16[2,64,4096]{2,1,0:T(8,128)(2,1)}, u32[]{:S(2)}) copy-start(bf16[2,64,4096]{2,1,0:T(8,128)(2,1)} %refs_5_.1) | copy-start | bytes 3145732
  6.5 0.9 %copy-start.1 = (bf16[192,2,256]{2,1,0:T(2,128)(2,1)S(1)}, bf16[192,2,256]{2,1,0:T(2,128)(2,1)}, u32[]{:S(2)}) copy-start(bf16[192,2,256]{2,1,0:T(2,128)(2,1)} %refs_4_.1) | copy-start | bytes 589828
  7.4 0.7 %copy-start.2 = (f32[8,2]{0,1:T(2,128)S(1)}, f32[8,2]{0,1:T(2,128)}, u32[]{:S(2)}) copy-start(f32[8,2]{0,1:T(2,128)} %param.7) | copy-start | bytes 196
  8.1 0.7 %copy-start.3 = (s32[2]{0:T(128)S(1)}, s32[2]{0:T(128)}, u32[]{:S(2)}) copy-start(s32[2]{0:T(128)} %refs_0_.1) | copy-start | bytes 28
  8.7 0.7 %copy-start.4 = (s32[48]{0:T(128)S(1)}, s32[48]{0:T(128)}, u32[]{:S(2)}) copy-start(s32[48]{0:T(128)} %param.11) | copy-start | bytes 580
  12.8 5.9 %collective-permute-start.3 = (bf16[192,2,256]{2,1,0:T(2,128)(2,1)S(1)}, bf16[192,2,256]{2,1,0:T(2,128)(2,1)S(1)}, u32[]{:S(2)}, u32[]{:S(2)}) collective-permute-start(bf16[192,2,256]{2,1,0:T(2,128)(2,1)S(1)} %collective-permute-done.2.refs_9_), channel_id=1, source_target_pairs={{0,4},{4,0},{8,12},{12,8},{1,5},{5,1},{9,13},{13,9},{2,6},{6,2},{1... | collective-permute-start | bytes 589832 | tf_op jit(solution)/shard_map/ppermute | solution.py:408
  17.2 6.0 %collective-permute-start.5 = (bf16[192,512]{1,0:T(8,128)(2,1)S(1)}, bf16[192,512]{1,0:T(8,128)(2,1)S(1)}, u32[]{:S(2)}, u32[]{:S(2)}) collective-permute-start(bf16[192,512]{1,0:T(8,128)(2,1)S(1)} %get-tuple-element.19.refs_6_), channel_id=1, source_target_pairs={{0,1},{1,0},{2,3},{3,2},{4,5},{5,4},{6,7},{7,6},{8,9},{9,8},{10,11... | collective-permute-start | bytes 589832 | tf_op jit(solution)/shard_map/ppermute | solution.py:408
  18.7 4.5 %collective-permute-start.6 = (bf16[192,2,256]{2,1,0:T(2,128)(2,1)S(1)}, bf16[192,2,256]{2,1,0:T(2,128)(2,1)S(1)}, u32[]{:S(2)}, u32[]{:S(2)}) collective-permute-start(bf16[192,2,256]{2,1,0:T(2,128)(2,1)S(1)} %collective-permute-done.3.refs_7_.refs_8_), channel_id=1, source_target_pairs={{0,1},{1,0},{2,3},{3,2},{4,5},{5,4},{6,7},{7,6},{8,9},{9,8},{10,11... | collective-permute-start | bytes 589832 | tf_op jit(solution)/shard_map/ppermute | solution.py:408

commit v3 on v2

--- a/solution.py
+++ b/solution.py
@@ -12,6 +12,7 @@
 FLOOR = -1e9
 MASKED = -1e30
 TINY = 1e-30
+PIECES = 4
 LOG2E = math.log2(math.e)
 VMEM_LIMIT = 48 * 1024 * 1024
 SMEM_SPEC = pl.BlockSpec(memory_space=pltpu.SMEM)
@@ -178,12 +179,6 @@
     spans = spans_of(count_refs, info_ref, steps, tokens)
     bases = [ints_ref[1 + c : 2 + c, :][0, 0] for c in range(sets)]
     scale_of = scale_reader(floats_ref, 0, heads)
-    if last:
-        outs, sems = refs
-
-    def finish(c, j):
-        here = pl.ds(j * group * half, group * half)
-        return pltpu.make_async_copy(outs.at[c, :, here], out_ref.at[c, :, here], sems.at[c * heads + j])
 
     def compute():
         signs = signs_ref[...]
@@ -249,22 +244,15 @@
                     total = total + alpha
                 else:
                     total = jnp.maximum(total, TINY)
-                target = outs if last else out_ref
                 for g in range(group):
                     one = slice(g * rows, (g + 1) * rows)
                     cols = slice((j * group + g) * half, (j * group + g + 1) * half)
                     part = acc[one]
                     if has_state:
                         part = part + state[0][c, :, cols].astype(jnp.float32) * alpha[one]
-                    target[c, :, cols] = (part / total[one]).astype(jnp.bfloat16)
-                if last:
-                    finish(c, j).start()
-                else:
+                    out_ref[c, :, cols] = (part / total[one]).astype(jnp.bfloat16)
+                if not last:
                     level_out[c, j] = top + jnp.log2(total) / factor
-        if last:
-            for c in range(sets):
-                for j in range(heads):
-                    finish(c, j).wait()
         return per_shard
 
     if last:
@@ -279,9 +267,7 @@
 
         @pl.when(jnp.logical_not(needed))
         def _():
-            whole = pltpu.make_async_copy(state[0], out_ref, sems.at[0])
-            whole.start()
-            whole.wait()
+            out_ref[...] = state[0][...]
 
     else:
         per_shard = compute()
@@ -314,14 +300,9 @@
         args.append(place)
     specs += [VMEM_SPEC] * (len(args) - len(specs))
     outs = [jax.ShapeDtypeStruct(query.shape, jnp.bfloat16)]
-    out_specs = [pl.BlockSpec(memory_space=pl.ANY) if last else VMEM_SPEC]
+    out_specs = [VMEM_SPEC]
     scratch = [pltpu.VMEM((2, tokens * heads, half), jnp.float32)]
-    if last:
-        scratch += [
-            pltpu.VMEM(query.shape, jnp.bfloat16),
-            pltpu.SemaphoreType.DMA((sets * heads,)),
-        ]
-    else:
+    if not last:
         outs += [
             jax.ShapeDtypeStruct((sets, heads, group * query_rows, half), jnp.float32),
             jax.ShapeDtypeStruct((tokens, heads * width), jnp.bfloat16),
@@ -350,52 +331,81 @@
     )(*args)
 
 
-def cache_kernel(metas, steps, *refs):
+def finish_kernel(metas, steps, *refs):
     refs = list(refs)
     info_ref = refs.pop(0) if metas == 0 else None
     count_refs = [refs.pop(0) for _ in range(metas)]
-    floats_ref, signs_ref, place_ref, own, other, own_rows, other_rows, out_ref, rot_scr = refs
+    floats_ref, signs_ref, place_ref, result_ref, own, other, own_rows, other_rows = refs[:8]
+    attention_out, cache_out, rot_scr, cache_scr, sems = refs[8:]
     tokens, heads, width = own_rows.shape
     half = width // 2
+    sets = result_ref.shape[0]
     rep_id = lax.axis_index("rep")
+    sent = [
+        pltpu.make_async_copy(result_ref.at[c], attention_out.at[c], sems.at[c]) for c in range(sets)
+    ]
+    for copy in sent:
+        copy.start()
     signs = signs_ref[...]
     ((offset, count),) = spans_of(count_refs, info_ref, steps, tokens)
     pick = picker(place_ref[...], offset, count)
-    full = []
+    sides = []
     for side, (moved, rows) in enumerate(((own, own_rows), (other, other_rows))):
         scale_of = scale_reader(floats_ref, side, heads)
-        found = codes_of(rows, scale_of, signs, rot_scr)
-        for j in range(heads):
-            for w in range(2):
-                here = slice((2 * j + w) * half, (2 * j + w + 1) * half)
-                part = jnp.dot(pick, found[j][w], preferred_element_type=jnp.float32)
-                full.append((part + moved[:, here].astype(jnp.float32)) * scale_of(j, w))
+        sides.append((moved, scale_of, codes_of(rows, scale_of, signs, rot_scr)))
+    size = tokens // PIECES
+    pieces = [
+        pltpu.make_async_copy(
+            cache_scr.at[pl.ds(i * size, size)],
+            cache_out.at[pl.ds(i * size, size)],
+            sems.at[sets + i],
+        )
+        for i in range(PIECES)
+    ]
 
     for turn in range(2):
 
         @pl.when(rep_id == turn)
         def _(turn=turn):
-            for side in range(2):
-                first = (side if turn == 0 else 1 - side) * heads
-                for j in range(heads):
-                    for w in range(2):
-                        value = full[(side * heads + j) * 2 + w]
-                        out_ref[:, first + j, w * half : (w + 1) * half] = value
-
-
-def fill_cache(counts, info, steps, ready, own, other, own_rows, other_rows):
+            for i, piece in enumerate(pieces):
+                here = slice(i * size, (i + 1) * size)
+                for side, (moved, scale_of, found) in enumerate(sides):
+                    first = (side if turn == 0 else 1 - side) * heads
+                    for j in range(heads):
+                        for w in range(2):
+                            cols = slice((2 * j + w) * half, (2 * j + w + 1) * half)
+                            part = jnp.dot(
+                                pick[here], found[j][w], preferred_element_type=jnp.float32
+                            )
+                            part = (part + moved[here, cols].astype(jnp.float32)) * scale_of(j, w)
+                            cache_scr[here, first + j, w * half : (w + 1) * half] = part
+                piece.start()
+
+    for copy in sent + pieces:
+        copy.wait()
+
+
+def finish(counts, info, steps, ready, result, own, other, own_rows, other_rows):
     _, floats, signs, place, _, _ = ready
     tokens, heads, width = own_rows.shape
+    cache = (tokens, 2 * heads, width)
     args = list(counts) if info is None else [info]
     specs = [VMEM_SPEC] * len(counts) if info is None else [SMEM_SPEC]
-    args += [floats, signs, place, own, other, own_rows, other_rows]
-    specs += [VMEM_SPEC] * 7
+    args += [floats, signs, place, result, own, other, own_rows, other_rows]
+    specs += [VMEM_SPEC] * 8
     return pl.pallas_call(
-        functools.partial(cache_kernel, len(counts) if info is None else 0, steps),
-        out_shape=jax.ShapeDtypeStruct((tokens, 2 * heads, width), jnp.float32),
+        functools.partial(finish_kernel, len(counts) if info is None else 0, steps),
+        out_shape=[
+            jax.ShapeDtypeStruct(result.shape, result.dtype),
+            jax.ShapeDtypeStruct(cache, jnp.float32),
+        ],
         in_specs=specs,
-        out_specs=VMEM_SPEC,
-        scratch_shapes=[pltpu.VMEM((2, tokens * heads, width // 2), jnp.float32)],
+        out_specs=[pl.BlockSpec(memory_space=pl.ANY)] * 2,
+        scratch_shapes=[
+            pltpu.VMEM((2, tokens * heads, width // 2), jnp.float32),
+            pltpu.VMEM(cache, jnp.float32),
+            pltpu.SemaphoreType.DMA((result.shape[0] + PIECES,)),
+        ],
         compiler_params=pltpu.CompilerParams(vmem_limit_bytes=VMEM_LIMIT),
         cost_estimate=pl.CostEstimate(
             flops=tokens * tokens * heads * width * 8, bytes_accessed=2 << 20, transcendentals=0
@@ -420,11 +430,8 @@
     *state, moved = attend(counts, None, (0, 1, 2), ready, [beside, across], ready[4])
     moved_other = pair(moved, "rep", 1)
     corner_other = pair(corner, "rep", 1)
-    (attention,) = attend(counts, None, (3,), ready, [corner], None, state, True)
-    decode_cache = fill_cache(
-        counts, None, (3,), ready, moved, moved_other, corner, corner_other
-    )
-    return attention, decode_cache
+    (result,) = attend(counts, None, (3,), ready, [corner], None, state, True)
+    return finish(counts, None, (3,), ready, result, moved, moved_other, corner, corner_other)
 
 
 def body_any(kv_rows, kv_scales, queries, shard_counts, span_starts, block_slots):
@@ -444,10 +451,8 @@
     *state, moved = attend([], info[:1], (0,), ready, [every[0]])
     (state, moved), _ = lax.scan(step, (tuple(state), moved), (every[1:], info[1:]))
     none = jnp.zeros((1, 2), jnp.int32)
-    decode_cache = fill_cache(
-        [], none, (0,), ready, moved, pair(moved, "rep", 1), kv_rows, kv_rows
-    )
-    return state[0], decode_cache
+    other = pair(moved, "rep", 1)
+    return finish([], none, (0,), ready, state[0], moved, other, kv_rows, kv_rows)
 
 
 def solution(mesh):

time: 25.8 us -> 24.5 us (0.950)
  Pallas kernels: 10.6 us -> 9.38 us
    pallas_call x2, Pallas kernels: 7.42 us -> 6.69 us  [attend(): pl.pallas_call(functools.partial(attend_kernel, len(counts) if info is No...]
    pallas_call x1, Pallas kernels: 2.32 us -> 1.81 us  [finish(): pl.pallas_call(functools.partial(finish_kernel, len(counts) if info is No...]
  transfers between devices with their start and end apart: 7 -> 7, of which waited for: 3 -> 3; matrix products, arithmetic and copies ran while one was open for 0% -> 0% of each run, Pallas kernels for 32% -> 31%
where the time goes in v3:
time: 24.5 us; the launch traced here: 24.3 us
  Pallas kernels  9.38 us (38%)
  starting transfers between devices  5.91 us (24%)
  local copies, waits for them, and re-layouts  4.14 us (17%)
  waiting for transfers between devices  3.5 us (14%)
  between operations  1.34 us (5%)
    pallas_call x2, Pallas kernels, attend(): pl.pallas_call(functools.partial(attend_kernel, len(counts) if info is No...  6.69 us
    ppermute x7, starting transfers between devices, pair(): return lax.ppermute(value, axis, [(i, i ^ step) for i in range(size)])  5.91 us
    unnamed x10, local copies, waits for them, and re-layouts  4.14 us
    ppermute x7, waiting for transfers between devices, pair(): return lax.ppermute(value, axis, [(i, i ^ step) for i in range(size)])  3.5 us
    pallas_call x1, Pallas kernels, finish(): pl.pallas_call(functools.partial(finish_kernel, len(counts) if info is No...  1.81 us
    pallas_call x1, Pallas kernels, make_ready(): pl.pallas_call(ready_kernel, out_shape=[jax.ShapeDtypeStruct((8, 128), jn...  0.87 us
  transfers between devices with their start and end apart: 7, of which 3 were waited for; matrix products, arithmetic and copies ran while one was open for 0% of the time, Pallas kernels for 31%

profile of v3, /device:TPU:31, one launch (start us, length us, event | category | flops | bytes accessed | tf_op | source)
XLA Modules:
  0.0 24.3 jit_solution(7400560391215743559)
XLA Ops:
  0.6 0.1 collective-permute-start.2
  0.8 0.2 collective-permute-start.4
  1.6 1.4 %collective-permute-start = (s32[8,128]{1,0:T(8,128)S(1)}, s32[8,128]{1,0:T(8,128)S(1)}, u32[]{:S(2)}, u32[]{:S(2)}) collective-permute-start(s32[8,128]{1,0:T(8,128)S(1)} %broadcast_in_dim.12.refs_0_), channel_id=1, source_target_pairs={{0,4},{4,0},{8,12},{12,8},{1,5},{5,1},{9,13},{13,9},{2,6},{6,2},{1... | collective-permute-start | bytes 12296 | tf_op jit(solution)/shard_map/ppermute | solution.py:418
  3.0 2.3 %collective-permute-start.1 = (s32[8,128]{1,0:T(8,128)S(1)}, s32[8,128]{1,0:T(8,128)S(1)}, u32[]{:S(2)}, u32[]{:S(2)}) collective-permute-start(s32[8,128]{1,0:T(8,128)S(1)} %broadcast_in_dim.12.refs_0_), channel_id=1, source_target_pairs={{0,8},{4,12},{8,0},{12,4},{1,9},{5,13},{9,1},{13,5},{2,10},{6,14},... | collective-permute-start | bytes 12296 | tf_op jit(solution)/shard_map/ppermute | solution.py:418
  5.3 0.0 copy-start
  5.3 1.2 %copy-done = bf16[2,64,4096]{2,1,0:T(8,128)(2,1)S(1)} copy-done((bf16[2,64,4096]{2,1,0:T(8,128)(2,1)S(1)}, bf16[2,64,4096]{2,1,0:T(8,128)(2,1)}, u32[]{:S(2)}) %copy-start) | copy-done | bytes 1048600
  6.5 0.0 copy-start.1
  6.5 0.9 %copy-done.1 = bf16[192,2,256]{2,1,0:T(2,128)(2,1)S(1)} copy-done((bf16[192,2,256]{2,1,0:T(2,128)(2,1)S(1)}, bf16[192,2,256]{2,1,0:T(2,128)(2,1)}, u32[]{:S(2)}) %copy-start.1) | copy-done | bytes 196632
  7.4 0.0 copy-start.2
  7.4 0.7 %copy-done.2 = f32[8,2]{0,1:T(2,128)S(1)} copy-done((f32[8,2]{0,1:T(2,128)S(1)}, f32[8,2]{0,1:T(2,128)}, u32[]{:S(2)}) %copy-start.2) | copy-done | bytes 88
  8.1 0.0 copy-start.3
  8.1 0.7 %copy-done.3 = s32[2]{0:T(128)S(1)} copy-done((s32[2]{0:T(128)S(1)}, s32[2]{0:T(128)}, u32[]{:S(2)}) %copy-start.3) | copy-done | bytes 32
  8.7 0.0 copy-start.4
  8.7 0.7 %copy-done.4 = s32[48]{0:T(128)S(1)} copy-done((s32[48]{0:T(128)S(1)}, s32[48]{0:T(128)}, u32[]{:S(2)}) %copy-start.4) | copy-done | bytes 216
  9.4 0.9 %shard_map.77 = (s32[8,128]{1,0:T(8,128)S(1)}, f32[8,128]{1,0:T(8,128)S(1)}, bf16[256,256]{1,0:T(8,128)(2,1)S(1)}, f32[192,192]{1,0:T(8,128)S(1)}, bf16[192,512]...) custom-call(s32[2]{0:T(128)S(1)} %copy-done.3, f32[2,8]{1,0:T(2,128)S(1)} %bitcast.4, s32[1]{0:T(128)} %copy.8.refs_2_, ...), custom_call_target="tpu_custom_call" | custom-call | flops 50331648 | bytes 2097152 | tf_op jit(solution)/shard_map/pallas_call | solution.py:131
  10.3 2.5 %collective-permute-done.2.refs_9_ = bf16[192,2,256]{2,1,0:T(2,128)(2,1)S(1)} collective-permute-done((bf16[192,2,256]{2,1,0:T(2,128)(2,1)}, bf16[192,2,256]{2,1,0:T(2,128)(2,1)S(1)}, u32[]{:S(2)}, u32[]{:S(2)}) %collective-permute-start.2) | collective-permute-done | bytes 196640 | tf_op jit(solution)/shard_map/ppermute | solution.py:418
  12.8 0.0 collective-permute-start.3
  12.8 0.0 collective-permute-done.refs_1_
  12.8 0.1 collective-permute-done.1.refs_2_
  12.9 0.0 collective-permute-done.4.refs_8_
  12.9 4.4 %shard_map.78 = (bf16[2,64,4096]{2,1,0:T(8,128)(2,1)S(1)}, f32[2,2,1024,128]{3,2,1,0:T(8,128)S(1)}, bf16[192,512]{1,0:T(8,128)(2,1)S(1)}) custom-call(s32[8,128]{1,0:T(8,128)S(1)} %broadcast_in_dim.12.refs_0_, s32[8,128]{1,0:T(8,128)S(1)} %collective-permute-done.refs_1_, s32[8,128]{1,0:T(8,128)S(1)} %collective-permute-done.1.refs_2_, ...), custom_call_target="tpu_custom_call" | custom-call | flops 2415919104 | bytes 4194304 | tf_op jit(solution)/shard_map/pallas_call | solution.py:313
  17.2 0.6 %collective-permute-start.5 = (bf16[192,512]{1,0:T(8,128)(2,1)S(1)}, bf16[192,512]{1,0:T(8,128)(2,1)S(1)}, u32[]{:S(2)}, u32[]{:S(2)}) collective-permute-start(bf16[192,512]{1,0:T(8,128)(2,1)S(1)} %get-tuple-element.19.refs_7_), channel_id=1, source_target_pairs={{0,1},{1,0},{2,3},{3,2},{4,5},{5,4},{6,7},{7,6},{8,9},{9,8},{10,11... | collective-permute-start | bytes 589832 | tf_op jit(solution)/shard_map/ppermute | solution.py:418
  17.8 0.9 %collective-permute-done.3.refs_7_.refs_9_ = bf16[192,2,256]{2,1,0:T(2,128)(2,1)S(1)} collective-permute-done((bf16[192,2,256]{2,1,0:T(2,128)(2,1)S(1)}, bf16[192,2,256]{2,1,0:T(2,128)(2,1)S(1)}, u32[]{:S(2)}, u32[]{:S(2)}) %collective-permute-start.3) | collective-permute-done | bytes 196640 | tf_op jit(solution)/shard_map/ppermute | solution.py:418
  18.7 1.4 %collective-permute-start.6 = (bf16[192,2,256]{2,1,0:T(2,128)(2,1)S(1)}, bf16[192,2,256]{2,1,0:T(2,128)(2,1)S(1)}, u32[]{:S(2)}, u32[]{:S(2)}) collective-permute-start(bf16[192,2,256]{2,1,0:T(2,128)(2,1)S(1)} %collective-permute-done.3.refs_7_.refs_9_), channel_id=1, source_target_pairs={{0,1},{1,0},{2,3},{3,2},{4,5},{5,4},{6,7},{7,6},{8,9},{9,8},{10,11... | collective-permute-start | bytes 589832 | tf_op jit(solution)/shard_map/ppermute | solution.py:418
  20.1 2.3 %shard_map.79.refs_6_ = bf16[2,64,4096]{2,1,0:T(8,128)(2,1)S(1)} custom-call(s32[8,128]{1,0:T(8,128)S(1)} %broadcast_in_dim.12.refs_0_, s32[8,128]{1,0:T(8,128)S(1)} %collective-permute-done.refs_1_, s32[8,128]{1,0:T(8,128)S(1)} %collective-permute-done.1.refs_2_, s32[8,128]{1,0:T(8,128)S(1)} %get-tuple-element.14.refs_3_, ...), custom_call_target="tpu_custom_call" | custom-call | flops 805306368 | bytes 4194304 | tf_op jit(solution)/shard_map/pallas_call | solution.py:313
  22.4 0.0 collective-permute-done.5.refs_8_
  22.4 0.0 collective-permute-done.6.refs_10_
  22.5 1.8 %shard_map.80 = (bf16[2,64,4096]{2,1,0:T(8,128)(2,1)}, f32[192,4,256]{2,1,0:T(4,128)}) custom-call(s32[8,128]{1,0:T(8,128)S(1)} %broadcast_in_dim.12.refs_0_, s32[8,128]{1,0:T(8,128)S(1)} %collective-permute-done.refs_1_, s32[8,128]{1,0:T(8,128)S(1)} %collective-permute-done.1.refs_2_, f32[8,128]{1,0:T(8,128)S(1)} %get-tuple-element.11.refs_4_.refs_3_, ...), custom_call_target="tpu_custom_call" | custom-call | flops 150994944 | bytes 2097152 | tf_op jit(solution)/shard_map/pallas_call | solution.py:396
  (1 shorter events, 0.0 us)
Async XLA Ops:
  0.6 12.1 %collective-permute-start.2 = (bf16[192,2,256]{2,1,0:T(2,128)(2,1)}, bf16[192,2,256]{2,1,0:T(2,128)(2,1)S(1)}, u32[]{:S(2)}, u32[]{:S(2)}) collective-permute-start(bf16[192,2,256]{2,1,0:T(2,128)(2,1)} %refs_4_.1), channel_id=1, source_target_pairs={{0,8},{4,12},{8,0},{12,4},{1,9},{5,13},{9,1},{13,5},{2,10},{6,14},... | collective-permute-start | bytes 589832 | tf_op jit(solution)/shard_map/ppermute | solution.py:418
  0.8 12.1 %collective-permute-start.4 = (bf16[192,2,256]{2,1,0:T(2,128)(2,1)}, bf16[192,2,256]{2,1,0:T(2,128)(2,1)S(1)}, u32[]{:S(2)}, u32[]{:S(2)}) collective-permute-start(bf16[192,2,256]{2,1,0:T(2,128)(2,1)} %refs_4_.1), channel_id=1, source_target_pairs={{0,4},{4,0},{8,12},{12,8},{1,5},{5,1},{9,13},{13,9},{2,6},{6,2},{1... | collective-permute-start | bytes 589832 | tf_op jit(solution)/shard_map/ppermute | solution.py:418
  1.6 11.2 %collective-permute-start = (s32[8,128]{1,0:T(8,128)S(1)}, s32[8,128]{1,0:T(8,128)S(1)}, u32[]{:S(2)}, u32[]{:S(2)}) collective-permute-start(s32[8,128]{1,0:T(8,128)S(1)} %broadcast_in_dim.12.refs_0_), channel_id=1, source_target_pairs={{0,4},{4,0},{8,12},{12,8},{1,5},{5,1},{9,13},{13,9},{2,6},{6,2},{1... | collective-permute-start | bytes 12296 | tf_op jit(solution)/shard_map/ppermute | solution.py:418
  3.0 9.9 %collective-permute-start.1 = (s32[8,128]{1,0:T(8,128)S(1)}, s32[8,128]{1,0:T(8,128)S(1)}, u32[]{:S(2)}, u32[]{:S(2)}) collective-permute-start(s32[8,128]{1,0:T(8,128)S(1)} %broadcast_in_dim.12.refs_0_), channel_id=1, source_target_pairs={{0,8},{4,12},{8,0},{12,4},{1,9},{5,13},{9,1},{13,5},{2,10},{6,14},... | collective-permute-start | bytes 12296 | tf_op jit(solution)/shard_map/ppermute | solution.py:418
  5.3 1.2 %copy-start = (bf16[2,64,4096]{2,1,0:T(8,128)(2,1)S(1)}, bf16[2,64,4096]{2,1,0:T(8,128)(2,1)}, u32[]{:S(2)}) copy-start(bf16[2,64,4096]{2,1,0:T(8,128)(2,1)} %refs_5_.1) | copy-start | bytes 3145732
  6.5 0.9 %copy-start.1 = (bf16[192,2,256]{2,1,0:T(2,128)(2,1)S(1)}, bf16[192,2,256]{2,1,0:T(2,128)(2,1)}, u32[]{:S(2)}) copy-start(bf16[192,2,256]{2,1,0:T(2,128)(2,1)} %refs_4_.1) | copy-start | bytes 589828
  7.4 0.7 %copy-start.2 = (f32[8,2]{0,1:T(2,128)S(1)}, f32[8,2]{0,1:T(2,128)}, u32[]{:S(2)}) copy-start(f32[8,2]{0,1:T(2,128)} %param.7) | copy-start | bytes 196
  8.1 0.7 %copy-start.3 = (s32[2]{0:T(128)S(1)}, s32[2]{0:T(128)}, u32[]{:S(2)}) copy-start(s32[2]{0:T(128)} %refs_0_.1) | copy-start | bytes 28
  8.7 0.7 %copy-start.4 = (s32[48]{0:T(128)S(1)}, s32[48]{0:T(128)}, u32[]{:S(2)}) copy-start(s32[48]{0:T(128)} %param.11) | copy-start | bytes 580
  12.8 5.9 %collective-permute-start.3 = (bf16[192,2,256]{2,1,0:T(2,128)(2,1)S(1)}, bf16[192,2,256]{2,1,0:T(2,128)(2,1)S(1)}, u32[]{:S(2)}, u32[]{:S(2)}) collective-permute-start(bf16[192,2,256]{2,1,0:T(2,128)(2,1)S(1)} %collective-permute-done.2.refs_9_), channel_id=1, source_target_pairs={{0,4},{4,0},{8,12},{12,8},{1,5},{5,1},{9,13},{13,9},{2,6},{6,2},{1... | collective-permute-start | bytes 589832 | tf_op jit(solution)/shard_map/ppermute | solution.py:418
  17.2 5.2 %collective-permute-start.5 = (bf16[192,512]{1,0:T(8,128)(2,1)S(1)}, bf16[192,512]{1,0:T(8,128)(2,1)S(1)}, u32[]{:S(2)}, u32[]{:S(2)}) collective-permute-start(bf16[192,512]{1,0:T(8,128)(2,1)S(1)} %get-tuple-element.19.refs_7_), channel_id=1, source_target_pairs={{0,1},{1,0},{2,3},{3,2},{4,5},{5,4},{6,7},{7,6},{8,9},{9,8},{10,11... | collective-permute-start | bytes 589832 | tf_op jit(solution)/shard_map/ppermute | solution.py:418
  18.7 3.8 %collective-permute-start.6 = (bf16[192,2,256]{2,1,0:T(2,128)(2,1)S(1)}, bf16[192,2,256]{2,1,0:T(2,128)(2,1)S(1)}, u32[]{:S(2)}, u32[]{:S(2)}) collective-permute-start(bf16[192,2,256]{2,1,0:T(2,128)(2,1)S(1)} %collective-permute-done.3.refs_7_.refs_9_), channel_id=1, source_target_pairs={{0,1},{1,0},{2,3},{3,2},{4,5},{5,4},{6,7},{7,6},{8,9},{9,8},{10,11... | collective-permute-start | bytes 589832 | tf_op jit(solution)/shard_map/ppermute | solution.py:418

commit v4 on v3

--- a/solution.py
+++ b/solution.py
@@ -12,6 +12,7 @@
 FLOOR = -1e9
 MASKED = -1e30
 TINY = 1e-30
+FAR = 60.0
 PIECES = 4
 LOG2E = math.log2(math.e)
 VMEM_LIMIT = 48 * 1024 * 1024
@@ -180,7 +181,7 @@
     bases = [ints_ref[1 + c : 2 + c, :][0, 0] for c in range(sets)]
     scale_of = scale_reader(floats_ref, 0, heads)
 
-    def compute():
+    def operands():
         signs = signs_ref[...]
         per_shard = []
         if with_codes:
@@ -201,26 +202,67 @@
         values = [jnp.concatenate([joined(j, 1), ones], axis=1) for j in range(heads)]
         row = lax.broadcasted_iota(jnp.int32, (rows, tokens), 0)
         key = lax.broadcasted_iota(jnp.int32, (rows, tokens), 1)
+        biases = []
         for c in range(sets):
             parts = []
             for offset, count in spans:
                 counted = (key < count) & (key + (offset - bases[c]) <= row)
                 parts.append(jnp.where(counted, 0.0, MASKED))
             bias = jnp.concatenate(parts, axis=1) if shards > 1 else parts[0]
-            bias = jnp.concatenate([bias] * group, axis=0)
+            biases.append(jnp.concatenate([bias] * group, axis=0))
+        return per_shard, keys, values, biases
+
+    def scores_of(c, j, keys, biases):
+        stacked = jnp.concatenate(
+            [
+                query_ref[c, :, (j * group + g) * half : (j * group + g + 1) * half]
+                for g in range(group)
+            ],
+            axis=0,
+        )
+        scores = lax.dot_general(
+            stacked, keys[j], (((1,), (1,)), ((), ())), preferred_element_type=jnp.float32
+        )
+        return scores + biases[c]
+
+    def tiles(scores):
+        for i in range(0, scores.shape[1], half):
+            yield scores[:, i : min(i + half, scores.shape[1])]
+
+    def compute_near():
+        _, keys, values, biases = operands()
+        worst = jnp.full((8, half), FLOOR, jnp.float32)
+        for c in range(sets):
             for j in range(heads):
                 factor = scale_of(j, 0) * LOG2E
-                stacked = jnp.concatenate(
-                    [
-                        query_ref[c, :, (j * group + g) * half : (j * group + g + 1) * half]
-                        for g in range(group)
-                    ],
-                    axis=0,
+                level = state[1][c, j]
+                probs = []
+                for part in tiles(scores_of(c, j, keys, biases)):
+                    size = part.shape[1]
+                    part = (part - level[:, :size]) * factor[:, :size]
+                    high = jnp.max(part.reshape(stack // 8, 8, size), axis=0)
+                    if size < half:
+                        high = jnp.concatenate([high, worst[:, size:]], axis=1)
+                    worst = jnp.maximum(worst, high)
+                    probs.append(jnp.exp2(part).astype(jnp.bfloat16))
+                weighted = jnp.dot(
+                    jnp.concatenate(probs, axis=1), values[j], preferred_element_type=jnp.float32
                 )
-                scores = lax.dot_general(
-                    stacked, keys[j], (((1,), (1,)), ((), ())), preferred_element_type=jnp.float32
-                )
-                scores = scores + bias
+                share = 1.0 / (weighted[:, half:] + 1.0)
+                for g in range(group):
+                    one = slice(g * rows, (g + 1) * rows)
+                    cols = slice((j * group + g) * half, (j * group + g + 1) * half)
+                    part = weighted[one, :half] * scale_of(j, 1)
+                    part = (part + state[0][c, :, cols].astype(jnp.float32)) * share[one]
+                    out_ref[c, :, cols] = part.astype(jnp.bfloat16)
+        return jnp.max(worst)
+
+    def compute():
+        per_shard, keys, values, biases = operands()
+        for c in range(sets):
+            for j in range(heads):
+                factor = scale_of(j, 0) * LOG2E
+                scores = scores_of(c, j, keys, biases)
                 top = jnp.max(scores, axis=1, keepdims=True)
                 top = jnp.broadcast_to(top, (stack, half))
                 if has_state:
@@ -229,8 +271,7 @@
                 else:
                     top = jnp.maximum(top, FLOOR)
                 probs = []
-                for i in range(0, scores.shape[1], half):
-                    part = scores[:, i : min(i + half, scores.shape[1])]
+                for part in tiles(scores):
                     size = part.shape[1]
                     part = jnp.exp2((part - top[:, :size]) * factor[:, :size])
                     probs.append(part.astype(jnp.bfloat16))
@@ -263,7 +304,11 @@
 
         @pl.when(needed)
         def _():
-            compute()
+            worst = compute_near()
+
+            @pl.when(worst > FAR)
+            def _():
+                compute()
 
         @pl.when(jnp.logical_not(needed))
         def _():

time: 24.5 us -> 24.1 us (0.984)
  Pallas kernels: 9.38 us -> 8.97 us
    pallas_call x2, Pallas kernels: 6.69 us -> 6.29 us  [attend(): pl.pallas_call(functools.partial(attend_kernel, len(counts) if info is No...]
  transfers between devices with their start and end apart: 7 -> 7, of which waited for: 3 -> 3; matrix products, arithmetic and copies ran while one was open for 0% -> 0% of each run, Pallas kernels for 31% -> 30%
where the time goes in v4:
time: 24.1 us; the launch traced here: 23.9 us
  Pallas kernels  8.97 us (37%)
  starting transfers between devices  5.91 us (25%)
  local copies, waits for them, and re-layouts  4.14 us (17%)
  waiting for transfers between devices  3.5 us (15%)
  between operations  1.34 us (6%)
    pallas_call x2, Pallas kernels, attend(): pl.pallas_call(functools.partial(attend_kernel, len(counts) if info is No...  6.29 us
    ppermute x7, starting transfers between devices, pair(): return lax.ppermute(value, axis, [(i, i ^ step) for i in range(size)])  5.91 us
    unnamed x10, local copies, waits for them, and re-layouts  4.14 us
    ppermute x7, waiting for transfers between devices, pair(): return lax.ppermute(value, axis, [(i, i ^ step) for i in range(size)])  3.5 us
    pallas_call x1, Pallas kernels, finish(): pl.pallas_call(functools.partial(finish_kernel, len(counts) if info is No...  1.81 us
    pallas_call x1, Pallas kernels, make_ready(): pl.pallas_call(ready_kernel, out_shape=[jax.ShapeDtypeStruct((8, 128), jn...  0.87 us
  transfers between devices with their start and end apart: 7, of which 3 were waited for; matrix products, arithmetic and copies ran while one was open for 0% of the time, Pallas kernels for 30%

profile of v4, /device:TPU:31, one launch (start us, length us, event | category | flops | bytes accessed | tf_op | source)
XLA Modules:
  0.0 23.9 jit_solution(8865033770171737321)
XLA Ops:
  0.6 0.1 collective-permute-start.2
  0.8 0.2 collective-permute-start.4
  1.6 1.4 %collective-permute-start = (s32[8,128]{1,0:T(8,128)S(1)}, s32[8,128]{1,0:T(8,128)S(1)}, u32[]{:S(2)}, u32[]{:S(2)}) collective-permute-start(s32[8,128]{1,0:T(8,128)S(1)} %broadcast_in_dim.12.refs_0_), channel_id=1, source_target_pairs={{0,4},{4,0},{8,12},{12,8},{1,5},{5,1},{9,13},{13,9},{2,6},{6,2},{1... | collective-permute-start | bytes 12296 | tf_op jit(solution)/shard_map/ppermute | solution.py:463
  3.0 2.3 %collective-permute-start.1 = (s32[8,128]{1,0:T(8,128)S(1)}, s32[8,128]{1,0:T(8,128)S(1)}, u32[]{:S(2)}, u32[]{:S(2)}) collective-permute-start(s32[8,128]{1,0:T(8,128)S(1)} %broadcast_in_dim.12.refs_0_), channel_id=1, source_target_pairs={{0,8},{4,12},{8,0},{12,4},{1,9},{5,13},{9,1},{13,5},{2,10},{6,14},... | collective-permute-start | bytes 12296 | tf_op jit(solution)/shard_map/ppermute | solution.py:463
  5.3 0.0 copy-start
  5.3 1.2 %copy-done = bf16[2,64,4096]{2,1,0:T(8,128)(2,1)S(1)} copy-done((bf16[2,64,4096]{2,1,0:T(8,128)(2,1)S(1)}, bf16[2,64,4096]{2,1,0:T(8,128)(2,1)}, u32[]{:S(2)}) %copy-start) | copy-done | bytes 1048600
  6.5 0.0 copy-start.1
  6.5 0.9 %copy-done.1 = bf16[192,2,256]{2,1,0:T(2,128)(2,1)S(1)} copy-done((bf16[192,2,256]{2,1,0:T(2,128)(2,1)S(1)}, bf16[192,2,256]{2,1,0:T(2,128)(2,1)}, u32[]{:S(2)}) %copy-start.1) | copy-done | bytes 196632
  7.4 0.0 copy-start.2
  7.4 0.7 %copy-done.2 = f32[8,2]{0,1:T(2,128)S(1)} copy-done((f32[8,2]{0,1:T(2,128)S(1)}, f32[8,2]{0,1:T(2,128)}, u32[]{:S(2)}) %copy-start.2) | copy-done | bytes 88
  8.1 0.0 copy-start.3
  8.1 0.7 %copy-done.3 = s32[2]{0:T(128)S(1)} copy-done((s32[2]{0:T(128)S(1)}, s32[2]{0:T(128)}, u32[]{:S(2)}) %copy-start.3) | copy-done | bytes 32
  8.7 0.0 copy-start.4
  8.7 0.7 %copy-done.4 = s32[48]{0:T(128)S(1)} copy-done((s32[48]{0:T(128)S(1)}, s32[48]{0:T(128)}, u32[]{:S(2)}) %copy-start.4) | copy-done | bytes 216
  9.4 0.9 %shard_map.77 = (s32[8,128]{1,0:T(8,128)S(1)}, f32[8,128]{1,0:T(8,128)S(1)}, bf16[256,256]{1,0:T(8,128)(2,1)S(1)}, f32[192,192]{1,0:T(8,128)S(1)}, bf16[192,512]...) custom-call(s32[2]{0:T(128)S(1)} %copy-done.3, f32[2,8]{1,0:T(2,128)S(1)} %bitcast.4, s32[1]{0:T(128)} %copy.8.refs_2_, ...), custom_call_target="tpu_custom_call" | custom-call | flops 50331648 | bytes 2097152 | tf_op jit(solution)/shard_map/pallas_call | solution.py:132
  10.3 2.5 %collective-permute-done.2.refs_9_ = bf16[192,2,256]{2,1,0:T(2,128)(2,1)S(1)} collective-permute-done((bf16[192,2,256]{2,1,0:T(2,128)(2,1)}, bf16[192,2,256]{2,1,0:T(2,128)(2,1)S(1)}, u32[]{:S(2)}, u32[]{:S(2)}) %collective-permute-start.2) | collective-permute-done | bytes 196640 | tf_op jit(solution)/shard_map/ppermute | solution.py:463
  12.8 0.0 collective-permute-start.3
  12.8 0.0 collective-permute-done.refs_1_
  12.8 0.1 collective-permute-done.1.refs_2_
  12.9 0.0 collective-permute-done.4.refs_8_
  12.9 4.4 %shard_map.78 = (bf16[2,64,4096]{2,1,0:T(8,128)(2,1)S(1)}, f32[2,2,1024,128]{3,2,1,0:T(8,128)S(1)}, bf16[192,512]{1,0:T(8,128)(2,1)S(1)}) custom-call(s32[8,128]{1,0:T(8,128)S(1)} %broadcast_in_dim.12.refs_0_, s32[8,128]{1,0:T(8,128)S(1)} %collective-permute-done.refs_1_, s32[8,128]{1,0:T(8,128)S(1)} %collective-permute-done.1.refs_2_, ...), custom_call_target="tpu_custom_call" | custom-call | flops 2415919104 | bytes 4194304 | tf_op jit(solution)/shard_map/pallas_call | solution.py:358
  17.2 0.6 %collective-permute-start.5 = (bf16[192,512]{1,0:T(8,128)(2,1)S(1)}, bf16[192,512]{1,0:T(8,128)(2,1)S(1)}, u32[]{:S(2)}, u32[]{:S(2)}) collective-permute-start(bf16[192,512]{1,0:T(8,128)(2,1)S(1)} %get-tuple-element.19.refs_7_), channel_id=1, source_target_pairs={{0,1},{1,0},{2,3},{3,2},{4,5},{5,4},{6,7},{7,6},{8,9},{9,8},{10,11... | collective-permute-start | bytes 589832 | tf_op jit(solution)/shard_map/ppermute | solution.py:463
  17.8 0.9 %collective-permute-done.3.refs_7_.refs_9_ = bf16[192,2,256]{2,1,0:T(2,128)(2,1)S(1)} collective-permute-done((bf16[192,2,256]{2,1,0:T(2,128)(2,1)S(1)}, bf16[192,2,256]{2,1,0:T(2,128)(2,1)S(1)}, u32[]{:S(2)}, u32[]{:S(2)}) %collective-permute-start.3) | collective-permute-done | bytes 196640 | tf_op jit(solution)/shard_map/ppermute | solution.py:463
  18.7 1.4 %collective-permute-start.6 = (bf16[192,2,256]{2,1,0:T(2,128)(2,1)S(1)}, bf16[192,2,256]{2,1,0:T(2,128)(2,1)S(1)}, u32[]{:S(2)}, u32[]{:S(2)}) collective-permute-start(bf16[192,2,256]{2,1,0:T(2,128)(2,1)S(1)} %collective-permute-done.3.refs_7_.refs_9_), channel_id=1, source_target_pairs={{0,1},{1,0},{2,3},{3,2},{4,5},{5,4},{6,7},{7,6},{8,9},{9,8},{10,11... | collective-permute-start | bytes 589832 | tf_op jit(solution)/shard_map/ppermute | solution.py:463
  20.1 1.9 %shard_map.79.refs_6_ = bf16[2,64,4096]{2,1,0:T(8,128)(2,1)S(1)} custom-call(s32[8,128]{1,0:T(8,128)S(1)} %broadcast_in_dim.12.refs_0_, s32[8,128]{1,0:T(8,128)S(1)} %collective-permute-done.refs_1_, s32[8,128]{1,0:T(8,128)S(1)} %collective-permute-done.1.refs_2_, s32[8,128]{1,0:T(8,128)S(1)} %get-tuple-element.14.refs_3_, ...), custom_call_target="tpu_custom_call" | custom-call | flops 805306368 | bytes 4194304 | tf_op jit(solution)/shard_map/pallas_call | solution.py:358
  22.0 0.0 collective-permute-done.5.refs_8_
  22.0 0.0 collective-permute-done.6.refs_10_
  22.1 1.8 %shard_map.80 = (bf16[2,64,4096]{2,1,0:T(8,128)(2,1)}, f32[192,4,256]{2,1,0:T(4,128)}) custom-call(s32[8,128]{1,0:T(8,128)S(1)} %broadcast_in_dim.12.refs_0_, s32[8,128]{1,0:T(8,128)S(1)} %collective-permute-done.refs_1_, s32[8,128]{1,0:T(8,128)S(1)} %collective-permute-done.1.refs_2_, f32[8,128]{1,0:T(8,128)S(1)} %get-tuple-element.11.refs_4_.refs_3_, ...), custom_call_target="tpu_custom_call" | custom-call | flops 150994944 | bytes 2097152 | tf_op jit(solution)/shard_map/pallas_call | solution.py:441
  (1 shorter events, 0.0 us)
Async XLA Ops:
  0.6 12.1 %collective-permute-start.2 = (bf16[192,2,256]{2,1,0:T(2,128)(2,1)}, bf16[192,2,256]{2,1,0:T(2,128)(2,1)S(1)}, u32[]{:S(2)}, u32[]{:S(2)}) collective-permute-start(bf16[192,2,256]{2,1,0:T(2,128)(2,1)} %refs_4_.1), channel_id=1, source_target_pairs={{0,8},{4,12},{8,0},{12,4},{1,9},{5,13},{9,1},{13,5},{2,10},{6,14},... | collective-permute-start | bytes 589832 | tf_op jit(solution)/shard_map/ppermute | solution.py:463
  0.8 12.1 %collective-permute-start.4 = (bf16[192,2,256]{2,1,0:T(2,128)(2,1)}, bf16[192,2,256]{2,1,0:T(2,128)(2,1)S(1)}, u32[]{:S(2)}, u32[]{:S(2)}) collective-permute-start(bf16[192,2,256]{2,1,0:T(2,128)(2,1)} %refs_4_.1), channel_id=1, source_target_pairs={{0,4},{4,0},{8,12},{12,8},{1,5},{5,1},{9,13},{13,9},{2,6},{6,2},{1... | collective-permute-start | bytes 589832 | tf_op jit(solution)/shard_map/ppermute | solution.py:463
  1.6 11.2 %collective-permute-start = (s32[8,128]{1,0:T(8,128)S(1)}, s32[8,128]{1,0:T(8,128)S(1)}, u32[]{:S(2)}, u32[]{:S(2)}) collective-permute-start(s32[8,128]{1,0:T(8,128)S(1)} %broadcast_in_dim.12.refs_0_), channel_id=1, source_target_pairs={{0,4},{4,0},{8,12},{12,8},{1,5},{5,1},{9,13},{13,9},{2,6},{6,2},{1... | collective-permute-start | bytes 12296 | tf_op jit(solution)/shard_map/ppermute | solution.py:463
  3.0 9.9 %collective-permute-start.1 = (s32[8,128]{1,0:T(8,128)S(1)}, s32[8,128]{1,0:T(8,128)S(1)}, u32[]{:S(2)}, u32[]{:S(2)}) collective-permute-start(s32[8,128]{1,0:T(8,128)S(1)} %broadcast_in_dim.12.refs_0_), channel_id=1, source_target_pairs={{0,8},{4,12},{8,0},{12,4},{1,9},{5,13},{9,1},{13,5},{2,10},{6,14},... | collective-permute-start | bytes 12296 | tf_op jit(solution)/shard_map/ppermute | solution.py:463
  5.3 1.2 %copy-start = (bf16[2,64,4096]{2,1,0:T(8,128)(2,1)S(1)}, bf16[2,64,4096]{2,1,0:T(8,128)(2,1)}, u32[]{:S(2)}) copy-start(bf16[2,64,4096]{2,1,0:T(8,128)(2,1)} %refs_5_.1) | copy-start | bytes 3145732
  6.5 0.9 %copy-start.1 = (bf16[192,2,256]{2,1,0:T(2,128)(2,1)S(1)}, bf16[192,2,256]{2,1,0:T(2,128)(2,1)}, u32[]{:S(2)}) copy-start(bf16[192,2,256]{2,1,0:T(2,128)(2,1)} %refs_4_.1) | copy-start | bytes 589828
  7.4 0.7 %copy-start.2 = (f32[8,2]{0,1:T(2,128)S(1)}, f32[8,2]{0,1:T(2,128)}, u32[]{:S(2)}) copy-start(f32[8,2]{0,1:T(2,128)} %param.7) | copy-start | bytes 196
  8.1 0.7 %copy-start.3 = (s32[2]{0:T(128)S(1)}, s32[2]{0:T(128)}, u32[]{:S(2)}) copy-start(s32[2]{0:T(128)} %refs_0_.1) | copy-start | bytes 28
  8.7 0.7 %copy-start.4 = (s32[48]{0:T(128)S(1)}, s32[48]{0:T(128)}, u32[]{:S(2)}) copy-start(s32[48]{0:T(128)} %param.11) | copy-start | bytes 580
  12.8 5.9 %collective-permute-start.3 = (bf16[192,2,256]{2,1,0:T(2,128)(2,1)S(1)}, bf16[192,2,256]{2,1,0:T(2,128)(2,1)S(1)}, u32[]{:S(2)}, u32[]{:S(2)}) collective-permute-start(bf16[192,2,256]{2,1,0:T(2,128)(2,1)S(1)} %collective-permute-done.2.refs_9_), channel_id=1, source_target_pairs={{0,4},{4,0},{8,12},{12,8},{1,5},{5,1},{9,13},{13,9},{2,6},{6,2},{1... | collective-permute-start | bytes 589832 | tf_op jit(solution)/shard_map/ppermute | solution.py:463
  17.2 4.8 %collective-permute-start.5 = (bf16[192,512]{1,0:T(8,128)(2,1)S(1)}, bf16[192,512]{1,0:T(8,128)(2,1)S(1)}, u32[]{:S(2)}, u32[]{:S(2)}) collective-permute-start(bf16[192,512]{1,0:T(8,128)(2,1)S(1)} %get-tuple-element.19.refs_7_), channel_id=1, source_target_pairs={{0,1},{1,0},{2,3},{3,2},{4,5},{5,4},{6,7},{7,6},{8,9},{9,8},{10,11... | collective-permute-start | bytes 589832 | tf_op jit(solution)/shard_map/ppermute | solution.py:463
  18.7 3.4 %collective-permute-start.6 = (bf16[192,2,256]{2,1,0:T(2,128)(2,1)S(1)}, bf16[192,2,256]{2,1,0:T(2,128)(2,1)S(1)}, u32[]{:S(2)}, u32[]{:S(2)}) collective-permute-start(bf16[192,2,256]{2,1,0:T(2,128)(2,1)S(1)} %collective-permute-done.3.refs_7_.refs_9_), channel_id=1, source_target_pairs={{0,1},{1,0},{2,3},{3,2},{4,5},{5,4},{6,7},{7,6},{8,9},{9,8},{10,11... | collective-permute-start | bytes 589832 | tf_op jit(solution)/shard_map/ppermute | solution.py:463

commit v5 on v4

--- a/solution.py
+++ b/solution.py
@@ -12,8 +12,8 @@
 FLOOR = -1e9
 MASKED = -1e30
 TINY = 1e-30
-FAR = 60.0
-PIECES = 4
+FAR = 2.0**60
+PIECES = (6, 4, 2)
 LOG2E = math.log2(math.e)
 VMEM_LIMIT = 48 * 1024 * 1024
 SMEM_SPEC = pl.BlockSpec(memory_space=pltpu.SMEM)
@@ -157,7 +157,7 @@
     )(starts, scales, counts, slots, rows, query)
 
 
-def attend_kernel(metas, steps, with_codes, has_state, last, with_pages, *refs):
+def attend_kernel(metas, steps, with_codes, has_state, last, *refs):
     refs = list(refs)
     info_ref = refs.pop(0) if metas == 0 else None
     count_refs = [refs.pop(0) for _ in range(metas)]
@@ -165,10 +165,12 @@
     codes_ref = refs.pop(0) if with_codes else None
     rows_refs = [refs.pop(0) for _ in range(len(steps) - with_codes)]
     state = [refs.pop(0) for _ in range(2)] if has_state else None
-    place_ref = refs.pop(0) if with_pages else None
+    place_ref = None if last else refs.pop(0)
+    pick_ref, moved_ref = (refs.pop(0), refs.pop(0)) if last else (None, None)
     out_ref = refs.pop(0)
     level_out = None if last else refs.pop(0)
-    moved_out = refs.pop(0) if with_pages else None
+    moved_out = refs.pop(0)
+    pick_out = refs.pop(0) if with_codes else None
     rot_scr = refs.pop(0)
 
     tokens, heads, width = rows_refs[0].shape
@@ -181,8 +183,7 @@
     bases = [ints_ref[1 + c : 2 + c, :][0, 0] for c in range(sets)]
     scale_of = scale_reader(floats_ref, 0, heads)
 
-    def operands():
-        signs = signs_ref[...]
+    def shard_codes():
         per_shard = []
         if with_codes:
             per_shard.append(
@@ -191,8 +192,9 @@
                     for j in range(heads)
                 ]
             )
-        per_shard += [codes_of(r, scale_of, signs, rot_scr) for r in rows_refs]
-
+        return per_shard + [codes_of(r, scale_of, signs_ref[...], rot_scr) for r in rows_refs]
+
+    def operands(per_shard):
         def joined(j, w):
             parts = [found[j][w] for found in per_shard]
             return jnp.concatenate(parts, axis=0) if shards > 1 else parts[0]
@@ -200,19 +202,24 @@
         keys = [joined(j, 0) for j in range(heads)]
         ones = jnp.ones((shards * tokens, half), jnp.bfloat16)
         values = [jnp.concatenate([joined(j, 1), ones], axis=1) for j in range(heads)]
-        row = lax.broadcasted_iota(jnp.int32, (rows, tokens), 0)
-        key = lax.broadcasted_iota(jnp.int32, (rows, tokens), 1)
-        biases = []
+        row = lax.broadcasted_iota(jnp.int32, (tokens, half), 1)
+        key = lax.broadcasted_iota(jnp.int32, (tokens, half), 0)
+        masked_keys = []
         for c in range(sets):
             parts = []
             for offset, count in spans:
                 counted = (key < count) & (key + (offset - bases[c]) <= row)
-                parts.append(jnp.where(counted, 0.0, MASKED))
-            bias = jnp.concatenate(parts, axis=1) if shards > 1 else parts[0]
-            biases.append(jnp.concatenate([bias] * group, axis=0))
-        return per_shard, keys, values, biases
-
-    def scores_of(c, j, keys, biases):
+                parts.append(jnp.where(counted, 0.0, MASKED).astype(jnp.bfloat16))
+            bias = jnp.concatenate(parts, axis=0) if shards > 1 else parts[0]
+            masked_keys.append([jnp.concatenate([keys[j], bias], axis=1) for j in range(heads)])
+        unit = (
+            lax.broadcasted_iota(jnp.int32, (rows, half), 0)
+            == lax.broadcasted_iota(jnp.int32, (rows, half), 1)
+        )
+        unit = jnp.where(unit, 1.0, 0.0).astype(jnp.bfloat16)
+        return masked_keys, values, jnp.concatenate([unit] * group, axis=0)
+
+    def scores_of(c, j, keys, units):
         stacked = jnp.concatenate(
             [
                 query_ref[c, :, (j * group + g) * half : (j * group + g + 1) * half]
@@ -220,35 +227,33 @@
             ],
             axis=0,
         )
-        scores = lax.dot_general(
-            stacked, keys[j], (((1,), (1,)), ((), ())), preferred_element_type=jnp.float32
+        stacked = jnp.concatenate([stacked, units], axis=1)
+        return lax.dot_general(
+            stacked, keys[c][j], (((1,), (1,)), ((), ())), preferred_element_type=jnp.float32
         )
-        return scores + biases[c]
 
     def tiles(scores):
         for i in range(0, scores.shape[1], half):
             yield scores[:, i : min(i + half, scores.shape[1])]
 
-    def compute_near():
-        _, keys, values, biases = operands()
-        worst = jnp.full((8, half), FLOOR, jnp.float32)
+    def compute_near(per_shard):
+        keys, values, units = operands(per_shard)
+        worst = jnp.zeros((8, half), jnp.float32)
         for c in range(sets):
             for j in range(heads):
                 factor = scale_of(j, 0) * LOG2E
                 level = state[1][c, j]
                 probs = []
-                for part in tiles(scores_of(c, j, keys, biases)):
+                for part in tiles(scores_of(c, j, keys, units)):
                     size = part.shape[1]
                     part = (part - level[:, :size]) * factor[:, :size]
-                    high = jnp.max(part.reshape(stack // 8, 8, size), axis=0)
-                    if size < half:
-                        high = jnp.concatenate([high, worst[:, size:]], axis=1)
-                    worst = jnp.maximum(worst, high)
                     probs.append(jnp.exp2(part).astype(jnp.bfloat16))
                 weighted = jnp.dot(
                     jnp.concatenate(probs, axis=1), values[j], preferred_element_type=jnp.float32
                 )
-                share = 1.0 / (weighted[:, half:] + 1.0)
+                total = weighted[:, half:]
+                worst = jnp.maximum(worst, jnp.max(total.reshape(stack // 8, 8, half), axis=0))
+                share = 1.0 / (total + 1.0)
                 for g in range(group):
                     one = slice(g * rows, (g + 1) * rows)
                     cols = slice((j * group + g) * half, (j * group + g + 1) * half)
@@ -257,12 +262,12 @@
                     out_ref[c, :, cols] = part.astype(jnp.bfloat16)
         return jnp.max(worst)
 
-    def compute():
-        per_shard, keys, values, biases = operands()
+    def compute(per_shard):
+        keys, values, units = operands(per_shard)
         for c in range(sets):
             for j in range(heads):
                 factor = scale_of(j, 0) * LOG2E
-                scores = scores_of(c, j, keys, biases)
+                scores = scores_of(c, j, keys, units)
                 top = jnp.max(scores, axis=1, keepdims=True)
                 top = jnp.broadcast_to(top, (stack, half))
                 if has_state:
@@ -294,9 +299,17 @@
                     out_ref[c, :, cols] = (part / total[one]).astype(jnp.bfloat16)
                 if not last:
                     level_out[c, j] = top + jnp.log2(total) / factor
-        return per_shard
+
+    def picked(pick, found):
+        own = jnp.concatenate([part for parts in found for part in parts], axis=1)
+        return jnp.dot(pick, own, preferred_element_type=jnp.float32)
 
     if last:
+
+        def deliver(per_shard):
+            total = picked(pick_ref[...], per_shard[0]) + moved_ref[...].astype(jnp.float32)
+            moved_out[...] = total.astype(jnp.bfloat16)
+
         latest = bases[0]
         for base in bases[1:]:
             latest = jnp.maximum(latest, base)
@@ -304,30 +317,34 @@
 
         @pl.when(needed)
         def _():
-            worst = compute_near()
+            per_shard = shard_codes()
+            worst = compute_near(per_shard)
+            deliver(per_shard)
 
             @pl.when(worst > FAR)
             def _():
-                compute()
+                compute(per_shard)
 
         @pl.when(jnp.logical_not(needed))
         def _():
+            deliver(shard_codes())
             out_ref[...] = state[0][...]
 
     else:
-        per_shard = compute()
-    if with_pages:
+        per_shard = shard_codes()
+        compute(per_shard)
         place = place_ref[...]
         total = None
         for (offset, count), found in zip(spans, per_shard):
-            pick = picker(place, offset, count)
-            own = jnp.concatenate([part for parts in found for part in parts], axis=1)
-            part = jnp.dot(pick, own, preferred_element_type=jnp.float32)
+            part = picked(picker(place, offset, count), found)
             total = part if total is None else total + part
+        if with_codes:
+            ((offset, count),) = spans_of(count_refs, info_ref, (3,), tokens)
+            pick_out[...] = picker(place, offset, count)
         moved_out[...] = total.astype(jnp.bfloat16)
 
 
-def attend(counts, info, steps, ready, rows, codes=None, state=None, last=False):
+def attend(counts, info, steps, ready, rows, codes=None, state=None, picked=None):
     ints, floats, signs, place, _, query = ready
     tokens, heads, width = rows[0].shape
     half = width // 2
@@ -341,18 +358,16 @@
     args += rows
     if state is not None:
         args += list(state)
-    if not last:
-        args.append(place)
+    last = picked is not None
+    args += list(picked) if last else [place]
     specs += [VMEM_SPEC] * (len(args) - len(specs))
     outs = [jax.ShapeDtypeStruct(query.shape, jnp.bfloat16)]
-    out_specs = [VMEM_SPEC]
-    scratch = [pltpu.VMEM((2, tokens * heads, half), jnp.float32)]
     if not last:
-        outs += [
-            jax.ShapeDtypeStruct((sets, heads, group * query_rows, half), jnp.float32),
-            jax.ShapeDtypeStruct((tokens, heads * width), jnp.bfloat16),
-        ]
-        out_specs += [VMEM_SPEC] * 2
+        stacked = (sets, heads, group * query_rows, half)
+        outs.append(jax.ShapeDtypeStruct(stacked, jnp.float32))
+    outs.append(jax.ShapeDtypeStruct((tokens, heads * width), jnp.bfloat16))
+    if codes is not None:
+        outs.append(jax.ShapeDtypeStruct((tokens, tokens), jnp.bfloat16))
     keys = tokens * len(steps)
     work = sets * heads * group * query_rows * keys
     return pl.pallas_call(
@@ -363,12 +378,11 @@
             codes is not None,
             state is not None,
             last,
-            not last,
         ),
         out_shape=outs,
         in_specs=specs,
-        out_specs=out_specs,
-        scratch_shapes=scratch,
+        out_specs=[VMEM_SPEC] * len(outs),
+        scratch_shapes=[pltpu.VMEM((2, tokens * heads, half), jnp.float32)],
         compiler_params=pltpu.CompilerParams(vmem_limit_bytes=VMEM_LIMIT),
         cost_estimate=pl.CostEstimate(
             flops=work * half * 8, bytes_accessed=4 << 20, transcendentals=work
@@ -376,13 +390,11 @@
     )(*args)
 
 
-def finish_kernel(metas, steps, *refs):
-    refs = list(refs)
-    info_ref = refs.pop(0) if metas == 0 else None
-    count_refs = [refs.pop(0) for _ in range(metas)]
-    floats_ref, signs_ref, place_ref, result_ref, own, other, own_rows, other_rows = refs[:8]
-    attention_out, cache_out, rot_scr, cache_scr, sems = refs[8:]
-    tokens, heads, width = own_rows.shape
+def finish_kernel(
+    floats_ref, signs_ref, pick_ref, result_ref, own, other, other_rows, *outs_and_scratch
+):
+    attention_out, cache_out, rot_scr, cache_scr, sems = outs_and_scratch
+    tokens, heads, width = other_rows.shape
     half = width // 2
     sets = result_ref.shape[0]
     rep_id = lax.axis_index("rep")
@@ -391,69 +403,66 @@
     ]
     for copy in sent:
         copy.start()
-    signs = signs_ref[...]
-    ((offset, count),) = spans_of(count_refs, info_ref, steps, tokens)
-    pick = picker(place_ref[...], offset, count)
-    sides = []
-    for side, (moved, rows) in enumerate(((own, own_rows), (other, other_rows))):
-        scale_of = scale_reader(floats_ref, side, heads)
-        sides.append((moved, scale_of, codes_of(rows, scale_of, signs, rot_scr)))
-    size = tokens // PIECES
-    pieces = [
-        pltpu.make_async_copy(
-            cache_scr.at[pl.ds(i * size, size)],
-            cache_out.at[pl.ds(i * size, size)],
-            sems.at[sets + i],
+    scales = [scale_reader(floats_ref, side, heads) for side in range(2)]
+    found = codes_of(other_rows, scales[1], signs_ref[...], rot_scr)
+    pick = pick_ref[...]
+    pieces = []
+    start = 0
+    for i, eighths in enumerate(PIECES):
+        size = tokens // 12 * eighths
+        here = pl.ds(start, size)
+        pieces.append(
+            (
+                slice(start, start + size),
+                pltpu.make_async_copy(cache_scr.at[here], cache_out.at[here], sems.at[sets + i]),
+            )
         )
-        for i in range(PIECES)
-    ]
+        start += size
 
     for turn in range(2):
 
         @pl.when(rep_id == turn)
         def _(turn=turn):
-            for i, piece in enumerate(pieces):
-                here = slice(i * size, (i + 1) * size)
-                for side, (moved, scale_of, found) in enumerate(sides):
+            for here, piece in pieces:
+                for side, moved in enumerate((own, other)):
                     first = (side if turn == 0 else 1 - side) * heads
                     for j in range(heads):
                         for w in range(2):
                             cols = slice((2 * j + w) * half, (2 * j + w + 1) * half)
-                            part = jnp.dot(
-                                pick[here], found[j][w], preferred_element_type=jnp.float32
-                            )
-                            part = (part + moved[here, cols].astype(jnp.float32)) * scale_of(j, w)
+                            part = moved[here, cols].astype(jnp.float32)
+                            if side == 1:
+                                part = part + jnp.dot(
+                                    pick[here], found[j][w], preferred_element_type=jnp.float32
+                                )
+                            part = part * scales[side](j, w)
                             cache_scr[here, first + j, w * half : (w + 1) * half] = part
                 piece.start()
 
-    for copy in sent + pieces:
+    for copy in sent + [piece for _, piece in pieces]:
         copy.wait()
 
 
-def finish(counts, info, steps, ready, result, own, other, own_rows, other_rows):
-    _, floats, signs, place, _, _ = ready
-    tokens, heads, width = own_rows.shape
+def finish(ready, pick, result, own, other, other_rows):
+    _, floats, signs, _, _, _ = ready
+    tokens, heads, width = other_rows.shape
     cache = (tokens, 2 * heads, width)
-    args = list(counts) if info is None else [info]
-    specs = [VMEM_SPEC] * len(counts) if info is None else [SMEM_SPEC]
-    args += [floats, signs, place, result, own, other, own_rows, other_rows]
-    specs += [VMEM_SPEC] * 8
+    args = [floats, signs, pick, result, own, other, other_rows]
     return pl.pallas_call(
-        functools.partial(finish_kernel, len(counts) if info is None else 0, steps),
+        finish_kernel,
         out_shape=[
             jax.ShapeDtypeStruct(result.shape, result.dtype),
             jax.ShapeDtypeStruct(cache, jnp.float32),
         ],
-        in_specs=specs,
+        in_specs=[VMEM_SPEC] * len(args),
         out_specs=[pl.BlockSpec(memory_space=pl.ANY)] * 2,
         scratch_shapes=[
             pltpu.VMEM((2, tokens * heads, width // 2), jnp.float32),
             pltpu.VMEM(cache, jnp.float32),
-            pltpu.SemaphoreType.DMA((result.shape[0] + PIECES,)),
+            pltpu.SemaphoreType.DMA((result.shape[0] + len(PIECES),)),
         ],
         compiler_params=pltpu.CompilerParams(vmem_limit_bytes=VMEM_LIMIT),
         cost_estimate=pl.CostEstimate(
-            flops=tokens * tokens * heads * width * 8, bytes_accessed=2 << 20, transcendentals=0
+            flops=tokens * tokens * heads * width * 4, bytes_accessed=2 << 20, transcendentals=0
         ),
     )(*args)
 
@@ -472,11 +481,11 @@
     count = jnp.broadcast_to(shard_counts[:, None], (8, 128))
     counts = [count, pair(count, "ctx", 1), pair(count, "ctx", 2)]
     corner = pair(across, "ctx", 1)
-    *state, moved = attend(counts, None, (0, 1, 2), ready, [beside, across], ready[4])
+    *state, moved, pick = attend(counts, None, (0, 1, 2), ready, [beside, across], ready[4])
     moved_other = pair(moved, "rep", 1)
     corner_other = pair(corner, "rep", 1)
-    (result,) = attend(counts, None, (3,), ready, [corner], None, state, True)
-    return finish(counts, None, (3,), ready, result, moved, moved_other, corner, corner_other)
+    result, own = attend(counts, None, (3,), ready, [corner], None, state, (pick, moved))
+    return finish(ready, pick, result, own, moved_other, corner_other)
 
 
 def body_any(kv_rows, kv_scales, queries, shard_counts, span_starts, block_slots):
@@ -495,9 +504,8 @@
 
     *state, moved = attend([], info[:1], (0,), ready, [every[0]])
     (state, moved), _ = lax.scan(step, (tuple(state), moved), (every[1:], info[1:]))
-    none = jnp.zeros((1, 2), jnp.int32)
-    other = pair(moved, "rep", 1)
-    return finish([], none, (0,), ready, state[0], moved, other, kv_rows, kv_rows)
+    none = jnp.zeros((kv_rows.shape[0],) * 2, jnp.bfloat16)
+    return finish(ready, none, state[0], moved, pair(moved, "rep", 1), kv_rows)
 
 
 def solution(mesh):

time: 24.1 us -> 23.8 us (0.988)
  waiting for transfers between devices: 3.5 us -> 3.15 us
    ppermute x7, waiting for transfers between devices: 3.5 us -> 3.15 us  [pair(): return lax.ppermute(value, axis, [(i, i ^ step) for i in range(size)])]
  transfers between devices with their start and end apart: 7 -> 7, of which waited for: 3 -> 3; matrix products, arithmetic and copies ran while one was open for 0% -> 0% of each run, Pallas kernels for 30% -> 31%
where the time goes in v5:
time: 23.8 us; the launch traced here: 23.5 us
  Pallas kernels  8.99 us (38%)
  starting transfers between devices  5.92 us (25%)
  local copies, waits for them, and re-layouts  4.14 us (17%)
  waiting for transfers between devices  3.15 us (13%)
  between operations  1.34 us (6%)
    pallas_call x2, Pallas kernels, attend(): pl.pallas_call(functools.partial(attend_kernel, len(counts) if info is No...  6.52 us
    ppermute x7, starting transfers between devices, pair(): return lax.ppermute(value, axis, [(i, i ^ step) for i in range(size)])  5.92 us
    unnamed x10, local copies, waits for them, and re-layouts  4.14 us
    ppermute x7, waiting for transfers between devices, pair(): return lax.ppermute(value, axis, [(i, i ^ step) for i in range(size)])  3.15 us
    pallas_call x1, Pallas kernels, finish(): pl.pallas_call(finish_kernel, out_shape=[jax.ShapeDtypeStruct(result.shap...  1.6 us
    pallas_call x1, Pallas kernels, make_ready(): pl.pallas_call(ready_kernel, out_shape=[jax.ShapeDtypeStruct((8, 128), jn...  0.87 us
  transfers between devices with their start and end apart: 7, of which 3 were waited for; matrix products, arithmetic and copies ran while one was open for 0% of the time, Pallas kernels for 31%

profile of v5, /device:TPU:31, one launch (start us, length us, event | category | flops | bytes accessed | tf_op | source)
XLA Modules:
  0.0 23.5 jit_solution(4320196717469272712)
XLA Ops:
  0.6 0.1 collective-permute-start.3
  0.8 0.2 collective-permute-start.2
  1.6 1.4 %collective-permute-start = (s32[8,128]{1,0:T(8,128)S(1)}, s32[8,128]{1,0:T(8,128)S(1)}, u32[]{:S(2)}, u32[]{:S(2)}) collective-permute-start(s32[8,128]{1,0:T(8,128)S(1)} %broadcast_in_dim.13.refs_0_), channel_id=1, source_target_pairs={{0,4},{4,0},{8,12},{12,8},{1,5},{5,1},{9,13},{13,9},{2,6},{6,2},{1... | collective-permute-start | bytes 12296 | tf_op jit(solution)/shard_map/ppermute | solution.py:472
  3.0 2.3 %collective-permute-start.1 = (s32[8,128]{1,0:T(8,128)S(1)}, s32[8,128]{1,0:T(8,128)S(1)}, u32[]{:S(2)}, u32[]{:S(2)}) collective-permute-start(s32[8,128]{1,0:T(8,128)S(1)} %broadcast_in_dim.13.refs_0_), channel_id=1, source_target_pairs={{0,8},{4,12},{8,0},{12,4},{1,9},{5,13},{9,1},{13,5},{2,10},{6,14},... | collective-permute-start | bytes 12296 | tf_op jit(solution)/shard_map/ppermute | solution.py:472
  5.3 0.0 copy-start
  5.3 1.2 %copy-done = bf16[2,64,4096]{2,1,0:T(8,128)(2,1)S(1)} copy-done((bf16[2,64,4096]{2,1,0:T(8,128)(2,1)S(1)}, bf16[2,64,4096]{2,1,0:T(8,128)(2,1)}, u32[]{:S(2)}) %copy-start) | copy-done | bytes 1048600
  6.5 0.0 copy-start.1
  6.5 0.9 %copy-done.1 = bf16[192,2,256]{2,1,0:T(2,128)(2,1)S(1)} copy-done((bf16[192,2,256]{2,1,0:T(2,128)(2,1)S(1)}, bf16[192,2,256]{2,1,0:T(2,128)(2,1)}, u32[]{:S(2)}) %copy-start.1) | copy-done | bytes 196632
  7.4 0.0 copy-start.2
  7.4 0.7 %copy-done.2 = f32[8,2]{0,1:T(2,128)S(1)} copy-done((f32[8,2]{0,1:T(2,128)S(1)}, f32[8,2]{0,1:T(2,128)}, u32[]{:S(2)}) %copy-start.2) | copy-done | bytes 88
  8.1 0.0 copy-start.3
  8.1 0.7 %copy-done.3 = s32[2]{0:T(128)S(1)} copy-done((s32[2]{0:T(128)S(1)}, s32[2]{0:T(128)}, u32[]{:S(2)}) %copy-start.3) | copy-done | bytes 32
  8.7 0.0 copy-start.4
  8.7 0.7 %copy-done.4 = s32[48]{0:T(128)S(1)} copy-done((s32[48]{0:T(128)S(1)}, s32[48]{0:T(128)}, u32[]{:S(2)}) %copy-start.4) | copy-done | bytes 216
  9.4 0.9 %shard_map.77 = (s32[8,128]{1,0:T(8,128)S(1)}, f32[8,128]{1,0:T(8,128)S(1)}, bf16[256,256]{1,0:T(8,128)(2,1)S(1)}, f32[192,192]{1,0:T(8,128)S(1)}, bf16[192,512]...) custom-call(s32[2]{0:T(128)S(1)} %copy-done.3, f32[2,8]{1,0:T(2,128)S(1)} %bitcast.4, s32[1]{0:T(128)} %copy.8.refs_2_, ...), custom_call_target="tpu_custom_call" | custom-call | flops 50331648 | bytes 2097152 | tf_op jit(solution)/shard_map/pallas_call | solution.py:132
  10.3 2.5 %collective-permute-done.3.refs_9_ = bf16[192,2,256]{2,1,0:T(2,128)(2,1)S(1)} collective-permute-done((bf16[192,2,256]{2,1,0:T(2,128)(2,1)}, bf16[192,2,256]{2,1,0:T(2,128)(2,1)S(1)}, u32[]{:S(2)}, u32[]{:S(2)}) %collective-permute-start.3) | collective-permute-done | bytes 196640 | tf_op jit(solution)/shard_map/ppermute | solution.py:472
  12.8 0.0 collective-permute-start.4
  12.8 0.0 collective-permute-done.refs_1_
  12.8 0.1 collective-permute-done.1.refs_2_
  12.9 0.0 collective-permute-done.2.refs_8_
  12.9 4.7 %shard_map.78 = (bf16[2,64,4096]{2,1,0:T(8,128)(2,1)S(1)}, f32[2,2,1024,128]{3,2,1,0:T(8,128)S(1)}, bf16[192,512]{1,0:T(8,128)(2,1)S(1)}, bf16[192,192]{1,0:T(8,128)(2,1)S(1)}) custom-call(s32[8,128]{1,0:T(8,128)S(1)} %broadcast_in_dim.13.refs_0_, s32[8,128]{1,0:T(8,128)S(1)} %collective-permute-done.refs_1_, s32[8,128]{1,0:T(8,128)S(1)} %collective-permute-done.1.refs_2_, ...), custom_call_target="tpu_custom_call" | custom-call | flops 2415919104 | bytes 4194304 | tf_op jit(solution)/shard_map/pallas_call | solution.py:373
  17.6 0.6 %collective-permute-start.5 = (bf16[192,512]{1,0:T(8,128)(2,1)S(1)}, bf16[192,512]{1,0:T(8,128)(2,1)S(1)}, u32[]{:S(2)}, u32[]{:S(2)}) collective-permute-start(bf16[192,512]{1,0:T(8,128)(2,1)S(1)} %get-tuple-element.23.refs_11_), channel_id=1, source_target_pairs={{0,1},{1,0},{2,3},{3,2},{4,5},{5,4},{6,7},{7,6},{8,9},{9,8},{10,11... | collective-permute-start | bytes 589832 | tf_op jit(solution)/shard_map/ppermute | solution.py:472
  18.1 0.6 %collective-permute-done.4.refs_7_ = bf16[192,2,256]{2,1,0:T(2,128)(2,1)S(1)} collective-permute-done((bf16[192,2,256]{2,1,0:T(2,128)(2,1)S(1)}, bf16[192,2,256]{2,1,0:T(2,128)(2,1)S(1)}, u32[]{:S(2)}, u32[]{:S(2)}) %collective-permute-start.4) | collective-permute-done | bytes 196640 | tf_op jit(solution)/shard_map/ppermute | solution.py:472
  18.7 1.4 %collective-permute-start.6 = (bf16[192,2,256]{2,1,0:T(2,128)(2,1)S(1)}, bf16[192,2,256]{2,1,0:T(2,128)(2,1)S(1)}, u32[]{:S(2)}, u32[]{:S(2)}) collective-permute-start(bf16[192,2,256]{2,1,0:T(2,128)(2,1)S(1)} %collective-permute-done.4.refs_7_), channel_id=1, source_target_pairs={{0,1},{1,0},{2,3},{3,2},{4,5},{5,4},{6,7},{7,6},{8,9},{9,8},{10,11... | collective-permute-start | bytes 589832 | tf_op jit(solution)/shard_map/ppermute | solution.py:472
  20.1 1.8 %shard_map.79 = (bf16[2,64,4096]{2,1,0:T(8,128)(2,1)S(1)}, bf16[192,512]{1,0:T(8,128)(2,1)S(1)}) custom-call(s32[8,128]{1,0:T(8,128)S(1)} %broadcast_in_dim.13.refs_0_, s32[8,128]{1,0:T(8,128)S(1)} %collective-permute-done.refs_1_, s32[8,128]{1,0:T(8,128)S(1)} %collective-permute-done.1.refs_2_, s32[8,128]{1,0:T(8,128)S(1)} %get-tuple-element.16.refs_3_, ...), custom_call_target="tpu_custom_call" | custom-call | flops 805306368 | bytes 4194304 | tf_op jit(solution)/shard_map/pallas_call | solution.py:373
  21.9 0.0 collective-permute-done.5.other
  21.9 0.0 collective-permute-done.6.other_rows
  21.9 1.6 %shard_map.80 = (bf16[2,64,4096]{2,1,0:T(8,128)(2,1)}, f32[192,4,256]{2,1,0:T(4,128)}) custom-call(f32[8,128]{1,0:T(8,128)S(1)} %get-tuple-element.14.refs_4_.floats_ref, bf16[256,256]{1,0:T(8,128)(2,1)S(1)} %get-tuple-element.15.refs_5_.signs_ref, bf16[192,192]{1,0:T(8,128)(2,1)S(1)} %get-tuple-element.20.refs_10_.pick_ref, ...), custom_call_target="tpu_custom_call" | custom-call | flops 75497472 | bytes 2097152 | tf_op jit(solution)/shard_map/pallas_call | solution.py:450
  (1 shorter events, 0.0 us)
Async XLA Ops:
  0.6 12.1 %collective-permute-start.3 = (bf16[192,2,256]{2,1,0:T(2,128)(2,1)}, bf16[192,2,256]{2,1,0:T(2,128)(2,1)S(1)}, u32[]{:S(2)}, u32[]{:S(2)}) collective-permute-start(bf16[192,2,256]{2,1,0:T(2,128)(2,1)} %refs_4_.1), channel_id=1, source_target_pairs={{0,8},{4,12},{8,0},{12,4},{1,9},{5,13},{9,1},{13,5},{2,10},{6,14},... | collective-permute-start | bytes 589832 | tf_op jit(solution)/shard_map/ppermute | solution.py:472
  0.8 12.1 %collective-permute-start.2 = (bf16[192,2,256]{2,1,0:T(2,128)(2,1)}, bf16[192,2,256]{2,1,0:T(2,128)(2,1)S(1)}, u32[]{:S(2)}, u32[]{:S(2)}) collective-permute-start(bf16[192,2,256]{2,1,0:T(2,128)(2,1)} %refs_4_.1), channel_id=1, source_target_pairs={{0,4},{4,0},{8,12},{12,8},{1,5},{5,1},{9,13},{13,9},{2,6},{6,2},{1... | collective-permute-start | bytes 589832 | tf_op jit(solution)/shard_map/ppermute | solution.py:472
  1.6 11.2 %collective-permute-start = (s32[8,128]{1,0:T(8,128)S(1)}, s32[8,128]{1,0:T(8,128)S(1)}, u32[]{:S(2)}, u32[]{:S(2)}) collective-permute-start(s32[8,128]{1,0:T(8,128)S(1)} %broadcast_in_dim.13.refs_0_), channel_id=1, source_target_pairs={{0,4},{4,0},{8,12},{12,8},{1,5},{5,1},{9,13},{13,9},{2,6},{6,2},{1... | collective-permute-start | bytes 12296 | tf_op jit(solution)/shard_map/ppermute | solution.py:472
  3.0 9.9 %collective-permute-start.1 = (s32[8,128]{1,0:T(8,128)S(1)}, s32[8,128]{1,0:T(8,128)S(1)}, u32[]{:S(2)}, u32[]{:S(2)}) collective-permute-start(s32[8,128]{1,0:T(8,128)S(1)} %broadcast_in_dim.13.refs_0_), channel_id=1, source_target_pairs={{0,8},{4,12},{8,0},{12,4},{1,9},{5,13},{9,1},{13,5},{2,10},{6,14},... | collective-permute-start | bytes 12296 | tf_op jit(solution)/shard_map/ppermute | solution.py:472
  5.3 1.2 %copy-start = (bf16[2,64,4096]{2,1,0:T(8,128)(2,1)S(1)}, bf16[2,64,4096]{2,1,0:T(8,128)(2,1)}, u32[]{:S(2)}) copy-start(bf16[2,64,4096]{2,1,0:T(8,128)(2,1)} %refs_5_.1) | copy-start | bytes 3145732
  6.5 0.9 %copy-start.1 = (bf16[192,2,256]{2,1,0:T(2,128)(2,1)S(1)}, bf16[192,2,256]{2,1,0:T(2,128)(2,1)}, u32[]{:S(2)}) copy-start(bf16[192,2,256]{2,1,0:T(2,128)(2,1)} %refs_4_.1) | copy-start | bytes 589828
  7.4 0.7 %copy-start.2 = (f32[8,2]{0,1:T(2,128)S(1)}, f32[8,2]{0,1:T(2,128)}, u32[]{:S(2)}) copy-start(f32[8,2]{0,1:T(2,128)} %param.7) | copy-start | bytes 196
  8.1 0.7 %copy-start.3 = (s32[2]{0:T(128)S(1)}, s32[2]{0:T(128)}, u32[]{:S(2)}) copy-start(s32[2]{0:T(128)} %refs_0_.1) | copy-start | bytes 28
  8.7 0.7 %copy-start.4 = (s32[48]{0:T(128)S(1)}, s32[48]{0:T(128)}, u32[]{:S(2)}) copy-start(s32[48]{0:T(128)} %param.11) | copy-start | bytes 580
  12.8 5.9 %collective-permute-start.4 = (bf16[192,2,256]{2,1,0:T(2,128)(2,1)S(1)}, bf16[192,2,256]{2,1,0:T(2,128)(2,1)S(1)}, u32[]{:S(2)}, u32[]{:S(2)}) collective-permute-start(bf16[192,2,256]{2,1,0:T(2,128)(2,1)S(1)} %collective-permute-done.3.refs_9_), channel_id=1, source_target_pairs={{0,4},{4,0},{8,12},{12,8},{1,5},{5,1},{9,13},{13,9},{2,6},{6,2},{1... | collective-permute-start | bytes 589832 | tf_op jit(solution)/shard_map/ppermute | solution.py:472
  17.6 4.3 %collective-permute-start.5 = (bf16[192,512]{1,0:T(8,128)(2,1)S(1)}, bf16[192,512]{1,0:T(8,128)(2,1)S(1)}, u32[]{:S(2)}, u32[]{:S(2)}) collective-permute-start(bf16[192,512]{1,0:T(8,128)(2,1)S(1)} %get-tuple-element.23.refs_11_), channel_id=1, source_target_pairs={{0,1},{1,0},{2,3},{3,2},{4,5},{5,4},{6,7},{7,6},{8,9},{9,8},{10,11... | collective-permute-start | bytes 589832 | tf_op jit(solution)/shard_map/ppermute | solution.py:472
  18.7 3.2 %collective-permute-start.6 = (bf16[192,2,256]{2,1,0:T(2,128)(2,1)S(1)}, bf16[192,2,256]{2,1,0:T(2,128)(2,1)S(1)}, u32[]{:S(2)}, u32[]{:S(2)}) collective-permute-start(bf16[192,2,256]{2,1,0:T(2,128)(2,1)S(1)} %collective-permute-done.4.refs_7_), channel_id=1, source_target_pairs={{0,1},{1,0},{2,3},{3,2},{4,5},{5,4},{6,7},{7,6},{8,9},{9,8},{10,11... | collective-permute-start | bytes 589832 | tf_op jit(solution)/shard_map/ppermute | solution.py:472

commit v6 on v5

--- a/solution.py
+++ b/solution.py
@@ -68,7 +68,7 @@
 
 def spans_of(count_refs, info_ref, steps, tokens):
     if info_ref is not None:
-        return [(info_ref[0, 0], info_ref[0, 1])]
+        return [(info_ref[i, 0], info_ref[i, 1]) for i in range(len(steps))]
     me = lax.axis_index("ctx")
     known = [ref[0:1, :][0, 0] for ref in count_refs]
     known.append(tokens * 3 - known[0] - known[1] - known[2])
@@ -492,17 +492,23 @@
     counts = lax.all_gather(shard_counts, "ctx", axis=0, tiled=True)
     info = jnp.stack([jnp.cumsum(counts) - counts, counts], axis=1)
     every = lax.all_gather(kv_rows, "ctx", axis=0)
+    size = 4 if every.shape[0] % 4 == 0 else 1
+    every = every.reshape(-1, size, *kv_rows.shape)
+    info = info.reshape(-1, size, 2)
     ready = make_ready(
         span_starts, kv_scales.T, shard_counts, block_slots[None, :], kv_rows, queries
     )
 
+    def take(some, rows, state=None):
+        return attend([], some, (0,) * size, ready, [rows[i] for i in range(size)], None, state)
+
     def step(carry, turn):
         state, moved = carry
-        rows, one = turn
-        *state, found = attend([], one[None], (0,), ready, [rows], None, state)
+        rows, some = turn
+        *state, found = take(some, rows, state)
         return (tuple(state), moved + found), None
 
-    *state, moved = attend([], info[:1], (0,), ready, [every[0]])
+    *state, moved = take(info[0], every[0])
     (state, moved), _ = lax.scan(step, (tuple(state), moved), (every[1:], info[1:]))
     none = jnp.zeros((kv_rows.shape[0],) * 2, jnp.bfloat16)
     return finish(ready, none, state[0], moved, pair(moved, "rep", 1), kv_rows)

time: 23.8 us -> 23.8 us (level)
  no operation moved by 1% of the time
where the time goes in v6:
time: 23.8 us; the launch traced here: 23.5 us
  Pallas kernels  8.99 us (38%)
  starting transfers between devices  5.92 us (25%)
  local copies, waits for them, and re-layouts  4.14 us (17%)
  waiting for transfers between devices  3.15 us (13%)
  between operations  1.34 us (6%)
    pallas_call x2, Pallas kernels, attend(): pl.pallas_call(functools.partial(attend_kernel, len(counts) if info is No...  6.52 us
    ppermute x7, starting transfers between devices, pair(): return lax.ppermute(value, axis, [(i, i ^ step) for i in range(size)])  5.92 us
    unnamed x10, local copies, waits for them, and re-layouts  4.14 us
    ppermute x7, waiting for transfers between devices, pair(): return lax.ppermute(value, axis, [(i, i ^ step) for i in range(size)])  3.15 us
    pallas_call x1, Pallas kernels, finish(): pl.pallas_call(finish_kernel, out_shape=[jax.ShapeDtypeStruct(result.shap...  1.6 us
    pallas_call x1, Pallas kernels, make_ready(): pl.pallas_call(ready_kernel, out_shape=[jax.ShapeDtypeStruct((8, 128), jn...  0.87 us
  transfers between devices with their start and end apart: 7, of which 3 were waited for; matrix products, arithmetic and copies ran while one was open for 0% of the time, Pallas kernels for 31%

profile of v6, /device:TPU:31, one launch (start us, length us, event | category | flops | bytes accessed | tf_op | source)
XLA Modules:
  0.0 23.5 jit_solution(4320196717469272712)
XLA Ops:
  0.6 0.1 collective-permute-start.3
  0.8 0.2 collective-permute-start.2
  1.6 1.4 %collective-permute-start = (s32[8,128]{1,0:T(8,128)S(1)}, s32[8,128]{1,0:T(8,128)S(1)}, u32[]{:S(2)}, u32[]{:S(2)}) collective-permute-start(s32[8,128]{1,0:T(8,128)S(1)} %broadcast_in_dim.13.refs_0_), channel_id=1, source_target_pairs={{0,4},{4,0},{8,12},{12,8},{1,5},{5,1},{9,13},{13,9},{2,6},{6,2},{1... | collective-permute-start | bytes 12296 | tf_op jit(solution)/shard_map/ppermute | solution.py:472
  3.0 2.3 %collective-permute-start.1 = (s32[8,128]{1,0:T(8,128)S(1)}, s32[8,128]{1,0:T(8,128)S(1)}, u32[]{:S(2)}, u32[]{:S(2)}) collective-permute-start(s32[8,128]{1,0:T(8,128)S(1)} %broadcast_in_dim.13.refs_0_), channel_id=1, source_target_pairs={{0,8},{4,12},{8,0},{12,4},{1,9},{5,13},{9,1},{13,5},{2,10},{6,14},... | collective-permute-start | bytes 12296 | tf_op jit(solution)/shard_map/ppermute | solution.py:472
  5.3 0.0 copy-start
  5.3 1.2 %copy-done = bf16[2,64,4096]{2,1,0:T(8,128)(2,1)S(1)} copy-done((bf16[2,64,4096]{2,1,0:T(8,128)(2,1)S(1)}, bf16[2,64,4096]{2,1,0:T(8,128)(2,1)}, u32[]{:S(2)}) %copy-start) | copy-done | bytes 1048600
  6.5 0.0 copy-start.1
  6.5 0.9 %copy-done.1 = bf16[192,2,256]{2,1,0:T(2,128)(2,1)S(1)} copy-done((bf16[192,2,256]{2,1,0:T(2,128)(2,1)S(1)}, bf16[192,2,256]{2,1,0:T(2,128)(2,1)}, u32[]{:S(2)}) %copy-start.1) | copy-done | bytes 196632
  7.4 0.0 copy-start.2
  7.4 0.7 %copy-done.2 = f32[8,2]{0,1:T(2,128)S(1)} copy-done((f32[8,2]{0,1:T(2,128)S(1)}, f32[8,2]{0,1:T(2,128)}, u32[]{:S(2)}) %copy-start.2) | copy-done | bytes 88
  8.1 0.0 copy-start.3
  8.1 0.7 %copy-done.3 = s32[2]{0:T(128)S(1)} copy-done((s32[2]{0:T(128)S(1)}, s32[2]{0:T(128)}, u32[]{:S(2)}) %copy-start.3) | copy-done | bytes 32
  8.7 0.0 copy-start.4
  8.7 0.7 %copy-done.4 = s32[48]{0:T(128)S(1)} copy-done((s32[48]{0:T(128)S(1)}, s32[48]{0:T(128)}, u32[]{:S(2)}) %copy-start.4) | copy-done | bytes 216
  9.4 0.9 %shard_map.77 = (s32[8,128]{1,0:T(8,128)S(1)}, f32[8,128]{1,0:T(8,128)S(1)}, bf16[256,256]{1,0:T(8,128)(2,1)S(1)}, f32[192,192]{1,0:T(8,128)S(1)}, bf16[192,512]...) custom-call(s32[2]{0:T(128)S(1)} %copy-done.3, f32[2,8]{1,0:T(2,128)S(1)} %bitcast.4, s32[1]{0:T(128)} %copy.8.refs_2_, ...), custom_call_target="tpu_custom_call" | custom-call | flops 50331648 | bytes 2097152 | tf_op jit(solution)/shard_map/pallas_call | solution.py:132
  10.3 2.5 %collective-permute-done.3.refs_9_ = bf16[192,2,256]{2,1,0:T(2,128)(2,1)S(1)} collective-permute-done((bf16[192,2,256]{2,1,0:T(2,128)(2,1)}, bf16[192,2,256]{2,1,0:T(2,128)(2,1)S(1)}, u32[]{:S(2)}, u32[]{:S(2)}) %collective-permute-start.3) | collective-permute-done | bytes 196640 | tf_op jit(solution)/shard_map/ppermute | solution.py:472
  12.8 0.0 collective-permute-start.4
  12.8 0.0 collective-permute-done.refs_1_
  12.8 0.1 collective-permute-done.1.refs_2_
  12.9 0.0 collective-permute-done.2.refs_8_
  12.9 4.7 %shard_map.78 = (bf16[2,64,4096]{2,1,0:T(8,128)(2,1)S(1)}, f32[2,2,1024,128]{3,2,1,0:T(8,128)S(1)}, bf16[192,512]{1,0:T(8,128)(2,1)S(1)}, bf16[192,192]{1,0:T(8,128)(2,1)S(1)}) custom-call(s32[8,128]{1,0:T(8,128)S(1)} %broadcast_in_dim.13.refs_0_, s32[8,128]{1,0:T(8,128)S(1)} %collective-permute-done.refs_1_, s32[8,128]{1,0:T(8,128)S(1)} %collective-permute-done.1.refs_2_, ...), custom_call_target="tpu_custom_call" | custom-call | flops 2415919104 | bytes 4194304 | tf_op jit(solution)/shard_map/pallas_call | solution.py:373
  17.6 0.6 %collective-permute-start.5 = (bf16[192,512]{1,0:T(8,128)(2,1)S(1)}, bf16[192,512]{1,0:T(8,128)(2,1)S(1)}, u32[]{:S(2)}, u32[]{:S(2)}) collective-permute-start(bf16[192,512]{1,0:T(8,128)(2,1)S(1)} %get-tuple-element.23.refs_11_), channel_id=1, source_target_pairs={{0,1},{1,0},{2,3},{3,2},{4,5},{5,4},{6,7},{7,6},{8,9},{9,8},{10,11... | collective-permute-start | bytes 589832 | tf_op jit(solution)/shard_map/ppermute | solution.py:472
  18.1 0.6 %collective-permute-done.4.refs_7_ = bf16[192,2,256]{2,1,0:T(2,128)(2,1)S(1)} collective-permute-done((bf16[192,2,256]{2,1,0:T(2,128)(2,1)S(1)}, bf16[192,2,256]{2,1,0:T(2,128)(2,1)S(1)}, u32[]{:S(2)}, u32[]{:S(2)}) %collective-permute-start.4) | collective-permute-done | bytes 196640 | tf_op jit(solution)/shard_map/ppermute | solution.py:472
  18.7 1.4 %collective-permute-start.6 = (bf16[192,2,256]{2,1,0:T(2,128)(2,1)S(1)}, bf16[192,2,256]{2,1,0:T(2,128)(2,1)S(1)}, u32[]{:S(2)}, u32[]{:S(2)}) collective-permute-start(bf16[192,2,256]{2,1,0:T(2,128)(2,1)S(1)} %collective-permute-done.4.refs_7_), channel_id=1, source_target_pairs={{0,1},{1,0},{2,3},{3,2},{4,5},{5,4},{6,7},{7,6},{8,9},{9,8},{10,11... | collective-permute-start | bytes 589832 | tf_op jit(solution)/shard_map/ppermute | solution.py:472
  20.1 1.8 %shard_map.79 = (bf16[2,64,4096]{2,1,0:T(8,128)(2,1)S(1)}, bf16[192,512]{1,0:T(8,128)(2,1)S(1)}) custom-call(s32[8,128]{1,0:T(8,128)S(1)} %broadcast_in_dim.13.refs_0_, s32[8,128]{1,0:T(8,128)S(1)} %collective-permute-done.refs_1_, s32[8,128]{1,0:T(8,128)S(1)} %collective-permute-done.1.refs_2_, s32[8,128]{1,0:T(8,128)S(1)} %get-tuple-element.16.refs_3_, ...), custom_call_target="tpu_custom_call" | custom-call | flops 805306368 | bytes 4194304 | tf_op jit(solution)/shard_map/pallas_call | solution.py:373
  21.9 0.0 collective-permute-done.5.other
  21.9 0.0 collective-permute-done.6.other_rows
  21.9 1.6 %shard_map.80 = (bf16[2,64,4096]{2,1,0:T(8,128)(2,1)}, f32[192,4,256]{2,1,0:T(4,128)}) custom-call(f32[8,128]{1,0:T(8,128)S(1)} %get-tuple-element.14.refs_4_.floats_ref, bf16[256,256]{1,0:T(8,128)(2,1)S(1)} %get-tuple-element.15.refs_5_.signs_ref, bf16[192,192]{1,0:T(8,128)(2,1)S(1)} %get-tuple-element.20.refs_10_.pick_ref, ...), custom_call_target="tpu_custom_call" | custom-call | flops 75497472 | bytes 2097152 | tf_op jit(solution)/shard_map/pallas_call | solution.py:450
  (1 shorter events, 0.0 us)
Async XLA Ops:
  0.6 12.1 %collective-permute-start.3 = (bf16[192,2,256]{2,1,0:T(2,128)(2,1)}, bf16[192,2,256]{2,1,0:T(2,128)(2,1)S(1)}, u32[]{:S(2)}, u32[]{:S(2)}) collective-permute-start(bf16[192,2,256]{2,1,0:T(2,128)(2,1)} %refs_4_.1), channel_id=1, source_target_pairs={{0,8},{4,12},{8,0},{12,4},{1,9},{5,13},{9,1},{13,5},{2,10},{6,14},... | collective-permute-start | bytes 589832 | tf_op jit(solution)/shard_map/ppermute | solution.py:472
  0.8 12.1 %collective-permute-start.2 = (bf16[192,2,256]{2,1,0:T(2,128)(2,1)}, bf16[192,2,256]{2,1,0:T(2,128)(2,1)S(1)}, u32[]{:S(2)}, u32[]{:S(2)}) collective-permute-start(bf16[192,2,256]{2,1,0:T(2,128)(2,1)} %refs_4_.1), channel_id=1, source_target_pairs={{0,4},{4,0},{8,12},{12,8},{1,5},{5,1},{9,13},{13,9},{2,6},{6,2},{1... | collective-permute-start | bytes 589832 | tf_op jit(solution)/shard_map/ppermute | solution.py:472
  1.6 11.2 %collective-permute-start = (s32[8,128]{1,0:T(8,128)S(1)}, s32[8,128]{1,0:T(8,128)S(1)}, u32[]{:S(2)}, u32[]{:S(2)}) collective-permute-start(s32[8,128]{1,0:T(8,128)S(1)} %broadcast_in_dim.13.refs_0_), channel_id=1, source_target_pairs={{0,4},{4,0},{8,12},{12,8},{1,5},{5,1},{9,13},{13,9},{2,6},{6,2},{1... | collective-permute-start | bytes 12296 | tf_op jit(solution)/shard_map/ppermute | solution.py:472
  3.0 9.9 %collective-permute-start.1 = (s32[8,128]{1,0:T(8,128)S(1)}, s32[8,128]{1,0:T(8,128)S(1)}, u32[]{:S(2)}, u32[]{:S(2)}) collective-permute-start(s32[8,128]{1,0:T(8,128)S(1)} %broadcast_in_dim.13.refs_0_), channel_id=1, source_target_pairs={{0,8},{4,12},{8,0},{12,4},{1,9},{5,13},{9,1},{13,5},{2,10},{6,14},... | collective-permute-start | bytes 12296 | tf_op jit(solution)/shard_map/ppermute | solution.py:472
  5.3 1.2 %copy-start = (bf16[2,64,4096]{2,1,0:T(8,128)(2,1)S(1)}, bf16[2,64,4096]{2,1,0:T(8,128)(2,1)}, u32[]{:S(2)}) copy-start(bf16[2,64,4096]{2,1,0:T(8,128)(2,1)} %refs_5_.1) | copy-start | bytes 3145732
  6.5 0.9 %copy-start.1 = (bf16[192,2,256]{2,1,0:T(2,128)(2,1)S(1)}, bf16[192,2,256]{2,1,0:T(2,128)(2,1)}, u32[]{:S(2)}) copy-start(bf16[192,2,256]{2,1,0:T(2,128)(2,1)} %refs_4_.1) | copy-start | bytes 589828
  7.4 0.7 %copy-start.2 = (f32[8,2]{0,1:T(2,128)S(1)}, f32[8,2]{0,1:T(2,128)}, u32[]{:S(2)}) copy-start(f32[8,2]{0,1:T(2,128)} %param.7) | copy-start | bytes 196
  8.1 0.7 %copy-start.3 = (s32[2]{0:T(128)S(1)}, s32[2]{0:T(128)}, u32[]{:S(2)}) copy-start(s32[2]{0:T(128)} %refs_0_.1) | copy-start | bytes 28
  8.7 0.7 %copy-start.4 = (s32[48]{0:T(128)S(1)}, s32[48]{0:T(128)}, u32[]{:S(2)}) copy-start(s32[48]{0:T(128)} %param.11) | copy-start | bytes 580
  12.8 5.9 %collective-permute-start.4 = (bf16[192,2,256]{2,1,0:T(2,128)(2,1)S(1)}, bf16[192,2,256]{2,1,0:T(2,128)(2,1)S(1)}, u32[]{:S(2)}, u32[]{:S(2)}) collective-permute-start(bf16[192,2,256]{2,1,0:T(2,128)(2,1)S(1)} %collective-permute-done.3.refs_9_), channel_id=1, source_target_pairs={{0,4},{4,0},{8,12},{12,8},{1,5},{5,1},{9,13},{13,9},{2,6},{6,2},{1... | collective-permute-start | bytes 589832 | tf_op jit(solution)/shard_map/ppermute | solution.py:472
  17.6 4.3 %collective-permute-start.5 = (bf16[192,512]{1,0:T(8,128)(2,1)S(1)}, bf16[192,512]{1,0:T(8,128)(2,1)S(1)}, u32[]{:S(2)}, u32[]{:S(2)}) collective-permute-start(bf16[192,512]{1,0:T(8,128)(2,1)S(1)} %get-tuple-element.23.refs_11_), channel_id=1, source_target_pairs={{0,1},{1,0},{2,3},{3,2},{4,5},{5,4},{6,7},{7,6},{8,9},{9,8},{10,11... | collective-permute-start | bytes 589832 | tf_op jit(solution)/shard_map/ppermute | solution.py:472
  18.7 3.2 %collective-permute-start.6 = (bf16[192,2,256]{2,1,0:T(2,128)(2,1)S(1)}, bf16[192,2,256]{2,1,0:T(2,128)(2,1)S(1)}, u32[]{:S(2)}, u32[]{:S(2)}) collective-permute-start(bf16[192,2,256]{2,1,0:T(2,128)(2,1)S(1)} %collective-permute-done.4.refs_7_), channel_id=1, source_target_pairs={{0,1},{1,0},{2,3},{3,2},{4,5},{5,4},{6,7},{7,6},{8,9},{9,8},{10,11... | collective-permute-start | bytes 589832 | tf_op jit(solution)/shard_map/ppermute | solution.py:472

commit v7 on v6

--- a/solution.py
+++ b/solution.py
@@ -202,6 +202,18 @@
         keys = [joined(j, 0) for j in range(heads)]
         ones = jnp.ones((shards * tokens, half), jnp.bfloat16)
         values = [jnp.concatenate([joined(j, 1), ones], axis=1) for j in range(heads)]
+        if not last:
+            row = lax.broadcasted_iota(jnp.int32, (rows, tokens), 0)
+            key = lax.broadcasted_iota(jnp.int32, (rows, tokens), 1)
+            biases = []
+            for c in range(sets):
+                parts = []
+                for offset, count in spans:
+                    counted = (key < count) & (key + (offset - bases[c]) <= row)
+                    parts.append(jnp.where(counted, 0.0, MASKED))
+                bias = jnp.concatenate(parts, axis=1) if shards > 1 else parts[0]
+                biases.append(jnp.concatenate([bias] * group, axis=0))
+            return [keys] * sets, values, biases
         row = lax.broadcasted_iota(jnp.int32, (tokens, half), 1)
         key = lax.broadcasted_iota(jnp.int32, (tokens, half), 0)
         masked_keys = []
@@ -227,10 +239,12 @@
             ],
             axis=0,
         )
-        stacked = jnp.concatenate([stacked, units], axis=1)
-        return lax.dot_general(
+        if last:
+            stacked = jnp.concatenate([stacked, units], axis=1)
+        scores = lax.dot_general(
             stacked, keys[c][j], (((1,), (1,)), ((), ())), preferred_element_type=jnp.float32
         )
+        return scores if last else scores + units[c]
 
     def tiles(scores):
         for i in range(0, scores.shape[1], half):
@@ -405,6 +419,7 @@
         copy.start()
     scales = [scale_reader(floats_ref, side, heads) for side in range(2)]
     found = codes_of(other_rows, scales[1], signs_ref[...], rot_scr)
+    both = jnp.concatenate([part for parts in found for part in parts], axis=1)
     pick = pick_ref[...]
     pieces = []
     start = 0
@@ -426,14 +441,14 @@
             for here, piece in pieces:
                 for side, moved in enumerate((own, other)):
                     first = (side if turn == 0 else 1 - side) * heads
+                    if side == 1:
+                        added = jnp.dot(pick[here], both, preferred_element_type=jnp.float32)
                     for j in range(heads):
                         for w in range(2):
                             cols = slice((2 * j + w) * half, (2 * j + w + 1) * half)
                             part = moved[here, cols].astype(jnp.float32)
                             if side == 1:
-                                part = part + jnp.dot(
-                                    pick[here], found[j][w], preferred_element_type=jnp.float32
-                                )
+                                part = part + added[:, cols]
                             part = part * scales[side](j, w)
                             cache_scr[here, first + j, w * half : (w + 1) * half] = part
                 piece.start()

time: 23.8 us -> 23.7 us (level)
  Pallas kernels: 8.99 us -> 8.63 us
  waiting for transfers between devices: 3.15 us -> 3.49 us
    pallas_call x2, Pallas kernels: 6.52 us -> 6.17 us  [attend(): pl.pallas_call(functools.partial(attend_kernel, len(counts) if info is No...]
    ppermute x7, waiting for transfers between devices: 3.15 us -> 3.49 us  [pair(): return lax.ppermute(value, axis, [(i, i ^ step) for i in range(size)])]
  transfers between devices with their start and end apart: 7 -> 7, of which waited for: 3 -> 3; matrix products, arithmetic and copies ran while one was open for 0% -> 0% of each run, Pallas kernels for 31% -> 30%
where the time goes in v7:
time: 23.7 us; the launch traced here: 23.5 us
  Pallas kernels  8.63 us (36%)
  starting transfers between devices  5.92 us (25%)
  local copies, waits for them, and re-layouts  4.14 us (17%)
  waiting for transfers between devices  3.49 us (15%)
  between operations  1.34 us (6%)
    pallas_call x2, Pallas kernels, attend(): pl.pallas_call(functools.partial(attend_kernel, len(counts) if info is No...  6.17 us
    ppermute x7, starting transfers between devices, pair(): return lax.ppermute(value, axis, [(i, i ^ step) for i in range(size)])  5.92 us
    unnamed x10, local copies, waits for them, and re-layouts  4.14 us
    ppermute x7, waiting for transfers between devices, pair(): return lax.ppermute(value, axis, [(i, i ^ step) for i in range(size)])  3.49 us
    pallas_call x1, Pallas kernels, finish(): pl.pallas_call(finish_kernel, out_shape=[jax.ShapeDtypeStruct(result.shap...  1.59 us
    pallas_call x1, Pallas kernels, make_ready(): pl.pallas_call(ready_kernel, out_shape=[jax.ShapeDtypeStruct((8, 128), jn...  0.87 us
  transfers between devices with their start and end apart: 7, of which 3 were waited for; matrix products, arithmetic and copies ran while one was open for 0% of the time, Pallas kernels for 30%

profile of v7, /device:TPU:31, one launch (start us, length us, event | category | flops | bytes accessed | tf_op | source)
XLA Modules:
  0.0 23.5 jit_solution(3948563433121389860)
XLA Ops:
  0.6 0.1 collective-permute-start.3
  0.8 0.2 collective-permute-start.2
  1.6 1.4 %collective-permute-start = (s32[8,128]{1,0:T(8,128)S(1)}, s32[8,128]{1,0:T(8,128)S(1)}, u32[]{:S(2)}, u32[]{:S(2)}) collective-permute-start(s32[8,128]{1,0:T(8,128)S(1)} %broadcast_in_dim.13.refs_0_), channel_id=1, source_target_pairs={{0,4},{4,0},{8,12},{12,8},{1,5},{5,1},{9,13},{13,9},{2,6},{6,2},{1... | collective-permute-start | bytes 12296 | tf_op jit(solution)/shard_map/ppermute | solution.py:487
  3.0 2.3 %collective-permute-start.1 = (s32[8,128]{1,0:T(8,128)S(1)}, s32[8,128]{1,0:T(8,128)S(1)}, u32[]{:S(2)}, u32[]{:S(2)}) collective-permute-start(s32[8,128]{1,0:T(8,128)S(1)} %broadcast_in_dim.13.refs_0_), channel_id=1, source_target_pairs={{0,8},{4,12},{8,0},{12,4},{1,9},{5,13},{9,1},{13,5},{2,10},{6,14},... | collective-permute-start | bytes 12296 | tf_op jit(solution)/shard_map/ppermute | solution.py:487
  5.3 0.0 copy-start
  5.3 1.2 %copy-done = bf16[2,64,4096]{2,1,0:T(8,128)(2,1)S(1)} copy-done((bf16[2,64,4096]{2,1,0:T(8,128)(2,1)S(1)}, bf16[2,64,4096]{2,1,0:T(8,128)(2,1)}, u32[]{:S(2)}) %copy-start) | copy-done | bytes 1048600
  6.5 0.0 copy-start.1
  6.5 0.9 %copy-done.1 = bf16[192,2,256]{2,1,0:T(2,128)(2,1)S(1)} copy-done((bf16[192,2,256]{2,1,0:T(2,128)(2,1)S(1)}, bf16[192,2,256]{2,1,0:T(2,128)(2,1)}, u32[]{:S(2)}) %copy-start.1) | copy-done | bytes 196632
  7.4 0.0 copy-start.2
  7.4 0.7 %copy-done.2 = f32[8,2]{0,1:T(2,128)S(1)} copy-done((f32[8,2]{0,1:T(2,128)S(1)}, f32[8,2]{0,1:T(2,128)}, u32[]{:S(2)}) %copy-start.2) | copy-done | bytes 88
  8.1 0.0 copy-start.3
  8.1 0.7 %copy-done.3 = s32[2]{0:T(128)S(1)} copy-done((s32[2]{0:T(128)S(1)}, s32[2]{0:T(128)}, u32[]{:S(2)}) %copy-start.3) | copy-done | bytes 32
  8.7 0.0 copy-start.4
  8.7 0.7 %copy-done.4 = s32[48]{0:T(128)S(1)} copy-done((s32[48]{0:T(128)S(1)}, s32[48]{0:T(128)}, u32[]{:S(2)}) %copy-start.4) | copy-done | bytes 216
  9.4 0.9 %shard_map.77 = (s32[8,128]{1,0:T(8,128)S(1)}, f32[8,128]{1,0:T(8,128)S(1)}, bf16[256,256]{1,0:T(8,128)(2,1)S(1)}, f32[192,192]{1,0:T(8,128)S(1)}, bf16[192,512]...) custom-call(s32[2]{0:T(128)S(1)} %copy-done.3, f32[2,8]{1,0:T(2,128)S(1)} %bitcast.4, s32[1]{0:T(128)} %copy.8.refs_2_, ...), custom_call_target="tpu_custom_call" | custom-call | flops 50331648 | bytes 2097152 | tf_op jit(solution)/shard_map/pallas_call | solution.py:132
  10.3 2.5 %collective-permute-done.3.refs_9_ = bf16[192,2,256]{2,1,0:T(2,128)(2,1)S(1)} collective-permute-done((bf16[192,2,256]{2,1,0:T(2,128)(2,1)}, bf16[192,2,256]{2,1,0:T(2,128)(2,1)S(1)}, u32[]{:S(2)}, u32[]{:S(2)}) %collective-permute-start.3) | collective-permute-done | bytes 196640 | tf_op jit(solution)/shard_map/ppermute | solution.py:487
  12.8 0.0 collective-permute-start.4
  12.8 0.0 collective-permute-done.refs_1_
  12.8 0.1 collective-permute-done.1.refs_2_
  12.9 0.0 collective-permute-done.2.refs_8_
  12.9 4.4 %shard_map.78 = (bf16[2,64,4096]{2,1,0:T(8,128)(2,1)S(1)}, f32[2,2,1024,128]{3,2,1,0:T(8,128)S(1)}, bf16[192,512]{1,0:T(8,128)(2,1)S(1)}, bf16[192,192]{1,0:T(8,128)(2,1)S(1)}) custom-call(s32[8,128]{1,0:T(8,128)S(1)} %broadcast_in_dim.13.refs_0_, s32[8,128]{1,0:T(8,128)S(1)} %collective-permute-done.refs_1_, s32[8,128]{1,0:T(8,128)S(1)} %collective-permute-done.1.refs_2_, ...), custom_call_target="tpu_custom_call" | custom-call | flops 2415919104 | bytes 4194304 | tf_op jit(solution)/shard_map/pallas_call | solution.py:387
  17.2 0.6 %collective-permute-start.5 = (bf16[192,512]{1,0:T(8,128)(2,1)S(1)}, bf16[192,512]{1,0:T(8,128)(2,1)S(1)}, u32[]{:S(2)}, u32[]{:S(2)}) collective-permute-start(bf16[192,512]{1,0:T(8,128)(2,1)S(1)} %get-tuple-element.23.refs_11_), channel_id=1, source_target_pairs={{0,1},{1,0},{2,3},{3,2},{4,5},{5,4},{6,7},{7,6},{8,9},{9,8},{10,11... | collective-permute-start | bytes 589832 | tf_op jit(solution)/shard_map/ppermute | solution.py:487
  17.8 0.9 %collective-permute-done.4.refs_7_ = bf16[192,2,256]{2,1,0:T(2,128)(2,1)S(1)} collective-permute-done((bf16[192,2,256]{2,1,0:T(2,128)(2,1)S(1)}, bf16[192,2,256]{2,1,0:T(2,128)(2,1)S(1)}, u32[]{:S(2)}, u32[]{:S(2)}) %collective-permute-start.4) | collective-permute-done | bytes 196640 | tf_op jit(solution)/shard_map/ppermute | solution.py:487
  18.7 1.4 %collective-permute-start.6 = (bf16[192,2,256]{2,1,0:T(2,128)(2,1)S(1)}, bf16[192,2,256]{2,1,0:T(2,128)(2,1)S(1)}, u32[]{:S(2)}, u32[]{:S(2)}) collective-permute-start(bf16[192,2,256]{2,1,0:T(2,128)(2,1)S(1)} %collective-permute-done.4.refs_7_), channel_id=1, source_target_pairs={{0,1},{1,0},{2,3},{3,2},{4,5},{5,4},{6,7},{7,6},{8,9},{9,8},{10,11... | collective-permute-start | bytes 589832 | tf_op jit(solution)/shard_map/ppermute | solution.py:487
  20.1 1.8 %shard_map.79 = (bf16[2,64,4096]{2,1,0:T(8,128)(2,1)S(1)}, bf16[192,512]{1,0:T(8,128)(2,1)S(1)}) custom-call(s32[8,128]{1,0:T(8,128)S(1)} %broadcast_in_dim.13.refs_0_, s32[8,128]{1,0:T(8,128)S(1)} %collective-permute-done.refs_1_, s32[8,128]{1,0:T(8,128)S(1)} %collective-permute-done.1.refs_2_, s32[8,128]{1,0:T(8,128)S(1)} %get-tuple-element.16.refs_3_, ...), custom_call_target="tpu_custom_call" | custom-call | flops 805306368 | bytes 4194304 | tf_op jit(solution)/shard_map/pallas_call | solution.py:387
  21.9 0.0 collective-permute-done.5.other
  21.9 0.0 collective-permute-done.6.other_rows
  21.9 1.6 %shard_map.80 = (bf16[2,64,4096]{2,1,0:T(8,128)(2,1)}, f32[192,4,256]{2,1,0:T(4,128)}) custom-call(f32[8,128]{1,0:T(8,128)S(1)} %get-tuple-element.14.refs_4_.floats_ref, bf16[256,256]{1,0:T(8,128)(2,1)S(1)} %get-tuple-element.15.refs_5_.signs_ref, bf16[192,192]{1,0:T(8,128)(2,1)S(1)} %get-tuple-element.20.refs_10_.pick_ref, ...), custom_call_target="tpu_custom_call" | custom-call | flops 75497472 | bytes 2097152 | tf_op jit(solution)/shard_map/pallas_call | solution.py:465
  (1 shorter events, 0.0 us)
Async XLA Ops:
  0.6 12.1 %collective-permute-start.3 = (bf16[192,2,256]{2,1,0:T(2,128)(2,1)}, bf16[192,2,256]{2,1,0:T(2,128)(2,1)S(1)}, u32[]{:S(2)}, u32[]{:S(2)}) collective-permute-start(bf16[192,2,256]{2,1,0:T(2,128)(2,1)} %refs_4_.1), channel_id=1, source_target_pairs={{0,8},{4,12},{8,0},{12,4},{1,9},{5,13},{9,1},{13,5},{2,10},{6,14},... | collective-permute-start | bytes 589832 | tf_op jit(solution)/shard_map/ppermute | solution.py:487
  0.8 12.1 %collective-permute-start.2 = (bf16[192,2,256]{2,1,0:T(2,128)(2,1)}, bf16[192,2,256]{2,1,0:T(2,128)(2,1)S(1)}, u32[]{:S(2)}, u32[]{:S(2)}) collective-permute-start(bf16[192,2,256]{2,1,0:T(2,128)(2,1)} %refs_4_.1), channel_id=1, source_target_pairs={{0,4},{4,0},{8,12},{12,8},{1,5},{5,1},{9,13},{13,9},{2,6},{6,2},{1... | collective-permute-start | bytes 589832 | tf_op jit(solution)/shard_map/ppermute | solution.py:487
  1.6 11.2 %collective-permute-start = (s32[8,128]{1,0:T(8,128)S(1)}, s32[8,128]{1,0:T(8,128)S(1)}, u32[]{:S(2)}, u32[]{:S(2)}) collective-permute-start(s32[8,128]{1,0:T(8,128)S(1)} %broadcast_in_dim.13.refs_0_), channel_id=1, source_target_pairs={{0,4},{4,0},{8,12},{12,8},{1,5},{5,1},{9,13},{13,9},{2,6},{6,2},{1... | collective-permute-start | bytes 12296 | tf_op jit(solution)/shard_map/ppermute | solution.py:487
  3.0 9.9 %collective-permute-start.1 = (s32[8,128]{1,0:T(8,128)S(1)}, s32[8,128]{1,0:T(8,128)S(1)}, u32[]{:S(2)}, u32[]{:S(2)}) collective-permute-start(s32[8,128]{1,0:T(8,128)S(1)} %broadcast_in_dim.13.refs_0_), channel_id=1, source_target_pairs={{0,8},{4,12},{8,0},{12,4},{1,9},{5,13},{9,1},{13,5},{2,10},{6,14},... | collective-permute-start | bytes 12296 | tf_op jit(solution)/shard_map/ppermute | solution.py:487
  5.3 1.2 %copy-start = (bf16[2,64,4096]{2,1,0:T(8,128)(2,1)S(1)}, bf16[2,64,4096]{2,1,0:T(8,128)(2,1)}, u32[]{:S(2)}) copy-start(bf16[2,64,4096]{2,1,0:T(8,128)(2,1)} %refs_5_.1) | copy-start | bytes 3145732
  6.5 0.9 %copy-start.1 = (bf16[192,2,256]{2,1,0:T(2,128)(2,1)S(1)}, bf16[192,2,256]{2,1,0:T(2,128)(2,1)}, u32[]{:S(2)}) copy-start(bf16[192,2,256]{2,1,0:T(2,128)(2,1)} %refs_4_.1) | copy-start | bytes 589828
  7.4 0.7 %copy-start.2 = (f32[8,2]{0,1:T(2,128)S(1)}, f32[8,2]{0,1:T(2,128)}, u32[]{:S(2)}) copy-start(f32[8,2]{0,1:T(2,128)} %param.7) | copy-start | bytes 196
  8.1 0.7 %copy-start.3 = (s32[2]{0:T(128)S(1)}, s32[2]{0:T(128)}, u32[]{:S(2)}) copy-start(s32[2]{0:T(128)} %refs_0_.1) | copy-start | bytes 28
  8.7 0.7 %copy-start.4 = (s32[48]{0:T(128)S(1)}, s32[48]{0:T(128)}, u32[]{:S(2)}) copy-start(s32[48]{0:T(128)} %param.11) | copy-start | bytes 580
  12.8 5.9 %collective-permute-start.4 = (bf16[192,2,256]{2,1,0:T(2,128)(2,1)S(1)}, bf16[192,2,256]{2,1,0:T(2,128)(2,1)S(1)}, u32[]{:S(2)}, u32[]{:S(2)}) collective-permute-start(bf16[192,2,256]{2,1,0:T(2,128)(2,1)S(1)} %collective-permute-done.3.refs_9_), channel_id=1, source_target_pairs={{0,4},{4,0},{8,12},{12,8},{1,5},{5,1},{9,13},{13,9},{2,6},{6,2},{1... | collective-permute-start | bytes 589832 | tf_op jit(solution)/shard_map/ppermute | solution.py:487
  17.2 4.7 %collective-permute-start.5 = (bf16[192,512]{1,0:T(8,128)(2,1)S(1)}, bf16[192,512]{1,0:T(8,128)(2,1)S(1)}, u32[]{:S(2)}, u32[]{:S(2)}) collective-permute-start(bf16[192,512]{1,0:T(8,128)(2,1)S(1)} %get-tuple-element.23.refs_11_), channel_id=1, source_target_pairs={{0,1},{1,0},{2,3},{3,2},{4,5},{5,4},{6,7},{7,6},{8,9},{9,8},{10,11... | collective-permute-start | bytes 589832 | tf_op jit(solution)/shard_map/ppermute | solution.py:487
  18.7 3.2 %collective-permute-start.6 = (bf16[192,2,256]{2,1,0:T(2,128)(2,1)S(1)}, bf16[192,2,256]{2,1,0:T(2,128)(2,1)S(1)}, u32[]{:S(2)}, u32[]{:S(2)}) collective-permute-start(bf16[192,2,256]{2,1,0:T(2,128)(2,1)S(1)} %collective-permute-done.4.refs_7_), channel_id=1, source_target_pairs={{0,1},{1,0},{2,3},{3,2},{4,5},{5,4},{6,7},{7,6},{8,9},{9,8},{10,11... | collective-permute-start | bytes 589832 | tf_op jit(solution)/shard_map/ppermute | solution.py:487

commit v8 on v7

--- a/solution.py
+++ b/solution.py
@@ -267,7 +267,9 @@
                 )
                 total = weighted[:, half:]
                 worst = jnp.maximum(worst, jnp.max(total.reshape(stack // 8, 8, half), axis=0))
-                share = 1.0 / (total + 1.0)
+                total = total + 1.0
+                share = pl.reciprocal(total, approx=True)
+                share = share * (2.0 - total * share)
                 for g in range(group):
                     one = slice(g * rows, (g + 1) * rows)
                     cols = slice((j * group + g) * half, (j * group + g + 1) * half)

time: 23.7 us -> 24 us (1.013)
  transfers between devices with their start and end apart: 7 -> 7, of which waited for: 3 -> 3; matrix products, arithmetic and copies ran while one was open for 0% -> 0% of each run, Pallas kernels for 30% -> 31%
where the time goes in v8:
time: 24 us; the launch traced here: 23.7 us
  Pallas kernels  8.84 us (37%)
  starting transfers between devices  5.92 us (25%)
  local copies, waits for them, and re-layouts  4.14 us (17%)
  waiting for transfers between devices  3.49 us (15%)
  between operations  1.34 us (6%)
    pallas_call x2, Pallas kernels, attend(): pl.pallas_call(functools.partial(attend_kernel, len(counts) if info is No...  6.38 us
    ppermute x7, starting transfers between devices, pair(): return lax.ppermute(value, axis, [(i, i ^ step) for i in range(size)])  5.92 us
    unnamed x10, local copies, waits for them, and re-layouts  4.14 us
    ppermute x7, waiting for transfers between devices, pair(): return lax.ppermute(value, axis, [(i, i ^ step) for i in range(size)])  3.49 us
    pallas_call x1, Pallas kernels, finish(): pl.pallas_call(finish_kernel, out_shape=[jax.ShapeDtypeStruct(result.shap...  1.59 us
    pallas_call x1, Pallas kernels, make_ready(): pl.pallas_call(ready_kernel, out_shape=[jax.ShapeDtypeStruct((8, 128), jn...  0.87 us
  transfers between devices with their start and end apart: 7, of which 3 were waited for; matrix products, arithmetic and copies ran while one was open for 0% of the time, Pallas kernels for 31%

profile of v8, /device:TPU:31, one launch (start us, length us, event | category | flops | bytes accessed | tf_op | source)
XLA Modules:
  0.0 23.7 jit_solution(12351593134305966448)
XLA Ops:
  0.6 0.1 collective-permute-start.3
  0.8 0.2 collective-permute-start.2
  1.6 1.4 %collective-permute-start = (s32[8,128]{1,0:T(8,128)S(1)}, s32[8,128]{1,0:T(8,128)S(1)}, u32[]{:S(2)}, u32[]{:S(2)}) collective-permute-start(s32[8,128]{1,0:T(8,128)S(1)} %broadcast_in_dim.13.refs_0_), channel_id=1, source_target_pairs={{0,4},{4,0},{8,12},{12,8},{1,5},{5,1},{9,13},{13,9},{2,6},{6,2},{1... | collective-permute-start | bytes 12296 | tf_op jit(solution)/shard_map/ppermute | solution.py:489
  3.0 2.3 %collective-permute-start.1 = (s32[8,128]{1,0:T(8,128)S(1)}, s32[8,128]{1,0:T(8,128)S(1)}, u32[]{:S(2)}, u32[]{:S(2)}) collective-permute-start(s32[8,128]{1,0:T(8,128)S(1)} %broadcast_in_dim.13.refs_0_), channel_id=1, source_target_pairs={{0,8},{4,12},{8,0},{12,4},{1,9},{5,13},{9,1},{13,5},{2,10},{6,14},... | collective-permute-start | bytes 12296 | tf_op jit(solution)/shard_map/ppermute | solution.py:489
  5.3 0.0 copy-start
  5.3 1.2 %copy-done = bf16[2,64,4096]{2,1,0:T(8,128)(2,1)S(1)} copy-done((bf16[2,64,4096]{2,1,0:T(8,128)(2,1)S(1)}, bf16[2,64,4096]{2,1,0:T(8,128)(2,1)}, u32[]{:S(2)}) %copy-start) | copy-done | bytes 1048600
  6.5 0.0 copy-start.1
  6.5 0.9 %copy-done.1 = bf16[192,2,256]{2,1,0:T(2,128)(2,1)S(1)} copy-done((bf16[192,2,256]{2,1,0:T(2,128)(2,1)S(1)}, bf16[192,2,256]{2,1,0:T(2,128)(2,1)}, u32[]{:S(2)}) %copy-start.1) | copy-done | bytes 196632
  7.4 0.0 copy-start.2
  7.4 0.7 %copy-done.2 = f32[8,2]{0,1:T(2,128)S(1)} copy-done((f32[8,2]{0,1:T(2,128)S(1)}, f32[8,2]{0,1:T(2,128)}, u32[]{:S(2)}) %copy-start.2) | copy-done | bytes 88
  8.1 0.0 copy-start.3
  8.1 0.7 %copy-done.3 = s32[2]{0:T(128)S(1)} copy-done((s32[2]{0:T(128)S(1)}, s32[2]{0:T(128)}, u32[]{:S(2)}) %copy-start.3) | copy-done | bytes 32
  8.7 0.0 copy-start.4
  8.7 0.7 %copy-done.4 = s32[48]{0:T(128)S(1)} copy-done((s32[48]{0:T(128)S(1)}, s32[48]{0:T(128)}, u32[]{:S(2)}) %copy-start.4) | copy-done | bytes 216
  9.4 0.9 %shard_map.77 = (s32[8,128]{1,0:T(8,128)S(1)}, f32[8,128]{1,0:T(8,128)S(1)}, bf16[256,256]{1,0:T(8,128)(2,1)S(1)}, f32[192,192]{1,0:T(8,128)S(1)}, bf16[192,512]...) custom-call(s32[2]{0:T(128)S(1)} %copy-done.3, f32[2,8]{1,0:T(2,128)S(1)} %bitcast.4, s32[1]{0:T(128)} %copy.8.refs_2_, ...), custom_call_target="tpu_custom_call" | custom-call | flops 50331648 | bytes 2097152 | tf_op jit(solution)/shard_map/pallas_call | solution.py:132
  10.3 2.5 %collective-permute-done.3.refs_9_ = bf16[192,2,256]{2,1,0:T(2,128)(2,1)S(1)} collective-permute-done((bf16[192,2,256]{2,1,0:T(2,128)(2,1)}, bf16[192,2,256]{2,1,0:T(2,128)(2,1)S(1)}, u32[]{:S(2)}, u32[]{:S(2)}) %collective-permute-start.3) | collective-permute-done | bytes 196640 | tf_op jit(solution)/shard_map/ppermute | solution.py:489
  12.8 0.0 collective-permute-start.4
  12.8 0.0 collective-permute-done.refs_1_
  12.8 0.1 collective-permute-done.1.refs_2_
  12.9 0.0 collective-permute-done.2.refs_8_
  12.9 4.4 %shard_map.78 = (bf16[2,64,4096]{2,1,0:T(8,128)(2,1)S(1)}, f32[2,2,1024,128]{3,2,1,0:T(8,128)S(1)}, bf16[192,512]{1,0:T(8,128)(2,1)S(1)}, bf16[192,192]{1,0:T(8,128)(2,1)S(1)}) custom-call(s32[8,128]{1,0:T(8,128)S(1)} %broadcast_in_dim.13.refs_0_, s32[8,128]{1,0:T(8,128)S(1)} %collective-permute-done.refs_1_, s32[8,128]{1,0:T(8,128)S(1)} %collective-permute-done.1.refs_2_, ...), custom_call_target="tpu_custom_call" | custom-call | flops 2415919104 | bytes 4194304 | tf_op jit(solution)/shard_map/pallas_call | solution.py:389
  17.2 0.6 %collective-permute-start.5 = (bf16[192,512]{1,0:T(8,128)(2,1)S(1)}, bf16[192,512]{1,0:T(8,128)(2,1)S(1)}, u32[]{:S(2)}, u32[]{:S(2)}) collective-permute-start(bf16[192,512]{1,0:T(8,128)(2,1)S(1)} %get-tuple-element.23.refs_11_), channel_id=1, source_target_pairs={{0,1},{1,0},{2,3},{3,2},{4,5},{5,4},{6,7},{7,6},{8,9},{9,8},{10,11... | collective-permute-start | bytes 589832 | tf_op jit(solution)/shard_map/ppermute | solution.py:489
  17.8 0.9 %collective-permute-done.4.refs_7_ = bf16[192,2,256]{2,1,0:T(2,128)(2,1)S(1)} collective-permute-done((bf16[192,2,256]{2,1,0:T(2,128)(2,1)S(1)}, bf16[192,2,256]{2,1,0:T(2,128)(2,1)S(1)}, u32[]{:S(2)}, u32[]{:S(2)}) %collective-permute-start.4) | collective-permute-done | bytes 196640 | tf_op jit(solution)/shard_map/ppermute | solution.py:489
  18.7 1.4 %collective-permute-start.6 = (bf16[192,2,256]{2,1,0:T(2,128)(2,1)S(1)}, bf16[192,2,256]{2,1,0:T(2,128)(2,1)S(1)}, u32[]{:S(2)}, u32[]{:S(2)}) collective-permute-start(bf16[192,2,256]{2,1,0:T(2,128)(2,1)S(1)} %collective-permute-done.4.refs_7_), channel_id=1, source_target_pairs={{0,1},{1,0},{2,3},{3,2},{4,5},{5,4},{6,7},{7,6},{8,9},{9,8},{10,11... | collective-permute-start | bytes 589832 | tf_op jit(solution)/shard_map/ppermute | solution.py:489
  20.1 2.0 %shard_map.79 = (bf16[2,64,4096]{2,1,0:T(8,128)(2,1)S(1)}, bf16[192,512]{1,0:T(8,128)(2,1)S(1)}) custom-call(s32[8,128]{1,0:T(8,128)S(1)} %broadcast_in_dim.13.refs_0_, s32[8,128]{1,0:T(8,128)S(1)} %collective-permute-done.refs_1_, s32[8,128]{1,0:T(8,128)S(1)} %collective-permute-done.1.refs_2_, s32[8,128]{1,0:T(8,128)S(1)} %get-tuple-element.16.refs_3_, ...), custom_call_target="tpu_custom_call" | custom-call | flops 805306368 | bytes 4194304 | tf_op jit(solution)/shard_map/pallas_call | solution.py:389
  22.1 0.0 collective-permute-done.5.other
  22.1 0.0 collective-permute-done.6.other_rows
  22.1 1.6 %shard_map.80 = (bf16[2,64,4096]{2,1,0:T(8,128)(2,1)}, f32[192,4,256]{2,1,0:T(4,128)}) custom-call(f32[8,128]{1,0:T(8,128)S(1)} %get-tuple-element.14.refs_4_.floats_ref, bf16[256,256]{1,0:T(8,128)(2,1)S(1)} %get-tuple-element.15.refs_5_.signs_ref, bf16[192,192]{1,0:T(8,128)(2,1)S(1)} %get-tuple-element.20.refs_10_.pick_ref, ...), custom_call_target="tpu_custom_call" | custom-call | flops 75497472 | bytes 2097152 | tf_op jit(solution)/shard_map/pallas_call | solution.py:467
  (1 shorter events, 0.0 us)
Async XLA Ops:
  0.6 12.1 %collective-permute-start.3 = (bf16[192,2,256]{2,1,0:T(2,128)(2,1)}, bf16[192,2,256]{2,1,0:T(2,128)(2,1)S(1)}, u32[]{:S(2)}, u32[]{:S(2)}) collective-permute-start(bf16[192,2,256]{2,1,0:T(2,128)(2,1)} %refs_4_.1), channel_id=1, source_target_pairs={{0,8},{4,12},{8,0},{12,4},{1,9},{5,13},{9,1},{13,5},{2,10},{6,14},... | collective-permute-start | bytes 589832 | tf_op jit(solution)/shard_map/ppermute | solution.py:489
  0.8 12.1 %collective-permute-start.2 = (bf16[192,2,256]{2,1,0:T(2,128)(2,1)}, bf16[192,2,256]{2,1,0:T(2,128)(2,1)S(1)}, u32[]{:S(2)}, u32[]{:S(2)}) collective-permute-start(bf16[192,2,256]{2,1,0:T(2,128)(2,1)} %refs_4_.1), channel_id=1, source_target_pairs={{0,4},{4,0},{8,12},{12,8},{1,5},{5,1},{9,13},{13,9},{2,6},{6,2},{1... | collective-permute-start | bytes 589832 | tf_op jit(solution)/shard_map/ppermute | solution.py:489
  1.6 11.2 %collective-permute-start = (s32[8,128]{1,0:T(8,128)S(1)}, s32[8,128]{1,0:T(8,128)S(1)}, u32[]{:S(2)}, u32[]{:S(2)}) collective-permute-start(s32[8,128]{1,0:T(8,128)S(1)} %broadcast_in_dim.13.refs_0_), channel_id=1, source_target_pairs={{0,4},{4,0},{8,12},{12,8},{1,5},{5,1},{9,13},{13,9},{2,6},{6,2},{1... | collective-permute-start | bytes 12296 | tf_op jit(solution)/shard_map/ppermute | solution.py:489
  3.0 9.9 %collective-permute-start.1 = (s32[8,128]{1,0:T(8,128)S(1)}, s32[8,128]{1,0:T(8,128)S(1)}, u32[]{:S(2)}, u32[]{:S(2)}) collective-permute-start(s32[8,128]{1,0:T(8,128)S(1)} %broadcast_in_dim.13.refs_0_), channel_id=1, source_target_pairs={{0,8},{4,12},{8,0},{12,4},{1,9},{5,13},{9,1},{13,5},{2,10},{6,14},... | collective-permute-start | bytes 12296 | tf_op jit(solution)/shard_map/ppermute | solution.py:489
  5.3 1.2 %copy-start = (bf16[2,64,4096]{2,1,0:T(8,128)(2,1)S(1)}, bf16[2,64,4096]{2,1,0:T(8,128)(2,1)}, u32[]{:S(2)}) copy-start(bf16[2,64,4096]{2,1,0:T(8,128)(2,1)} %refs_5_.1) | copy-start | bytes 3145732
  6.5 0.9 %copy-start.1 = (bf16[192,2,256]{2,1,0:T(2,128)(2,1)S(1)}, bf16[192,2,256]{2,1,0:T(2,128)(2,1)}, u32[]{:S(2)}) copy-start(bf16[192,2,256]{2,1,0:T(2,128)(2,1)} %refs_4_.1) | copy-start | bytes 589828
  7.4 0.7 %copy-start.2 = (f32[8,2]{0,1:T(2,128)S(1)}, f32[8,2]{0,1:T(2,128)}, u32[]{:S(2)}) copy-start(f32[8,2]{0,1:T(2,128)} %param.7) | copy-start | bytes 196
  8.1 0.7 %copy-start.3 = (s32[2]{0:T(128)S(1)}, s32[2]{0:T(128)}, u32[]{:S(2)}) copy-start(s32[2]{0:T(128)} %refs_0_.1) | copy-start | bytes 28
  8.7 0.7 %copy-start.4 = (s32[48]{0:T(128)S(1)}, s32[48]{0:T(128)}, u32[]{:S(2)}) copy-start(s32[48]{0:T(128)} %param.11) | copy-start | bytes 580
  12.8 5.9 %collective-permute-start.4 = (bf16[192,2,256]{2,1,0:T(2,128)(2,1)S(1)}, bf16[192,2,256]{2,1,0:T(2,128)(2,1)S(1)}, u32[]{:S(2)}, u32[]{:S(2)}) collective-permute-start(bf16[192,2,256]{2,1,0:T(2,128)(2,1)S(1)} %collective-permute-done.3.refs_9_), channel_id=1, source_target_pairs={{0,4},{4,0},{8,12},{12,8},{1,5},{5,1},{9,13},{13,9},{2,6},{6,2},{1... | collective-permute-start | bytes 589832 | tf_op jit(solution)/shard_map/ppermute | solution.py:489
  17.2 4.9 %collective-permute-start.5 = (bf16[192,512]{1,0:T(8,128)(2,1)S(1)}, bf16[192,512]{1,0:T(8,128)(2,1)S(1)}, u32[]{:S(2)}, u32[]{:S(2)}) collective-permute-start(bf16[192,512]{1,0:T(8,128)(2,1)S(1)} %get-tuple-element.23.refs_11_), channel_id=1, source_target_pairs={{0,1},{1,0},{2,3},{3,2},{4,5},{5,4},{6,7},{7,6},{8,9},{9,8},{10,11... | collective-permute-start | bytes 589832 | tf_op jit(solution)/shard_map/ppermute | solution.py:489
  18.7 3.4 %collective-permute-start.6 = (bf16[192,2,256]{2,1,0:T(2,128)(2,1)S(1)}, bf16[192,2,256]{2,1,0:T(2,128)(2,1)S(1)}, u32[]{:S(2)}, u32[]{:S(2)}) collective-permute-start(bf16[192,2,256]{2,1,0:T(2,128)(2,1)S(1)} %collective-permute-done.4.refs_7_), channel_id=1, source_target_pairs={{0,1},{1,0},{2,3},{3,2},{4,5},{5,4},{6,7},{7,6},{8,9},{9,8},{10,11... | collective-permute-start | bytes 589832 | tf_op jit(solution)/shard_map/ppermute | solution.py:489
